TPU v7x, 128 devices: a whole 4x4x4 slice. The times are simulated.
128 devices in a mesh: section: 16 (over z, x_lo, core), dp: 8 (over y, x_hi).
Axes of the slice: x: 4 (x_hi: 2, x_lo: 2; x = x_hi * 2 + x_lo), y: 4, z: 4, core: 2. Of those that a mesh axis runs over, the one named last changes fastest.
Arguments:
- weight_old: bfloat16 [3072, 3072], P('section'), may hold values from -0.109375 to 0.109375
- moment_one: float32 [3072, 3072], P('section'), may hold values from -3 to 3
- moment_two: float32 [3072, 3072], P('section'), may hold values from 0.05 to 2
- residual_old: bfloat16 [8, 3072, 3072], P('dp', 'section'), may hold values from -4 to 4
- grads: bfloat16 [8, 16, 384, 3072], P('dp', 'section'), may hold values from -6 to 6
- exponents: int32 [8, 16, 384, 12], P('dp', 'section'), may hold values from -1 to 1
Outputs:
- new_weight: bfloat16 [16, 384, 3072], P('section')
- new_moment_one: float32 [16, 384, 3072], P('section')
- new_moment_two: float32 [16, 384, 3072], P('section')
- new_residual: bfloat16 [8, 16, 384, 3072], P('dp', 'section')
All inputs are finite; a program needn't handle non-finite values.
Results may differ from a plain program's by a relative error of at most 0.0075.
Values may be sent and summed in bfloat16 or wider, within the bound.
No kernel may reach another device: no remote copies, remote signals or barrier semaphores. Data moves between devices by JAX's collectives and lax.ppermute only.
A program may use at most 128 MiB of HBM per device.

v0:
```python
import jax
import jax.numpy as jnp
from jax import lax
from jax.sharding import PartitionSpec as P

BETA_ONE = 0.9
BETA_TWO = 0.95
LEARN_RATE = 0.001
EPSILON = 1e-08
BIAS_ONE = 1.0 - 0.9**10
BIAS_TWO = 1.0 - 0.95**10


def swapped(value, axis, apart):
    mask = 2**apart
    pairs = [(source, source ^ mask) for source in range(lax.axis_size(axis))]
    return lax.ppermute(value, axis, pairs)


def adam_update(weight, moment_a, moment_b, averaged):
    moment_a = BETA_ONE * moment_a + (1.0 - BETA_ONE) * averaged
    moment_b = BETA_TWO * moment_b + (1.0 - BETA_TWO) * averaged * averaged
    update = LEARN_RATE * (moment_a / BIAS_ONE) / (jnp.sqrt(moment_b / BIAS_TWO) + EPSILON)
    return ((weight.astype(jnp.float32) - update).astype(jnp.bfloat16), moment_a, moment_b)


def arrange(own_part, partner_part, parity):
    lower = jnp.where(parity == 0, own_part, partner_part)
    upper = jnp.where(parity == 0, partner_part, own_part)
    return jnp.concatenate([lower, upper], axis=0)


def shards(weight_old, moment_one, moment_two, residual_old, grads, exponents):
    parity = lax.axis_index("section") % 2
    partner_res, partner_weight = swapped((residual_old, weight_old), "section", 0)
    carried = arrange(residual_old[0], partner_res[0], parity).astype(jnp.float32)
    summand = grads[0, 0].astype(jnp.float32) + carried
    group_rows, columns = summand.shape
    scales = jnp.exp2(exponents[0, 0].astype(jnp.float32))[..., None]
    scale_count = scales.shape[1]
    clipped = jnp.clip(
        summand.reshape(group_rows, scale_count, columns // scale_count), -scales, scales
    )
    clipped = clipped.reshape(group_rows, columns).astype(jnp.bfloat16)
    new_residual = (summand - clipped.astype(jnp.float32)).astype(jnp.bfloat16)[None, None]
    replica_count = 2 * lax.axis_size("dp")
    partner_one, partner_two = (
        swapped(moment_one.astype(jnp.bfloat16), "section", 0).astype(moment_one.dtype),
        swapped(moment_two.astype(jnp.bfloat16), "section", 0).astype(moment_two.dtype),
    )
    weight_group = arrange(weight_old, partner_weight, parity)
    moment_group_a = arrange(moment_one, partner_one, parity)
    moment_group_b = arrange(moment_two, partner_two, parity)
    summed = lax.psum(clipped.astype(jnp.float32).astype(jnp.bfloat16), "dp").astype(jnp.float32)
    summed = summed + swapped(summed.astype(jnp.bfloat16), "section", 0).astype(summed.dtype)
    averaged = summed / replica_count
    updated, moment_a, moment_b = adam_update(
        weight_group, moment_group_a, moment_group_b, averaged
    )
    return (updated[None], moment_a[None], moment_b[None], new_residual)


def solution(mesh):
    in_specs = (
        P("section", None),
        P("section", None),
        P("section", None),
        P("dp", "section", None),
        P("dp", "section", None, None),
        P("dp", "section", None, None),
    )
    out_specs = (
        P("section", None, None),
        P("section", None, None),
        P("section", None, None),
        P("dp", "section", None, None),
    )
    return jax.shard_map(shards, mesh=mesh, in_specs=in_specs, out_specs=out_specs, check_vma=False)
```

profile of v0, /device:TPU:1, one launch (start us, length us, event | category | flops | bytes accessed | tf_op | source)
XLA Modules:
  0.0 184.2 jit_solution(14899554723121263357)
XLA Ops:
  7.2 1.5 collective-permute-start.2
  8.7 2.5 %copy.37 = bf16[1,192,3072]{1,2,0:T(8,128)(2,1)} copy(bf16[1,192,3072]{2,1,0:T(8,128)(2,1)} %param.9) | data formatting | bytes 2359296 | tf_op args[3]
  11.2 0.8 multiply_exponential_fusion
  12.0 0.6 copy-done.8
  12.6 3.0 %copy.36 = bf16[1,1,384,3072]{2,3,1,0:T(8,128)(2,1)S(1)} copy(bf16[1,1,384,3072]{3,2,1,0:T(8,128)(2,1)} %param.10) | data formatting | bytes 4718592 | tf_op args[4]
  15.6 1.3 fusion.11
  16.9 1.5 copy.38
  18.5 4.0 %fusion.7 = (bf16[1,1,192,3072]{2,3,1,0:T(8,128)(2,1)}, bf16[1,1,192,3072]{2,3,1,0:T(8,128)(2,1)}, bf16[192,3072]{0,1:T(8,128)(2,1)S(1)}, bf16[192,3072]{0,1:T(8,128)(2,1)S(1)}) fusion(bf16[1,192,3072]{1,2,0:T(8,128)(2,1)} %copy.37, bf16[1,192,3072]{1,2,0:T(8,128)(2,1)} %copy.38, pred[]{:T(512)S(6)} %eq.4), kind=kLoop, calls=%fused_computation.23 | loop fusion | flops 1179648 | bytes 7077889 | tf_op jit(solution)/shard_map/concatenate | solution.py:30
  22.4 2.8 %fusion.3 = bf16[384,3072]{0,1:T(8,128)(2,1)} fusion(bf16[1,1,384,3072]{2,3,1,0:T(8,128)(2,1)S(1)} %copy.36, bf16[192,3072]{0,1:T(8,128)(2,1)S(1)} %get-tuple-element.21, bf16[192,3072]{0,1:T(8,128)(2,1)S(1)} %get-tuple-element.22, bf16[384,12]{0,1:T(8,128)(2,1)S(1)} %copy-done.9, bf16[384,12]{0,1:T(8,128)(2,1)S(1)} %bitcast.37), kind=kLoop, calls=%fused_computation.5 | loop fusion | flops 12976128 | bytes 7096320 | tf_op jit(solution)/shard_map/convert_element_type | solution.py:44
  25.3 3.0 %convert_element_type.89 = bf16[192,3072]{1,0:T(8,128)(2,1)} convert(f32[192,3072]{1,0:T(8,128)} %param.8) | non-fusion elementwise | flops 589824 | bytes 3538944 | tf_op jit(solution)/shard_map/convert_element_type | solution.py:49
  28.5 0.6 collective-permute-start.1
  29.2 2.6 %copy.29 = bf16[192,3072]{0,1:T(8,128)(2,1)} copy(bf16[192,3072]{1,0:T(8,128)(2,1)} %param.6) | data formatting | bytes 2359296 | tf_op args[0]
  31.7 3.4 %copy.34 = f32[192,3072]{0,1:T(8,128)} copy(f32[192,3072]{1,0:T(8,128)} %param.7) | data formatting | bytes 4718592 | tf_op args[1]
  35.1 3.4 %copy.42 = f32[192,3072]{0,1:T(8,128)} copy(f32[192,3072]{1,0:T(8,128)} %param.8) | data formatting | bytes 4718592 | tf_op args[2]
  38.8 1.1 max.20
  40.0 0.5 copy-done.4
  40.5 3.4 %subtract_convert_fusion = bf16[1,1,384,3072]{2,3,1,0:T(8,128)(2,1)} fusion(bf16[1,1,384,3072]{2,3,1,0:T(8,128)(2,1)S(1)} %bitcast.35, bf16[1,1,384,3072]{2,3,1,0:T(8,128)(2,1)S(1)} %bitcast.36, bf16[1,1,384,3072]{2,3,1,0:T(8,128)(2,1)S(1)} %copy.36, bf16[1,1,192,3072]{2,3,1,0:T(8,128)(2,1)S(1)} %copy-done.4, bf16[1,1,192,3072]{2,3,1,0:T(8,128)(2,1)S(1)} %copy-done.3), kind=kLoop, calls=%fused_computation.10 | loop fusion | flops 15335424 | bytes 11796480 | tf_op jit(solution)/shard_map/convert_element_type | solution.py:45
  43.9 4.3 %copy.47 = bf16[1,1,384,3072]{3,2,1,0:T(8,128)(2,1)} copy(bf16[1,1,384,3072]{2,3,1,0:T(8,128)(2,1)} %subtract_convert_fusion) | data formatting | bytes 4718592
  48.1 2.5 %copy.41 = bf16[192,3072]{0,1:T(8,128)(2,1)} copy(bf16[192,3072]{1,0:T(8,128)(2,1)} %collective-permute-done.4) | data formatting | bytes 2359296 | tf_op jit(solution)/shard_map/ppermute | solution.py:17
  50.7 2.5 %copy.33 = bf16[192,3072]{0,1:T(8,128)(2,1)} copy(bf16[192,3072]{1,0:T(8,128)(2,1)} %collective-permute-done.1) | data formatting | bytes 2359296 | tf_op jit(solution)/shard_map/ppermute | solution.py:17
  53.2 2.5 %copy.30 = bf16[192,3072]{0,1:T(8,128)(2,1)} copy(bf16[192,3072]{1,0:T(8,128)(2,1)} %collective-permute-done) | data formatting | bytes 2359296 | tf_op jit(solution)/shard_map/ppermute | solution.py:17
  55.7 87.9 %all-reduce.2.cloned.1.call-done = bf16[384,3072]{0,1:T(8,128)(2,1)} async-done(((bf16[384,3072]{0,1:T(8,128)(2,1)}), bf16[384,3072]{0,1:T(8,128)(2,1)}) %all-reduce.2.cloned.1.call-update) | async-done | bytes 2359312 | tf_op jit(solution)/shard_map/psum | solution.py:54
  143.6 0.9 collective-permute-start.3
  144.5 3.8 %broadcast_select_fusion.3 = (bf16[192,3072]{0,1:T(8,128)(2,1)}, bf16[192,3072]{0,1:T(8,128)(2,1)}) fusion(bf16[192,3072]{0,1:T(8,128)(2,1)} %copy.29, bf16[192,3072]{0,1:T(8,128)(2,1)} %copy.30, pred[]{:T(512)S(6)} %eq.4), kind=kLoop, calls=%fused_computation.22 | loop fusion | flops 1179648 | bytes 4718593 | tf_op jit(solution)/shard_map/jit(_where)/select_n | solution.py:28
  148.3 0.5 convert_select_fusion.3
  148.8 1.4 copy-done
  150.2 0.5 copy-done.5
  151.1 1.4 copy-done.7
  152.5 10.2 %fusion.13 = (f32[1,384,3072]{1,2,0:T(8,128)}, bf16[1,384,3072]{1,2,0:T(8,128)(2,1)S(1)}, f32[1,384,3072]{1,2,0:T(8,128)}) fusion(bf16[384,3072]{0,1:T(8,128)(2,1)} %copy-done.7, bf16[384,3072]{0,1:T(8,128)(2,1)} %all-reduce.2.cloned.1.call-done, f32[192,3072]{0,1:T(8,128)S(1)} %get-tuple-element.16, f32[192,3072]{0,1:T(8,128)S(1)} %get-tuple-element.15, ...), kind=kLoop, calls=%fused_computation.31 | loop fusion | flops 27131904 | bytes 28311552 | tf_op jit(solution)/shard_map/broadcast_in_dim | solution.py:60
  162.7 6.0 %copy.46 = f32[1,384,3072]{2,1,0:T(8,128)} copy(f32[1,384,3072]{1,2,0:T(8,128)} %get-tuple-element.12) | data formatting | bytes 9437184
  168.8 2.6 %copy.44 = bf16[1,384,3072]{2,1,0:T(8,128)(2,1)} copy(bf16[1,384,3072]{1,2,0:T(8,128)(2,1)S(1)} %get-tuple-element.13) | data formatting | bytes 4718592
  171.3 6.0 %copy.45 = f32[1,384,3072]{2,1,0:T(8,128)} copy(f32[1,384,3072]{1,2,0:T(8,128)} %get-tuple-element.14) | data formatting | bytes 9437184
  (28 shorter events, 1.1 us)
Async XLA Ops:
  7.2 136.5 %all-reduce.2.cloned.1.call-start = ((), (), s32[]{:S(2)}) async-start(), calls=%async_computation | async-start | bytes 4718592 | tf_op jit(solution)/shard_map/psum | solution.py:54
  7.2 9.7 %collective-permute-start.2 = (bf16[1,192,3072]{2,1,0:T(8,128)(2,1)}, bf16[1,192,3072]{2,1,0:T(8,128)(2,1)S(1)}, u32[]{:S(2)}, u32[]{:S(2)}) collective-permute-start(bf16[1,192,3072]{2,1,0:T(8,128)(2,1)} %param.9), channel_id=1, source_target_pairs={{0,8},{8,0},{16,24},{24,16},{32,40},{40,32},{48,56},{56,48},{64,72... | collective-permute-start | bytes 3538952 | tf_op jit(solution)/shard_map/ppermute | solution.py:17
  12.0 0.6 copy-start.8
  18.4 4.0 %copy-start.9 = (bf16[384,12]{0,1:T(8,128)(2,1)S(1)}, bf16[384,12]{0,1:T(8,128)(2,1)}, u32[]{:S(2)}) copy-start(bf16[384,12]{0,1:T(8,128)(2,1)} %fusion.11) | copy-start | bytes 27652
  25.3 3.0 %copy-start.2 = (f32[192,3072]{1,0:T(8,128)S(1)}, f32[192,3072]{1,0:T(8,128)}, u32[]{:S(2)}) copy-start(f32[192,3072]{1,0:T(8,128)} %param.7) | copy-start | bytes 7077892
  28.3 19.8 %collective-permute-start.4 = (bf16[192,3072]{1,0:T(8,128)(2,1)}, bf16[192,3072]{1,0:T(8,128)(2,1)}, u32[]{:S(2)}, u32[]{:S(2)}) collective-permute-start(bf16[192,3072]{1,0:T(8,128)(2,1)} %convert_element_type.89), channel_id=1, source_target_pairs={{0,8},{8,0},{16,24},{24,16},{32,40},{40,32},{48,56},{56,48},{64,72... | collective-permute-start | bytes 3538952 | tf_op jit(solution)/shard_map/ppermute | solution.py:17
  28.5 22.2 %collective-permute-start.1 = (bf16[192,3072]{1,0:T(8,128)(2,1)S(1)}, bf16[192,3072]{1,0:T(8,128)(2,1)}, u32[]{:S(2)}, u32[]{:S(2)}) collective-permute-start(bf16[192,3072]{1,0:T(8,128)(2,1)S(1)} %convert_element_type.80), channel_id=1, source_target_pairs={{0,8},{8,0},{16,24},{24,16},{32,40},{40,32},{48,56},{56,48},{64,72... | collective-permute-start | bytes 3538952 | tf_op jit(solution)/shard_map/ppermute | solution.py:17
  29.1 24.2 %collective-permute-start = (bf16[192,3072]{1,0:T(8,128)(2,1)}, bf16[192,3072]{1,0:T(8,128)(2,1)}, u32[]{:S(2)}, u32[]{:S(2)}) collective-permute-start(bf16[192,3072]{1,0:T(8,128)(2,1)} %param.6), channel_id=1, source_target_pairs={{0,8},{8,0},{16,24},{24,16},{32,40},{40,32},{48,56},{56,48},{64,72... | collective-permute-start | bytes 3538952 | tf_op jit(solution)/shard_map/ppermute | solution.py:17
  38.6 1.4 copy-start.3
  38.6 1.9 %copy-start.4 = (bf16[1,1,192,3072]{2,3,1,0:T(8,128)(2,1)S(1)}, bf16[1,1,192,3072]{2,3,1,0:T(8,128)(2,1)}, u32[]{:S(2)}) copy-start(bf16[1,1,192,3072]{2,3,1,0:T(8,128)(2,1)} %get-tuple-element.20) | copy-start | bytes 3538948
  55.7 92.6 %copy-start.1 = (f32[192,3072]{0,1:T(8,128)S(1)}, f32[192,3072]{0,1:T(8,128)}, u32[]{:S(2)}) copy-start(f32[192,3072]{0,1:T(8,128)} %copy.34) | copy-start | bytes 7077892
  143.6 4.7 %copy-start.6 = (bf16[192,3072]{0,1:T(8,128)(2,1)S(1)}, bf16[192,3072]{0,1:T(8,128)(2,1)}, u32[]{:S(2)}) copy-start(bf16[192,3072]{0,1:T(8,128)(2,1)} %copy.33) | copy-start | bytes 3538948
  143.6 7.5 %collective-permute-start.3 = (bf16[384,3072]{0,1:T(8,128)(2,1)}, bf16[384,3072]{0,1:T(8,128)(2,1)S(1)}, u32[]{:S(2)}, u32[]{:S(2)}) collective-permute-start(bf16[384,3072]{0,1:T(8,128)(2,1)} %all-reduce.2.cloned.1.call-done), channel_id=1, source_target_pairs={{0,8},{8,0},{16,24},{24,16},{32,40},{40,32},{48,56},{56,48},{64,72... | collective-permute-start | bytes 7077896 | tf_op jit(solution)/shard_map/ppermute | solution.py:17
  148.3 1.9 %copy-start = (f32[192,3072]{0,1:T(8,128)S(1)}, f32[192,3072]{0,1:T(8,128)}, u32[]{:S(2)}) copy-start(f32[192,3072]{0,1:T(8,128)} %copy.42) | copy-start | bytes 7077892
  148.3 2.4 %copy-start.5 = (bf16[192,3072]{0,1:T(8,128)(2,1)S(1)}, bf16[192,3072]{0,1:T(8,128)(2,1)}, u32[]{:S(2)}) copy-start(bf16[192,3072]{0,1:T(8,128)(2,1)} %copy.41) | copy-start | bytes 3538948
  151.1 1.4 copy-start.7
Sparse Core Ops, SparseCore 0:
  25.4 118.1 all-reduce.1
where the time goes:
time: 185 us; the launch traced here: 184 us
  waiting for transfers between devices  87.9 us (48%)
  local copies, waits for them, and re-layouts  48.7 us (26%)
  other arithmetic  30.3 us (16%)
  between operations  14.1 us (8%)
  starting transfers between devices  3.12 us (2%)
    psum x1, waiting for transfers between devices, shards(): lax.psum(clipped.astype(jnp.float32).astype(jnp.bfloat16), 'dp')  87.9 us
    unnamed x30, local copies, waits for them, and re-layouts  38.3 us
    broadcast_in_dim x1, other arithmetic, shards(): return (updated[None], moment_a[None], moment_b[None], new_residual)  10.2 us
    ppermute x4, local copies, waits for them, and re-layouts, swapped(): return lax.ppermute(value, axis, pairs)  9.1 us
    select_n x3, other arithmetic, arrange(): lower = jnp.where(parity == 0, own_part, partner_part)  4.7 us
    concatenate x1, other arithmetic, arrange(): return jnp.concatenate([lower, upper], axis=0)  3.99 us
  transfers between devices with their start and end apart: 6, of which 1 were waited for; matrix products, arithmetic and copies ran while one was open for 22% of the time, Pallas kernels for 0%

commit v1 on v0

v1 whole, which is shorter than its diff:
```python
import functools

import jax
import jax.numpy as jnp
from jax import lax
from jax.experimental import pallas as pl
from jax.experimental.pallas import tpu as pltpu
from jax.sharding import PartitionSpec as P

BETA_ONE = 0.9
BETA_TWO = 0.95
LEARN_RATE = 0.001
EPSILON = 1e-08
BIAS_ONE = 1.0 - 0.9**10
BIAS_TWO = 1.0 - 0.95**10
BLOCK = 256
STEP = 48
F32 = jnp.float32
BF16 = jnp.bfloat16


def swapped(value):
    pairs = [(source, source ^ 1) for source in range(lax.axis_size("section"))]
    return lax.ppermute(value, "section", pairs)


def clipped_block(grads, residual, scales, block):
    columns = slice(block * BLOCK, (block + 1) * BLOCK)
    summand = grads[:, columns].astype(F32) + residual[:, columns].astype(F32)
    scale = scales[:, block : block + 1]
    return summand, jnp.clip(summand, -scale, scale).astype(BF16), columns


def own_kernel(half, grads, residual, scales, clipped, left):
    for block in range(grads.shape[1] // BLOCK):
        summand, kept, columns = clipped_block(grads, residual, scales, block)
        clipped[:, columns] = kept
        left[:, columns] = (summand - kept.astype(F32)).astype(BF16)


def other_kernel(half, grads, residual, scales, held, left):
    for block in range(grads.shape[1] // BLOCK):
        summand, kept, columns = clipped_block(grads, residual, scales, block)
        left[:, columns] = (summand - kept.astype(F32)).astype(BF16)


def pair_kernel(grads, residual, scales, clipped, summed):
    width = summed.shape[2]
    for block in range(grads.shape[1] // BLOCK):
        _, kept, columns = clipped_block(grads, residual, scales, block)
        total = (kept.astype(F32) + clipped[:, columns].astype(F32)).astype(BF16)
        for part in range(BLOCK // 128):
            start = block * BLOCK + part * 128
            at = start % width
            summed[start // width, :, at : at + 128] = total[:, part * 128 : (part + 1) * 128]


def sum_kernel(parts, out):
    total = parts[0].astype(F32)
    for part in range(1, parts.shape[0]):
        total = total + parts[part].astype(F32)
    total = total.astype(BF16)
    for part in range(out.shape[0]):
        out[part] = total


def adam_kernel(half, summed, weight, moment_one, moment_two, *rest):
    new_weight, new_one, new_two = rest[-3:]
    replicas = 16.0
    for part in range(summed.shape[0]):
        width = summed.shape[2]
        columns = slice(part * width, (part + 1) * width)
        averaged = summed[part].astype(F32) / replicas
        moment_a = BETA_ONE * moment_one[:, columns] + (1.0 - BETA_ONE) * averaged
        moment_b = BETA_TWO * moment_two[:, columns] + (1.0 - BETA_TWO) * averaged * averaged
        update = LEARN_RATE * (moment_a / BIAS_ONE) / (jnp.sqrt(moment_b / BIAS_TWO) + EPSILON)
        new_weight[:, columns] = (weight[:, columns].astype(F32) - update).astype(BF16)
        new_one[:, columns] = moment_a
        new_two[:, columns] = moment_b


def cost(flops, moved):
    return pl.CostEstimate(flops=flops, bytes_accessed=moved, transcendentals=0)


def rows_of(half_rows):
    steps = half_rows // STEP
    return steps, lambda step, half: (half[0] * steps + step, 0)


def clip_half(half, grads, residual, scales, left_held):
    rows, columns = residual.shape
    steps, at_half = rows_of(rows)
    at_step = lambda step, half: (step, 0)
    in_specs = [
        pl.BlockSpec((STEP, columns), at_half),
        pl.BlockSpec((STEP, columns), at_step),
        pl.BlockSpec((STEP, scales.shape[1]), at_half),
    ]
    left_spec = pl.BlockSpec((STEP, columns), at_half)
    left_shape = jax.ShapeDtypeStruct(grads.shape, BF16)
    size = rows * columns
    if left_held is None:
        return pl.pallas_call(
            own_kernel,
            grid_spec=pltpu.PrefetchScalarGridSpec(
                num_scalar_prefetch=1,
                grid=(steps,),
                in_specs=in_specs,
                out_specs=[pl.BlockSpec((STEP, columns), at_step), left_spec],
            ),
            out_shape=[jax.ShapeDtypeStruct((rows, columns), BF16), left_shape],
            cost_estimate=cost(6 * size, 8 * size),
            name="clip_own",
        )(half, grads, residual, scales)
    return pl.pallas_call(
        other_kernel,
        grid_spec=pltpu.PrefetchScalarGridSpec(
            num_scalar_prefetch=1,
            grid=(steps,),
            in_specs=in_specs + [pl.BlockSpec(memory_space=pl.ANY)],
            out_specs=left_spec,
        ),
        out_shape=left_shape,
        input_output_aliases={4: 0},
        cost_estimate=cost(6 * size, 6 * size),
        name="clip_other",
    )(half, grads, residual, scales, left_held)


def pair_sum(grads, residual, scales, clipped, parts):
    rows, columns = residual.shape
    at_step = lambda step: (step, 0)
    spec = pl.BlockSpec((STEP, columns), at_step)
    size = rows * columns
    return pl.pallas_call(
        pair_kernel,
        grid=(rows // STEP,),
        in_specs=[spec, spec, pl.BlockSpec((STEP, scales.shape[1]), at_step), spec],
        out_specs=pl.BlockSpec((parts, STEP, columns // parts), lambda step: (0, step, 0)),
        out_shape=jax.ShapeDtypeStruct((parts, rows, columns // parts), BF16),
        cost_estimate=cost(6 * size, 8 * size),
        name="pair_sum",
    )(grads, residual, scales, clipped)


def replica_sum(parts):
    count, rows, columns = parts.shape
    spec = pl.BlockSpec((count, STEP, columns), lambda step: (0, step, 0))
    return pl.pallas_call(
        sum_kernel,
        grid=(rows // STEP,),
        in_specs=[spec],
        out_specs=spec,
        out_shape=jax.ShapeDtypeStruct(parts.shape, BF16),
        cost_estimate=cost(count * rows * columns, 4 * count * rows * columns),
        name="replica_sum",
    )(parts)


def adam_half(half, summed, weight, moment_one, moment_two, held):
    parts, rows, width = summed.shape
    columns = parts * width
    steps, at_half = rows_of(rows)
    at_step = lambda step, half: (step, 0)
    spec = pl.BlockSpec((STEP, columns), at_step)
    any_spec = pl.BlockSpec(memory_space=pl.ANY)
    out_spec = pl.BlockSpec((STEP, columns), at_half)
    size = rows * columns
    return pl.pallas_call(
        adam_kernel,
        grid_spec=pltpu.PrefetchScalarGridSpec(
            num_scalar_prefetch=1,
            grid=(steps,),
            in_specs=[pl.BlockSpec((parts, STEP, width), lambda step, half: (0, step, 0))]
            + [spec] * 3
            + [any_spec] * len(held),
            out_specs=[out_spec] * 3,
        ),
        out_shape=[jax.ShapeDtypeStruct((2 * rows, columns), kind) for kind in (BF16, F32, F32)],
        input_output_aliases={5 + at: at for at in range(len(held))},
        cost_estimate=cost(20 * size, 22 * size),
        name="adam_half",
    )(half, summed, weight, moment_one, moment_two, *held)


def shards(weight_old, moment_one, moment_two, residual_old, grads, exponents):
    parity = lax.axis_index("section") % 2
    own = parity.astype(jnp.int32).reshape(1)
    other = 1 - own
    replicas = lax.axis_size("dp")
    residual = residual_old[0]
    grads = grads[0, 0]
    rows = residual.shape[0]
    scales = jnp.exp2(exponents[0, 0].astype(F32))

    partner_grads, partner_scales = swapped(
        (
            lax.dynamic_slice_in_dim(grads, other[0] * rows, rows, axis=0),
            lax.dynamic_slice_in_dim(scales, other[0] * rows, rows, axis=0),
        )
    )
    partner_residual = swapped(residual)
    clipped, left = clip_half(own, grads, residual, scales, None)
    paired = pair_sum(partner_grads, residual, partner_scales, clipped, replicas)
    partner_one, partner_two, partner_weight = swapped((moment_one, moment_two, weight_old))

    scattered = lax.all_to_all(paired, "dp", 0, 0, tiled=True)
    summed = lax.all_to_all(replica_sum(scattered), "dp", 0, 0, tiled=True)
    partner_summed = swapped(summed)
    left = clip_half(other, grads, partner_residual, scales, left)
    updated = adam_half(own, summed, weight_old, moment_one, moment_two, ())
    updated = adam_half(
        other, partner_summed, partner_weight, partner_one, partner_two, tuple(updated)
    )
    return (updated[0][None], updated[1][None], updated[2][None], left[None, None])


def solution(mesh):
    in_specs = (
        P("section", None),
        P("section", None),
        P("section", None),
        P("dp", "section", None),
        P("dp", "section", None, None),
        P("dp", "section", None, None),
    )
    out_specs = (
        P("section", None, None),
        P("section", None, None),
        P("section", None, None),
        P("dp", "section", None, None),
    )
    return jax.shard_map(shards, mesh=mesh, in_specs=in_specs, out_specs=out_specs, check_vma=False)
```

time: 185 us -> 83.6 us (0.45)
  waiting for transfers between devices: 87.9 us -> 31.9 us
  local copies, waits for them, and re-layouts: 48.7 us -> 4.28 us
  other arithmetic: 30.3 us -> 0.02 us
  Pallas kernels: 0 us -> 28.5 us
  starting transfers between devices: 3.12 us -> 17.5 us
  between operations: 14.1 us -> 0.75 us
    psum x1 -> x0, waiting for transfers between devices: 87.9 us -> none  [shards(): lax.psum(clipped.astype(jnp.float32).astype(jnp.bfloat16), 'dp')]
    unnamed x30 -> x14, local copies, waits for them, and re-layouts: 38.3 us -> 2.05 us
    all_to_all x0 -> x2, waiting for transfers between devices: none -> 31.9 us  [the longest x1 17 us: shards(): scattered = lax.all_to_all(paired, 'dp', 0, 0, tiled=True)]
    pallas_call x0 -> x6, Pallas kernels: none -> 28.5 us  [the longest x2 12.5 us: adam_half(): pl.pallas_call(adam_kernel, grid_spec=pltpu.PrefetchScalarGridSpec(num_sc...]
    all_to_all x0 -> x2, starting transfers between devices: none -> 10.3 us  [the longest x1 6.73 us: shards(): scattered = lax.all_to_all(paired, 'dp', 0, 0, tiled=True)]
    broadcast_in_dim x1 -> x0, other arithmetic: 10.2 us -> none  [shards(): return (updated[None], moment_a[None], moment_b[None], new_residual)]
    convert_element_type x4 -> x0, other arithmetic: 9.36 us -> none  [the longest x1 3.39 us: shards(): (summand - clipped.astype(jnp.float32)).astype(jnp.bfloat16)[None, None]]
    ppermute x4 -> x0, local copies, waits for them, and re-layouts: 9.1 us -> none  [swapped(): return lax.ppermute(value, axis, pairs)]
  transfers between devices with their start and end apart: 6 -> 9, of which waited for: 1 -> 2; matrix products, arithmetic and copies ran while one was open for 22% -> 1% of each run, Pallas kernels for 0% -> 22%
where the time goes in v1:
time: 83.6 us; the launch traced here: 83 us
  waiting for transfers between devices  31.9 us (38%)
  Pallas kernels  28.5 us (34%)
  starting transfers between devices  17.5 us (21%)
  local copies, waits for them, and re-layouts  4.28 us (5%)
    all_to_all x1, waiting for transfers between devices, shards(): scattered = lax.all_to_all(paired, 'dp', 0, 0, tiled=True)  17 us
    all_to_all x1, waiting for transfers between devices, shards(): summed = lax.all_to_all(replica_sum(scattered), 'dp', 0, 0, tiled=True)  14.9 us
    pallas_call x2, Pallas kernels, adam_half(): pl.pallas_call(adam_kernel, grid_spec=pltpu.PrefetchScalarGridSpec(num_sc...  12.5 us
    ppermute x7, starting transfers between devices, swapped(): return lax.ppermute(value, 'section', pairs)  7.17 us
    all_to_all x1, starting transfers between devices, shards(): scattered = lax.all_to_all(paired, 'dp', 0, 0, tiled=True)  6.73 us
    pallas_call x1, Pallas kernels, pair_sum(): pl.pallas_call(pair_kernel, grid=(rows // STEP,), in_specs=[spec, spec, p...  4.29 us
    pallas_call x1, Pallas kernels, clip_half(): pl.pallas_call(own_kernel, grid_spec=pltpu.PrefetchScalarGridSpec(num_sca...  4.23 us
    pallas_call x1, Pallas kernels, clip_half(): pl.pallas_call(other_kernel, grid_spec=pltpu.PrefetchScalarGridSpec(num_s...  4 us
  transfers between devices with their start and end apart: 9, of which 2 were waited for; matrix products, arithmetic and copies ran while one was open for 1% of the time, Pallas kernels for 22%

profile of v1, /device:TPU:1, one launch (start us, length us, event | category | flops | bytes accessed | tf_op | source)
XLA Modules:
  0.0 83.0 jit_solution(9514757789038998724)
XLA Ops:
  0.7 1.4 %dynamic-slice_bitcast_fusion = bf16[192,3072]{1,0:T(8,128)(2,1)S(1)} fusion(bf16[1,1,384,3072]{3,2,1,0:T(8,128)(2,1)} %param.10, s32[]{:T(128)S(6)} %select_n.12), kind=kLoop, calls=%fused_computation | loop fusion | bytes 2359300 | tf_op jit(solution)/shard_map/dynamic_slice | solution.py:199
  2.0 1.5 %collective-permute-start = (bf16[192,3072]{1,0:T(8,128)(2,1)S(1)}, bf16[192,3072]{1,0:T(8,128)(2,1)S(1)}, u32[]{:S(2)}, u32[]{:S(2)}) collective-permute-start(bf16[192,3072]{1,0:T(8,128)(2,1)S(1)} %dynamic-slice_bitcast_fusion), channel_id=1, source_target_pairs={{0,8},{8,0},{16,24},{24,16},{32,40},{40,32},{48,56},{56,48},{64,72... | collective-permute-start | bytes 3538952 | tf_op jit(solution)/shard_map/ppermute | solution.py:24
  3.5 0.1 copy.16
  3.7 0.7 exponential_bitcast_fusion
  4.4 0.1 collective-permute-start.1
  4.5 4.2 %clip_own.1 = (bf16[192,3072]{1,0:T(8,128)(2,1)}, bf16[384,3072]{1,0:T(8,128)(2,1)}) custom-call(s32[1]{0:T(128)} %bitcast.half, bf16[384,3072]{1,0:T(8,128)(2,1)} %bitcast.14, bf16[192,3072]{1,0:T(8,128)(2,1)} %bitcast.18, f32[384,12]{1,0:T(8,128)} %get-tuple-element.20.scales), custom_call_target="tpu_custom_call" | custom-call | flops 3538944 | bytes 4718592 | tf_op jit(solution)/shard_map/clip_own/pallas_call | solution.py:104
  8.8 0.0 collective-permute-done.1.scales
  8.8 0.0 collective-permute-done.grads
  8.8 0.0 copy-start.4
  8.8 0.6 copy-done.5
  9.4 0.4 copy-done.4
  9.8 4.3 %pair_sum.1 = bf16[8,192,384]{2,1,0:T(8,128)(2,1)} custom-call(bf16[192,3072]{1,0:T(8,128)(2,1)} %copy-done.4, bf16[192,3072]{1,0:T(8,128)(2,1)} %bitcast.19, f32[192,12]{1,0:T(8,128)} %copy-done.5, bf16[192,3072]{1,0:T(8,128)(2,1)} %get-tuple-element.12.clipped), custom_call_target="tpu_custom_call" | custom-call | flops 3538944 | bytes 4718592 | tf_op jit(solution)/shard_map/pair_sum/pallas_call | solution.py:136
  14.1 6.7 %all-to-all-start = ((bf16[8,192,384]{2,1,0:T(8,128)(2,1)}), bf16[8,192,384]{2,1,0:T(8,128)(2,1)S(1)}, u32[]{:S(2)}, u32[]{:S(2)}) async-start(bf16[8,192,384]{2,1,0:T(8,128)(2,1)} %pair_sum.1), calls=%async_computation | async-start | bytes 2359296 | tf_op jit(solution)/shard_map/all_to_all | solution.py:208
  20.8 0.0 copy-start.3
  20.8 0.8 collective-permute-start.4
  21.7 0.1 collective-permute-start.5
  21.8 17.0 %all-to-all-done.parts = bf16[8,192,384]{2,1,0:T(8,128)(2,1)S(1)} async-done(((bf16[8,192,384]{2,1,0:T(8,128)(2,1)}), bf16[8,192,384]{2,1,0:T(8,128)(2,1)S(1)}, u32[]{:S(2)}, u32[]{:S(2)}) %all-to-all-start) | async-done | bytes 1179680 | tf_op jit(solution)/shard_map/all_to_all | solution.py:208
  38.8 1.0 %copy-done.1 = bf16[8,192,384]{2,1,0:T(8,128)(2,1)} copy-done((bf16[8,192,384]{2,1,0:T(8,128)(2,1)}, bf16[8,192,384]{2,1,0:T(8,128)(2,1)S(1)}, u32[]{:S(2)}) %copy-start.1) | copy-done | bytes 1179672
  39.8 3.5 %replica_sum.1 = bf16[8,192,384]{2,1,0:T(8,128)(2,1)} custom-call(bf16[8,192,384]{2,1,0:T(8,128)(2,1)} %copy-done.1), custom_call_target="tpu_custom_call" | custom-call | flops 589824 | bytes 2359296 | tf_op jit(solution)/shard_map/replica_sum/pallas_call | solution.py:150
  43.2 3.6 %all-to-all-start.1 = ((bf16[8,192,384]{2,1,0:T(8,128)(2,1)}), bf16[8,192,384]{2,1,0:T(8,128)(2,1)S(1)}, u32[]{:S(2)}, u32[]{:S(2)}) async-start(bf16[8,192,384]{2,1,0:T(8,128)(2,1)} %replica_sum.1), calls=%async_computation.1 | async-start | bytes 2359296 | tf_op jit(solution)/shard_map/all_to_all | solution.py:209
  46.8 1.7 %collective-permute-start.6 = (bf16[192,3072]{1,0:T(8,128)(2,1)S(1)}, bf16[192,3072]{1,0:T(8,128)(2,1)}, u32[]{:S(2)}, u32[]{:S(2)}) collective-permute-start(bf16[192,3072]{1,0:T(8,128)(2,1)S(1)} %bitcast.20), channel_id=1, source_target_pairs={{0,8},{8,0},{16,24},{24,16},{32,40},{40,32},{48,56},{56,48},{64,72... | collective-permute-start | bytes 3538952 | tf_op jit(solution)/shard_map/ppermute | solution.py:24
  48.6 0.1 collective-permute-start.3
  48.7 14.9 %all-to-all-done.1.summed = bf16[8,192,384]{2,1,0:T(8,128)(2,1)S(1)} async-done(((bf16[8,192,384]{2,1,0:T(8,128)(2,1)}), bf16[8,192,384]{2,1,0:T(8,128)(2,1)S(1)}, u32[]{:S(2)}, u32[]{:S(2)}) %all-to-all-start.1) | async-done | bytes 1179680 | tf_op jit(solution)/shard_map/all_to_all | solution.py:209
  63.6 2.8 %collective-permute-start.2 = (bf16[8,192,384]{2,1,0:T(8,128)(2,1)S(1)}, bf16[8,192,384]{2,1,0:T(8,128)(2,1)}, u32[]{:S(2)}, u32[]{:S(2)}) collective-permute-start(bf16[8,192,384]{2,1,0:T(8,128)(2,1)S(1)} %all-to-all-done.1.summed), channel_id=1, source_target_pairs={{0,8},{8,0},{16,24},{24,16},{32,40},{40,32},{48,56},{56,48},{64,72... | collective-permute-start | bytes 3538952 | tf_op jit(solution)/shard_map/ppermute | solution.py:24
  66.4 0.0 collective-permute-done.6.residual
  66.4 4.0 %clip_other.1 = bf16[384,3072]{1,0:T(8,128)(2,1)} custom-call(s32[1]{0:T(128)S(6)} %sub.3.half, bf16[384,3072]{1,0:T(8,128)(2,1)} %bitcast.15, bf16[192,3072]{1,0:T(8,128)(2,1)} %collective-permute-done.6.residual, f32[384,12]{1,0:T(8,128)} %get-tuple-element.20.scales, bf16[384,3072]{1,0:T(8,128)(2,1)} %get-tuple-element.19.held), custom_call_target="tpu_custom_call", output_to_operand_aliasing={{}: (4, {})} | custom-call | flops 3538944 | bytes 3538944 | tf_op jit(solution)/shard_map/clip_other/pallas_call | solution.py:116
  70.4 6.3 %adam_half.2 = (bf16[384,3072]{1,0:T(8,128)(2,1)}, f32[384,3072]{1,0:T(8,128)}, f32[384,3072]{1,0:T(8,128)}) custom-call(s32[1]{0:T(128)} %bitcast.half, bf16[8,192,384]{2,1,0:T(8,128)(2,1)} %copy-done, bf16[192,3072]{1,0:T(8,128)(2,1)} %weight.1, f32[192,3072]{1,0:T(8,128)} %moment_one.1, f32[192,3072]{1,0:T(8,128)} %moment_two.1), custom_call_target="tpu_custom_call" | custom-call | flops 11796480 | bytes 12976128 | tf_op jit(solution)/shard_map/adam_half/pallas_call | solution.py:170
  76.7 0.0 collective-permute-done.3.weight
  76.7 0.0 collective-permute-done.4.moment_one
  76.7 0.0 collective-permute-done.5.moment_two
  76.7 0.0 collective-permute-done.2.summed
  76.7 6.3 %adam_half.3 = (bf16[384,3072]{1,0:T(8,128)(2,1)}, f32[384,3072]{1,0:T(8,128)}, f32[384,3072]{1,0:T(8,128)}) custom-call(s32[1]{0:T(128)S(6)} %sub.3.half, bf16[8,192,384]{2,1,0:T(8,128)(2,1)} %collective-permute-done.2.summed, bf16[192,3072]{1,0:T(8,128)(2,1)} %collective-permute-done.3.weight, ...), custom_call_target="tpu_custom_call", output_to_operand_aliasing={{0}: (5, {}), {1}: (6, {}), {2}: (7, {})} | custom-call | flops 11796480 | bytes 12976128 | tf_op jit(solution)/shard_map/adam_half/pallas_call | solution.py:170
  (11 shorter events, 0.0 us)
Async XLA Ops:
  0.6 2.9 %copy-start.6 = (s32[1,1,384,12]{2,1,3,0:T(1,128)S(1)}, s32[1,1,384,12]{2,1,3,0:T(1,128)}, u32[]{:S(2)}) copy-start(s32[1,1,384,12]{2,1,3,0:T(1,128)} %param.11) | copy-start | bytes 55300
  2.0 6.8 %collective-permute-start = (bf16[192,3072]{1,0:T(8,128)(2,1)S(1)}, bf16[192,3072]{1,0:T(8,128)(2,1)S(1)}, u32[]{:S(2)}, u32[]{:S(2)}) collective-permute-start(bf16[192,3072]{1,0:T(8,128)(2,1)S(1)} %dynamic-slice_bitcast_fusion), channel_id=1, source_target_pairs={{0,8},{8,0},{16,24},{24,16},{32,40},{40,32},{48,56},{56,48},{64,72... | collective-permute-start | bytes 3538952 | tf_op jit(solution)/shard_map/ppermute | solution.py:24
  4.4 4.3 %collective-permute-start.1 = (f32[192,12]{1,0:T(8,128)S(1)}, f32[192,12]{1,0:T(8,128)S(1)}, u32[]{:S(2)}, u32[]{:S(2)}) collective-permute-start(f32[192,12]{1,0:T(8,128)S(1)} %dynamic-slice_bitcast_fusion.1), channel_id=1, source_target_pairs={{0,8},{8,0},{16,24},{24,16},{32,40},{40,32},{48,56},{56,48},{64,72... | collective-permute-start | bytes 27656 | tf_op jit(solution)/shard_map/ppermute | solution.py:24
  8.8 0.6 copy-start.5
  8.8 1.0 %copy-start.4 = (bf16[192,3072]{1,0:T(8,128)(2,1)}, bf16[192,3072]{1,0:T(8,128)(2,1)S(1)}, u32[]{:S(2)}) copy-start(bf16[192,3072]{1,0:T(8,128)(2,1)S(1)} %collective-permute-done.grads) | copy-start | bytes 3538948
  14.1 24.7 %all-to-all-start = ((bf16[8,192,384]{2,1,0:T(8,128)(2,1)}), bf16[8,192,384]{2,1,0:T(8,128)(2,1)S(1)}, u32[]{:S(2)}, u32[]{:S(2)}) async-start(bf16[8,192,384]{2,1,0:T(8,128)(2,1)} %pair_sum.1), calls=%async_computation | async-start | bytes 2359296 | tf_op jit(solution)/shard_map/all_to_all | solution.py:208
  20.8 26.0 %copy-start.2 = (bf16[1,192,3072]{2,1,0:T(8,128)(2,1)S(1)}, bf16[1,192,3072]{2,1,0:T(8,128)(2,1)}, u32[]{:S(2)}) copy-start(bf16[1,192,3072]{2,1,0:T(8,128)(2,1)} %param.9) | copy-start | bytes 3538948
  20.8 27.7 %copy-start.3 = (bf16[192,3072]{1,0:T(8,128)(2,1)S(1)}, bf16[192,3072]{1,0:T(8,128)(2,1)}, u32[]{:S(2)}) copy-start(bf16[192,3072]{1,0:T(8,128)(2,1)} %weight.1) | copy-start | bytes 3538948
  20.8 55.8 %collective-permute-start.4 = (f32[192,3072]{1,0:T(8,128)}, f32[192,3072]{1,0:T(8,128)}, u32[]{:S(2)}, u32[]{:S(2)}) collective-permute-start(f32[192,3072]{1,0:T(8,128)} %moment_one.1), channel_id=1, source_target_pairs={{0,8},{8,0},{16,24},{24,16},{32,40},{40,32},{48,56},{56,48},{64,72... | collective-permute-start | bytes 7077896 | tf_op jit(solution)/shard_map/ppermute | solution.py:24
  21.7 55.0 %collective-permute-start.5 = (f32[192,3072]{1,0:T(8,128)}, f32[192,3072]{1,0:T(8,128)}, u32[]{:S(2)}, u32[]{:S(2)}) collective-permute-start(f32[192,3072]{1,0:T(8,128)} %moment_two.1), channel_id=1, source_target_pairs={{0,8},{8,0},{16,24},{24,16},{32,40},{40,32},{48,56},{56,48},{64,72... | collective-permute-start | bytes 7077896 | tf_op jit(solution)/shard_map/ppermute | solution.py:24
  38.8 1.0 %copy-start.1 = (bf16[8,192,384]{2,1,0:T(8,128)(2,1)}, bf16[8,192,384]{2,1,0:T(8,128)(2,1)S(1)}, u32[]{:S(2)}) copy-start(bf16[8,192,384]{2,1,0:T(8,128)(2,1)S(1)} %all-to-all-done.parts) | copy-start | bytes 3538948
  43.2 20.4 %all-to-all-start.1 = ((bf16[8,192,384]{2,1,0:T(8,128)(2,1)}), bf16[8,192,384]{2,1,0:T(8,128)(2,1)S(1)}, u32[]{:S(2)}, u32[]{:S(2)}) async-start(bf16[8,192,384]{2,1,0:T(8,128)(2,1)} %replica_sum.1), calls=%async_computation.1 | async-start | bytes 2359296 | tf_op jit(solution)/shard_map/all_to_all | solution.py:209
  46.8 19.6 %collective-permute-start.6 = (bf16[192,3072]{1,0:T(8,128)(2,1)S(1)}, bf16[192,3072]{1,0:T(8,128)(2,1)}, u32[]{:S(2)}, u32[]{:S(2)}) collective-permute-start(bf16[192,3072]{1,0:T(8,128)(2,1)S(1)} %bitcast.20), channel_id=1, source_target_pairs={{0,8},{8,0},{16,24},{24,16},{32,40},{40,32},{48,56},{56,48},{64,72... | collective-permute-start | bytes 3538952 | tf_op jit(solution)/shard_map/ppermute | solution.py:24
  48.6 28.1 %collective-permute-start.3 = (bf16[192,3072]{1,0:T(8,128)(2,1)S(1)}, bf16[192,3072]{1,0:T(8,128)(2,1)}, u32[]{:S(2)}, u32[]{:S(2)}) collective-permute-start(bf16[192,3072]{1,0:T(8,128)(2,1)S(1)} %copy-done.3), channel_id=1, source_target_pairs={{0,8},{8,0},{16,24},{24,16},{32,40},{40,32},{48,56},{56,48},{64,72... | collective-permute-start | bytes 3538952 | tf_op jit(solution)/shard_map/ppermute | solution.py:24
  63.6 6.8 %copy-start = (bf16[8,192,384]{2,1,0:T(8,128)(2,1)}, bf16[8,192,384]{2,1,0:T(8,128)(2,1)S(1)}, u32[]{:S(2)}) copy-start(bf16[8,192,384]{2,1,0:T(8,128)(2,1)S(1)} %all-to-all-done.1.summed) | copy-start | bytes 3538948
  63.6 13.1 %collective-permute-start.2 = (bf16[8,192,384]{2,1,0:T(8,128)(2,1)S(1)}, bf16[8,192,384]{2,1,0:T(8,128)(2,1)}, u32[]{:S(2)}, u32[]{:S(2)}) collective-permute-start(bf16[8,192,384]{2,1,0:T(8,128)(2,1)S(1)} %all-to-all-done.1.summed), channel_id=1, source_target_pairs={{0,8},{8,0},{16,24},{24,16},{32,40},{40,32},{48,56},{56,48},{64,72... | collective-permute-start | bytes 3538952 | tf_op jit(solution)/shard_map/ppermute | solution.py:24

commit v2 on v0

v2 whole, which is shorter than its diff:
```python
import functools

import jax
import jax.numpy as jnp
from jax import lax
from jax.experimental import pallas as pl
from jax.experimental.pallas import tpu as pltpu
from jax.sharding import PartitionSpec as P

BETA_ONE = 0.9
BETA_TWO = 0.95
LEARN_RATE = 0.001
EPSILON = 1e-08
BIAS_ONE = 1.0 - 0.9**10
BIAS_TWO = 1.0 - 0.95**10
BLOCK = 256
PIECES = 3
LANES = 128
OWN_STEPS = 4
VMEM_LIMIT = 12 * 2**20
F32 = jnp.float32
BF16 = jnp.bfloat16
IN_VMEM = pl.BlockSpec(memory_space=pltpu.VMEM)
IN_HBM = pl.BlockSpec(memory_space=pltpu.HBM)


def core_swap(value):
    pairs = [(source, source ^ 1) for source in range(lax.axis_size("section"))]
    return lax.ppermute(value, "section", pairs)


def cube_swap(value, dim):
    count = lax.axis_size("dp")
    if dim == 0:
        pairs = [(source, source ^ 2) for source in range(count)]
    elif dim == 1:
        pairs = [(source, (3 - source // 2) * 2 + source % 2) for source in range(count)]
    else:
        pairs = [(source, source ^ 1) for source in range(count)]
    return lax.ppermute(value, "dp", pairs)


def core_parity():
    return lax.axis_index("section").astype(jnp.int32) % 2


def cube_bits():
    replica = lax.axis_index("dp").astype(jnp.int32)
    y = replica // 2
    return [((y + 1) // 2) % 2, y // 2, replica % 2]


class HbmOut(tuple):
    pass


def call(body, outs, operands, flops, moved, name, scratch=(), aliases=None, in_hbm=0):
    near = operands[: len(operands) - in_hbm]
    far = operands[len(operands) - in_hbm :]
    return pl.pallas_call(
        body,
        in_specs=[IN_VMEM] * len(near) + [IN_HBM] * in_hbm,
        out_specs=[IN_HBM if isinstance(out, HbmOut) else IN_VMEM for out in outs],
        out_shape=[
            (pltpu.HBM if isinstance(out, HbmOut) else pltpu.VMEM)(out[0], out[1]) for out in outs
        ],
        scratch_shapes=list(scratch),
        input_output_aliases=aliases or {},
        compiler_params=pltpu.CompilerParams(vmem_limit_bytes=VMEM_LIMIT),
        cost_estimate=pl.CostEstimate(flops=flops, bytes_accessed=moved, transcendentals=0),
        name=name,
    )(
        *[pltpu.with_memory_space_constraint(value, pltpu.VMEM) for value in near],
        *[pltpu.with_memory_space_constraint(value, pltpu.HBM) for value in far],
    )


def aligned(start, size):
    return pl.ds(pl.multiple_of(start, 32), size)


def message_kernel(exponents, grads, message, scales, read, turned, sems):
    rows, columns = message.shape[0], grads.shape[1]
    base = (1 - core_parity()) * rows
    part = rows // 4
    first = pltpu.make_async_copy(exponents, read, sems.at[4])
    first.start()
    copies = []
    for at in range(4):
        copies.append(
            pltpu.make_async_copy(
                grads.at[aligned(base + at * part, part)],
                message.at[pl.ds(at * part, part), pl.ds(0, columns)],
                sems.at[at],
            )
        )
        copies[-1].start()
    turned[...] = jnp.zeros_like(turned)
    first.wait()
    for block in range(exponents.shape[0]):
        turned[block : block + 1, :] = read[block].astype(F32)
    scales[...] = jnp.exp2(turned[...].T).astype(BF16)
    message[:, columns:] = scales[aligned(base, rows), :]
    for copy in copies:
        copy.wait()


def make_message(exponents, grads, rows):
    blocks, _, all_rows = exponents.shape
    columns = grads.shape[1]
    return call(
        message_kernel,
        [((rows, columns + LANES), BF16), ((all_rows, LANES), BF16)],
        [exponents, grads],
        0,
        2 * rows * columns,
        "make_message",
        scratch=[
            pltpu.VMEM(exponents.shape, exponents.dtype),
            pltpu.VMEM((LANES, all_rows), F32),
            pltpu.SemaphoreType.DMA((5,)),
        ],
        in_hbm=2,
    )


def own_kernel(scales, grads, residual, clipped, carried, read, sems):
    rows, columns = residual.shape
    base = core_parity() * rows
    part = rows // OWN_STEPS
    copies = []
    for step in range(OWN_STEPS):
        here = pl.ds(step * part, part)
        there = aligned(base + step * part, part)
        copies.append(
            (
                pltpu.make_async_copy(grads.at[there], read.at[here], sems.at[0, step]),
                pltpu.make_async_copy(residual.at[here], carried.at[here], sems.at[1, step]),
            )
        )
        for copy in copies[-1]:
            copy.start()
    for step in range(OWN_STEPS):
        for copy in copies[step]:
            copy.wait()
        here = slice(step * part, (step + 1) * part)
        scale = scales[aligned(base + step * part, part), :]
        for block in range(columns // BLOCK):
            at = slice(block * BLOCK, (block + 1) * BLOCK)
            limit = scale[:, block : block + 1]
            clipped[here, at] = jnp.clip(read[here, at] + carried[here, at], -limit, limit)


def clip_own(scales, grads, residual):
    rows, columns = residual.shape
    return call(
        own_kernel,
        [(residual.shape, BF16)] * 2,
        [scales, grads, residual],
        4 * rows * columns,
        4 * rows * columns,
        "clip_own",
        scratch=[pltpu.VMEM(residual.shape, BF16), pltpu.SemaphoreType.DMA((2, OWN_STEPS))],
        in_hbm=2,
    )


def pair_kernel(clipped, residual, message, *outs):
    rows, columns = residual.shape
    half, width = rows // 2, columns // PIECES
    for piece in range(PIECES):
        bit = cube_bits()[piece]
        for out, start in ((outs[piece], 1 - bit), (outs[PIECES + piece], bit)):
            here = aligned(start * half, half)
            scale = message[here, columns:]
            for block in range(piece * width // BLOCK, (piece + 1) * width // BLOCK):
                at = slice(block * BLOCK, (block + 1) * BLOCK)
                to = slice(block * BLOCK - piece * width, (block + 1) * BLOCK - piece * width)
                limit = scale[:, block : block + 1]
                partner = jnp.clip(message[here, at] + residual[here, at], -limit, limit)
                out[:, to] = clipped[here, at] + partner


def pair_sums(clipped, residual, message):
    rows, columns = residual.shape
    size = rows * columns
    outs = call(
        pair_kernel,
        [((rows // 2, columns // PIECES), BF16)] * (2 * PIECES),
        [clipped, residual, message],
        5 * size,
        size,
        "pair_sums",
    )
    return outs[:PIECES], outs[PIECES:]


def add_kernel(*refs):
    for mine, theirs, out in zip(refs[:PIECES], refs[PIECES : 2 * PIECES], refs[2 * PIECES :]):
        out[...] = mine[...] + theirs[...]


def added(mine, theirs):
    outs = [(value.shape, BF16) for value in mine]
    return call(add_kernel, outs, [*mine, *theirs], 3 * mine[0].size, 0, "added")


def residual_kernel(scales, residual, partner_residual, grads, out, held, read, sems):
    rows, columns = residual.shape
    part = rows // OWN_STEPS
    parity = core_parity()
    work = []
    for side, source in ((0, residual), (1, partner_residual)):
        base = (parity if side == 0 else 1 - parity) * rows
        for step in range(OWN_STEPS):
            here = pl.ds(step * part, part)
            there = aligned(base + step * part, part)
            work.append(
                (
                    pltpu.make_async_copy(
                        grads.at[there], read.at[side, here], sems.at[0, side, step]
                    ),
                    pltpu.make_async_copy(
                        held.at[side, here], out.at[there], sems.at[1, side, step]
                    ),
                    side,
                    source,
                    here,
                    there,
                )
            )
            work[-1][0].start()
    for arrive, leave, side, source, here, there in work:
        arrive.wait()
        scale = scales[there, :]
        for block in range(columns // BLOCK):
            at = slice(block * BLOCK, (block + 1) * BLOCK)
            limit = scale[:, block : block + 1]
            summand = read[side, here, at].astype(F32) + source[here, at].astype(F32)
            kept = jnp.clip(summand.astype(BF16), -limit, limit)
            held[side, here, at] = (summand - kept.astype(F32)).astype(BF16)
        leave.start()
    for arrive, leave, *_ in work:
        leave.wait()


def new_residual(scales, residual, partner_residual, grads):
    rows, columns = residual.shape
    size = rows * columns
    return call(
        residual_kernel,
        [HbmOut((grads.shape, BF16))],
        [scales, residual, partner_residual, grads],
        12 * size,
        12 * size,
        "new_residual",
        scratch=[
            pltpu.VMEM((2, rows, columns), BF16),
            pltpu.VMEM((2, rows, columns), BF16),
            pltpu.SemaphoreType.DMA((2, 2, OWN_STEPS)),
        ],
        in_hbm=1,
    )[0]


def adam_kernel(flip_core, flip_cube, *refs):
    summed = refs[:PIECES]
    weight, moment_one, moment_two = refs[PIECES : PIECES + 3]
    outs = refs[-7:-4]
    held, sems = refs[-4:-1], refs[-1]
    _, half, width = held[0].shape
    parity = core_parity()
    parity = 1 - parity if flip_core else parity
    copies = []
    for piece in range(PIECES):
        bit = cube_bits()[piece]
        start = (1 - bit if flip_cube else bit) * half
        here = aligned(start, half)
        there = aligned(parity * 2 * half + start, half)
        for block in range(width // BLOCK):
            to = slice(block * BLOCK, (block + 1) * BLOCK)
            at = slice(piece * width + block * BLOCK, piece * width + (block + 1) * BLOCK)
            averaged = summed[piece][:, to].astype(F32) * (1.0 / 16.0)
            moment_a = BETA_ONE * moment_one[here, at] + (1.0 - BETA_ONE) * averaged
            moment_b = BETA_TWO * moment_two[here, at] + (1.0 - BETA_TWO) * averaged * averaged
            update = (LEARN_RATE / BIAS_ONE) * moment_a
            update = update / (jnp.sqrt(moment_b * (1.0 / BIAS_TWO)) + EPSILON)
            held[0][piece, :, to] = (weight[here, at].astype(F32) - update).astype(BF16)
            held[1][piece, :, to] = moment_a
            held[2][piece, :, to] = moment_b
        for kind in range(3):
            copies.append(
                pltpu.make_async_copy(
                    held[kind].at[piece],
                    outs[kind].at[there, pl.ds(piece * width, width)],
                    sems.at[kind, piece],
                )
            )
            copies[-1].start()
    for copy in copies:
        copy.wait()


def adam_quarter(flip_core, flip_cube, summed, weight, moment_one, moment_two, filled):
    rows, columns = weight.shape
    half, width = rows // 2, columns // PIECES
    kinds = (BF16, F32, F32)
    size = half * columns
    given = [*summed, weight, moment_one, moment_two]
    return call(
        functools.partial(adam_kernel, flip_core, flip_cube),
        [HbmOut(((2 * rows, columns), kind)) for kind in kinds],
        given + list(filled),
        30 * size,
        10 * size,
        "adam_quarter",
        scratch=[pltpu.VMEM((PIECES, half, width), kind) for kind in kinds]
        + [pltpu.SemaphoreType.DMA((3, PIECES))],
        aliases={len(given) + at: at for at in range(len(filled))},
        in_hbm=len(filled),
    )


def together(*values):
    return lax.optimization_barrier(values)


def shards(weight_old, moment_one, moment_two, residual_old, grads, exponents):
    residual = residual_old[0]
    grads = grads[0, 0]
    rows = residual.shape[0]
    exponents = exponents[0].transpose(2, 0, 1)

    message, scales = make_message(exponents, grads, rows)
    partner_message = core_swap(message)
    clipped, carried = clip_own(scales, grads, residual)
    sent, kept = pair_sums(clipped, carried, partner_message)

    def cube_step(sent, step):
        return [cube_swap(sent[piece], (piece + step) % 3) for piece in range(PIECES)]

    sent, residual, weight = together(sent, residual, weight_old)
    arrived = cube_step(sent, 0)
    arrived, partner_residual, partner_weight = together(
        arrived, core_swap(residual), core_swap(weight)
    )
    kept = added(kept, arrived)

    kept, one, two, partner_residual = together(kept, moment_one, moment_two, partner_residual)
    arrived = cube_step(kept, 1)
    left = new_residual(scales, carried, partner_residual, grads)
    arrived, partner_one, partner_two, left = together(
        arrived, core_swap(one), core_swap(two), left
    )
    kept = added(kept, arrived)

    arrived = cube_step(kept, 2)
    arrived = together(*arrived)
    kept = added(kept, arrived)

    own_old = (weight_old, moment_one, moment_two)
    partner_old = (partner_weight, partner_one, partner_two)
    gathered = cube_step(kept, 0)
    partner_kept = [core_swap(value) for value in kept]
    filled = adam_quarter(False, False, kept, *own_old, ())
    filled = adam_quarter(True, False, partner_kept, *partner_old, filled)
    gathered, filled = together(gathered, filled)
    partner_gathered = [core_swap(value) for value in gathered]
    filled = adam_quarter(False, True, gathered, *own_old, filled)
    filled = adam_quarter(True, True, partner_gathered, *partner_old, filled)
    return (filled[0][None], filled[1][None], filled[2][None], left[None, None])


def solution(mesh):
    in_specs = (
        P("section", None),
        P("section", None),
        P("section", None),
        P("dp", "section", None),
        P("dp", "section", None, None),
        P("dp", "section", None, None),
    )
    out_specs = (
        P("section", None, None),
        P("section", None, None),
        P("section", None, None),
        P("dp", "section", None, None),
    )
    return jax.shard_map(shards, mesh=mesh, in_specs=in_specs, out_specs=out_specs, check_vma=False)
```

time: 185 us -> 56 us (0.30)
  waiting for transfers between devices: 87.9 us -> 12.1 us
  local copies, waits for them, and re-layouts: 48.7 us -> 0.01 us
  other arithmetic: 30.3 us -> 0 us
  starting transfers between devices: 3.12 us -> 26.7 us
  Pallas kernels: 0 us -> 16.2 us
  between operations: 14.1 us -> 0.8 us
    psum x1 -> x0, waiting for transfers between devices: 87.9 us -> none  [shards(): lax.psum(clipped.astype(jnp.float32).astype(jnp.bfloat16), 'dp')]
    unnamed x30 -> x8, local copies, waits for them, and re-layouts: 38.3 us -> 0.01 us
    ppermute x5 -> x23, starting transfers between devices: 3.08 us -> 26.7 us  [the longest x12 17.3 us: cube_swap(): return lax.ppermute(value, 'dp', pairs)]
    pallas_call x0 -> x11, Pallas kernels: none -> 16.2 us  [call(): pl.pallas_call(body, in_specs=[IN_VMEM] * len(near) + [IN_HBM] * in_hbm,...]
    ppermute x5 -> x23, waiting for transfers between devices: 0.01 us -> 12.1 us  [the longest x12 11.8 us: cube_swap(): return lax.ppermute(value, 'dp', pairs)]
    broadcast_in_dim x1 -> x0, other arithmetic: 10.2 us -> none  [shards(): return (updated[None], moment_a[None], moment_b[None], new_residual)]
    convert_element_type x4 -> x0, other arithmetic: 9.36 us -> none  [the longest x1 3.39 us: shards(): (summand - clipped.astype(jnp.float32)).astype(jnp.bfloat16)[None, None]]
    ppermute x4 -> x0, local copies, waits for them, and re-layouts: 9.1 us -> none  [swapped(): return lax.ppermute(value, axis, pairs)]
  transfers between devices with their start and end apart: 6 -> 23, of which waited for: 1 -> 10; matrix products, arithmetic and copies ran while one was open for 22% -> 0% of each run, Pallas kernels for 0% -> 22%
where the time goes in v2:
time: 56 us; the launch traced here: 55.8 us
  starting transfers between devices  26.7 us (48%)
  Pallas kernels  16.2 us (29%)
  waiting for transfers between devices  12.1 us (22%)
  between operations  0.8 us (1%)
    ppermute x12, starting transfers between devices, cube_swap(): return lax.ppermute(value, 'dp', pairs)  17.3 us
    pallas_call x11, Pallas kernels, call(): pl.pallas_call(body, in_specs=[IN_VMEM] * len(near) + [IN_HBM] * in_hbm,...  16.2 us
    ppermute x12, waiting for transfers between devices, cube_swap(): return lax.ppermute(value, 'dp', pairs)  11.8 us
    ppermute x11, starting transfers between devices, core_swap(): return lax.ppermute(value, 'section', pairs)  9.42 us
  transfers between devices with their start and end apart: 23, of which 10 were waited for; matrix products, arithmetic and copies ran while one was open for 0% of the time, Pallas kernels for 22%

profile of v2, /device:TPU:1, one launch (start us, length us, event | category | flops | bytes accessed | tf_op | source)
XLA Modules:
  0.0 55.8 jit_solution(9570891601850135923)
XLA Ops:
  0.6 1.3 %make_message.1 = (bf16[192,3200]{1,0:T(8,128)(2,1)S(1)}, bf16[384,128]{1,0:T(8,128)(2,1)S(1)}) custom-call(s32[12,1,384]{2,1,0:T(1,128)} %bitcast.18, bf16[384,3072]{1,0:T(8,128)(2,1)} %bitcast.12), custom_call_target="tpu_custom_call" | custom-call | bytes 1179648 | tf_op jit(solution)/shard_map/make_message/pallas_call | solution.py:60
  1.9 1.5 %collective-permute-start = (bf16[192,3200]{1,0:T(8,128)(2,1)S(1)}, bf16[192,3200]{1,0:T(8,128)(2,1)S(1)}, u32[]{:S(2)}, u32[]{:S(2)}) collective-permute-start(bf16[192,3200]{1,0:T(8,128)(2,1)S(1)} %get-tuple-element.69), channel_id=1, source_target_pairs={{0,8},{8,0},{16,24},{24,16},{32,40},{40,32},{48,56},{56,48},{64,72... | collective-permute-start | bytes 3686408 | tf_op jit(solution)/shard_map/ppermute | solution.py:29
  3.4 2.2 %clip_own.1 = (bf16[192,3072]{1,0:T(8,128)(2,1)S(1)}, bf16[192,3072]{1,0:T(8,128)(2,1)S(1)}) custom-call(bf16[384,128]{1,0:T(8,128)(2,1)S(1)} %get-tuple-element.66.scales, bf16[384,3072]{1,0:T(8,128)(2,1)} %bitcast.13, bf16[192,3072]{1,0:T(8,128)(2,1)} %bitcast.16), custom_call_target="tpu_custom_call" | custom-call | flops 2359296 | bytes 2359296 | tf_op jit(solution)/shard_map/clip_own/pallas_call | solution.py:60
  6.0 0.7 %pair_sums.1 = (bf16[96,1024]{1,0:T(8,128)(2,1)S(1)}, bf16[96,1024]{1,0:T(8,128)(2,1)S(1)}, bf16[96,1024]{1,0:T(8,128)(2,1)S(1)}, bf16[96,1024]{1,0:T(8,128)(2,1...) custom-call(bf16[192,3072]{1,0:T(8,128)(2,1)S(1)} %get-tuple-element.67.clipped, ...), custom_call_target="tpu_custom_call" | custom-call | flops 2949120 | bytes 589824 | tf_op jit(solution)/shard_map/pair_sums/pallas_call | solution.py:60
  6.7 0.5 collective-permute-start.4
  7.3 1.4 %collective-permute-start.1 = (bf16[96,1024]{1,0:T(8,128)(2,1)S(1)}, bf16[96,1024]{1,0:T(8,128)(2,1)S(1)}, u32[]{:S(2)}, u32[]{:S(2)}) collective-permute-start(bf16[96,1024]{1,0:T(8,128)(2,1)S(1)} %get-tuple-element.76), channel_id=1, source_target_pairs={{0,2},{1,3},{2,0},{3,1},{4,6},{5,7},{6,4},{7,5},{8,10},{9,11},{10,... | collective-permute-start | bytes 589832 | tf_op jit(solution)/shard_map/ppermute | solution.py:40
  8.7 1.9 %collective-permute-start.2 = (bf16[96,1024]{1,0:T(8,128)(2,1)S(1)}, bf16[96,1024]{1,0:T(8,128)(2,1)S(1)}, u32[]{:S(2)}, u32[]{:S(2)}) collective-permute-start(bf16[96,1024]{1,0:T(8,128)(2,1)S(1)} %get-tuple-element.77), channel_id=1, source_target_pairs={{0,6},{1,7},{2,4},{3,5},{4,2},{5,3},{6,0},{7,1},{8,14},{9,15},{10,... | collective-permute-start | bytes 589832 | tf_op jit(solution)/shard_map/ppermute | solution.py:40
  10.6 2.7 %collective-permute-start.3 = (bf16[96,1024]{1,0:T(8,128)(2,1)S(1)}, bf16[96,1024]{1,0:T(8,128)(2,1)S(1)}, u32[]{:S(2)}, u32[]{:S(2)}) collective-permute-start(bf16[96,1024]{1,0:T(8,128)(2,1)S(1)} %get-tuple-element.78), channel_id=1, source_target_pairs={{0,1},{1,0},{2,3},{3,2},{4,5},{5,4},{6,7},{7,6},{8,9},{9,8},{10,11... | collective-permute-start | bytes 589832 | tf_op jit(solution)/shard_map/ppermute | solution.py:40
  13.4 2.3 %collective-permute-done.2.refs_4_ = bf16[96,1024]{1,0:T(8,128)(2,1)S(1)} collective-permute-done((bf16[96,1024]{1,0:T(8,128)(2,1)S(1)}, bf16[96,1024]{1,0:T(8,128)(2,1)S(1)}, u32[]{:S(2)}, u32[]{:S(2)}) %collective-permute-start.2) | collective-permute-done | bytes 196640 | tf_op jit(solution)/shard_map/ppermute | solution.py:40
  15.7 1.9 %collective-permute-done.3.refs_5_ = bf16[96,1024]{1,0:T(8,128)(2,1)S(1)} collective-permute-done((bf16[96,1024]{1,0:T(8,128)(2,1)S(1)}, bf16[96,1024]{1,0:T(8,128)(2,1)S(1)}, u32[]{:S(2)}, u32[]{:S(2)}) %collective-permute-start.3) | collective-permute-done | bytes 196640 | tf_op jit(solution)/shard_map/ppermute | solution.py:40
  17.7 1.9 %collective-permute-start.9 = (f32[192,3072]{1,0:T(8,128)S(1)}, f32[192,3072]{1,0:T(8,128)S(1)}, u32[]{:S(2)}, u32[]{:S(2)}) collective-permute-start(f32[192,3072]{1,0:T(8,128)S(1)} %copy-done), channel_id=1, source_target_pairs={{0,8},{8,0},{16,24},{24,16},{32,40},{40,32},{48,56},{56,48},{64,72... | collective-permute-start | bytes 7077896 | tf_op jit(solution)/shard_map/ppermute | solution.py:29
  19.7 0.8 %collective-permute-start.6 = (bf16[96,1024]{1,0:T(8,128)(2,1)S(1)}, bf16[96,1024]{1,0:T(8,128)(2,1)S(1)}, u32[]{:S(2)}, u32[]{:S(2)}) collective-permute-start(bf16[96,1024]{1,0:T(8,128)(2,1)S(1)} %get-tuple-element.88.refs_0_), channel_id=1, source_target_pairs={{0,6},{1,7},{2,4},{3,5},{4,2},{5,3},{6,0},{7,1},{8,14},{9,15},{10,... | collective-permute-start | bytes 589832 | tf_op jit(solution)/shard_map/ppermute | solution.py:40
  20.5 2.7 %collective-permute-start.7 = (bf16[96,1024]{1,0:T(8,128)(2,1)S(1)}, bf16[96,1024]{1,0:T(8,128)(2,1)S(1)}, u32[]{:S(2)}, u32[]{:S(2)}) collective-permute-start(bf16[96,1024]{1,0:T(8,128)(2,1)S(1)} %get-tuple-element.89.refs_1_), channel_id=1, source_target_pairs={{0,1},{1,0},{2,3},{3,2},{4,5},{5,4},{6,7},{7,6},{8,9},{9,8},{10,11... | collective-permute-start | bytes 589832 | tf_op jit(solution)/shard_map/ppermute | solution.py:40
  23.2 3.8 %new_residual.1 = bf16[384,3072]{1,0:T(8,128)(2,1)} custom-call(bf16[384,128]{1,0:T(8,128)(2,1)S(1)} %get-tuple-element.66.scales, bf16[192,3072]{1,0:T(8,128)(2,1)S(1)} %get-tuple-element.68.residual, bf16[192,3072]{1,0:T(8,128)(2,1)S(1)} %collective-permute-done.4.partner_residual, bf16[384,3072]{1,0:T(8,128)(2,1)} %bitcast.14), custom_call_target="tpu_custom_call" | custom-call | flops 7077888 | bytes 7077888 | tf_op jit(solution)/shard_map/new_residual/pallas_call | solution.py:60
  27.0 0.7 %collective-permute-done.7.refs_4_ = bf16[96,1024]{1,0:T(8,128)(2,1)S(1)} collective-permute-done((bf16[96,1024]{1,0:T(8,128)(2,1)S(1)}, bf16[96,1024]{1,0:T(8,128)(2,1)S(1)}, u32[]{:S(2)}, u32[]{:S(2)}) %collective-permute-start.7) | collective-permute-done | bytes 196640 | tf_op jit(solution)/shard_map/ppermute | solution.py:40
  27.7 0.9 %collective-permute-done.8.refs_5_ = bf16[96,1024]{1,0:T(8,128)(2,1)S(1)} collective-permute-done((bf16[96,1024]{1,0:T(8,128)(2,1)S(1)}, bf16[96,1024]{1,0:T(8,128)(2,1)S(1)}, u32[]{:S(2)}, u32[]{:S(2)}) %collective-permute-start.8) | collective-permute-done | bytes 196640 | tf_op jit(solution)/shard_map/ppermute | solution.py:40
  28.7 1.9 %collective-permute-start.11 = (bf16[96,1024]{1,0:T(8,128)(2,1)S(1)}, bf16[96,1024]{1,0:T(8,128)(2,1)S(1)}, u32[]{:S(2)}, u32[]{:S(2)}) collective-permute-start(bf16[96,1024]{1,0:T(8,128)(2,1)S(1)} %get-tuple-element.97.refs_0_), channel_id=1, source_target_pairs={{0,1},{1,0},{2,3},{3,2},{4,5},{5,4},{6,7},{7,6},{8,9},{9,8},{10,11... | collective-permute-start | bytes 589832 | tf_op jit(solution)/shard_map/ppermute | solution.py:40
  30.6 1.9 %collective-permute-start.13 = (bf16[96,1024]{1,0:T(8,128)(2,1)S(1)}, bf16[96,1024]{1,0:T(8,128)(2,1)S(1)}, u32[]{:S(2)}, u32[]{:S(2)}) collective-permute-start(bf16[96,1024]{1,0:T(8,128)(2,1)S(1)} %get-tuple-element.99.refs_2_), channel_id=1, source_target_pairs={{0,6},{1,7},{2,4},{3,5},{4,2},{5,3},{6,0},{7,1},{8,14},{9,15},{10,... | collective-permute-start | bytes 589832 | tf_op jit(solution)/shard_map/ppermute | solution.py:40
  32.5 2.3 %collective-permute-done.11.refs_3_ = bf16[96,1024]{1,0:T(8,128)(2,1)S(1)} collective-permute-done((bf16[96,1024]{1,0:T(8,128)(2,1)S(1)}, bf16[96,1024]{1,0:T(8,128)(2,1)S(1)}, u32[]{:S(2)}, u32[]{:S(2)}) %collective-permute-start.11) | collective-permute-done | bytes 196640 | tf_op jit(solution)/shard_map/ppermute | solution.py:40
  34.8 0.6 %collective-permute-done.12.refs_4_ = bf16[96,1024]{1,0:T(8,128)(2,1)S(1)} collective-permute-done((bf16[96,1024]{1,0:T(8,128)(2,1)S(1)}, bf16[96,1024]{1,0:T(8,128)(2,1)S(1)}, u32[]{:S(2)}, u32[]{:S(2)}) %collective-permute-start.12) | collective-permute-done | bytes 196640 | tf_op jit(solution)/shard_map/ppermute | solution.py:40
  35.4 1.2 %collective-permute-done.13.refs_5_ = bf16[96,1024]{1,0:T(8,128)(2,1)S(1)} collective-permute-done((bf16[96,1024]{1,0:T(8,128)(2,1)S(1)}, bf16[96,1024]{1,0:T(8,128)(2,1)S(1)}, u32[]{:S(2)}, u32[]{:S(2)}) %collective-permute-start.13) | collective-permute-done | bytes 196640 | tf_op jit(solution)/shard_map/ppermute | solution.py:40
  36.7 2.8 %collective-permute-start.17 = (bf16[96,1024]{1,0:T(8,128)(2,1)S(1)}, bf16[96,1024]{1,0:T(8,128)(2,1)S(1)}, u32[]{:S(2)}, u32[]{:S(2)}) collective-permute-start(bf16[96,1024]{1,0:T(8,128)(2,1)S(1)} %get-tuple-element.103.refs_0_), channel_id=1, source_target_pairs={{0,8},{8,0},{16,24},{24,16},{32,40},{40,32},{48,56},{56,48},{64,72... | collective-permute-start | bytes 589832 | tf_op jit(solution)/shard_map/ppermute | solution.py:29
  40.0 0.5 collective-permute-start.14
  40.6 1.9 %collective-permute-start.15 = (bf16[96,1024]{1,0:T(8,128)(2,1)S(1)}, bf16[96,1024]{1,0:T(8,128)(2,1)S(1)}, u32[]{:S(2)}, u32[]{:S(2)}) collective-permute-start(bf16[96,1024]{1,0:T(8,128)(2,1)S(1)} %get-tuple-element.104.refs_1_), channel_id=1, source_target_pairs={{0,6},{1,7},{2,4},{3,5},{4,2},{5,3},{6,0},{7,1},{8,14},{9,15},{10,... | collective-permute-start | bytes 589832 | tf_op jit(solution)/shard_map/ppermute | solution.py:40
  42.5 1.5 %collective-permute-start.16 = (bf16[96,1024]{1,0:T(8,128)(2,1)S(1)}, bf16[96,1024]{1,0:T(8,128)(2,1)S(1)}, u32[]{:S(2)}, u32[]{:S(2)}) collective-permute-start(bf16[96,1024]{1,0:T(8,128)(2,1)S(1)} %get-tuple-element.105.refs_2_), channel_id=1, source_target_pairs={{0,1},{1,0},{2,3},{3,2},{4,5},{5,4},{6,7},{7,6},{8,9},{9,8},{10,11... | collective-permute-start | bytes 589832 | tf_op jit(solution)/shard_map/ppermute | solution.py:40
  43.9 2.0 %adam_quarter.4 = (bf16[384,3072]{1,0:T(8,128)(2,1)}, f32[384,3072]{1,0:T(8,128)}, f32[384,3072]{1,0:T(8,128)}) custom-call(bf16[96,1024]{1,0:T(8,128)(2,1)S(1)} %get-tuple-element.103.refs_0_, bf16[96,1024]{1,0:T(8,128)(2,1)S(1)} %get-tuple-element.104.refs_1_, bf16[96,1024]{1,0:T(8,128)(2,1)S(1)} %get-tuple-element.105.refs_2_, ...), custom_call_target="tpu_custom_call" | custom-call | flops 8847360 | bytes 2949120 | tf_op jit(solution)/shard_map/adam_quarter/pallas_call | solution.py:60
  45.9 2.0 %adam_quarter.5 = (bf16[384,3072]{1,0:T(8,128)(2,1)}, f32[384,3072]{1,0:T(8,128)}, f32[384,3072]{1,0:T(8,128)}) custom-call(bf16[96,1024]{1,0:T(8,128)(2,1)S(1)} %collective-permute-done.17.refs_0_, bf16[96,1024]{1,0:T(8,128)(2,1)S(1)} %collective-permute-done.18.refs_1_, ...), custom_call_target="tpu_custom_call", output_to_operand_aliasing={{0}: (6, {}), {1}: (7, {}), {2}: (8, {})} | custom-call | flops 8847360 | bytes 2949120 | tf_op jit(solution)/shard_map/adam_quarter/pallas_call | solution.py:60
  48.0 1.8 %collective-permute-done.16.refs_2_ = bf16[96,1024]{1,0:T(8,128)(2,1)S(1)} collective-permute-done((bf16[96,1024]{1,0:T(8,128)(2,1)S(1)}, bf16[96,1024]{1,0:T(8,128)(2,1)S(1)}, u32[]{:S(2)}, u32[]{:S(2)}) %collective-permute-start.16) | collective-permute-done | bytes 196640 | tf_op jit(solution)/shard_map/ppermute | solution.py:40
  49.8 1.5 %collective-permute-start.20 = (bf16[96,1024]{1,0:T(8,128)(2,1)S(1)}, bf16[96,1024]{1,0:T(8,128)(2,1)S(1)}, u32[]{:S(2)}, u32[]{:S(2)}) collective-permute-start(bf16[96,1024]{1,0:T(8,128)(2,1)S(1)} %collective-permute-done.14.refs_0_), channel_id=1, source_target_pairs={{0,8},{8,0},{16,24},{24,16},{32,40},{40,32},{48,56},{56,48},{64,72... | collective-permute-start | bytes 589832 | tf_op jit(solution)/shard_map/ppermute | solution.py:29
  51.3 0.5 collective-permute-start.22
  51.8 2.0 %adam_quarter.6 = (bf16[384,3072]{1,0:T(8,128)(2,1)}, f32[384,3072]{1,0:T(8,128)}, f32[384,3072]{1,0:T(8,128)}) custom-call(bf16[96,1024]{1,0:T(8,128)(2,1)S(1)} %collective-permute-done.14.refs_0_, bf16[96,1024]{1,0:T(8,128)(2,1)S(1)} %collective-permute-done.15.refs_1_, ...), custom_call_target="tpu_custom_call", output_to_operand_aliasing={{0}: (6, {}), {1}: (7, {}), {2}: (8, {})} | custom-call | flops 8847360 | bytes 2949120 | tf_op jit(solution)/shard_map/adam_quarter/pallas_call | solution.py:60
  53.8 2.0 %adam_quarter.7 = (bf16[384,3072]{1,0:T(8,128)(2,1)}, f32[384,3072]{1,0:T(8,128)}, f32[384,3072]{1,0:T(8,128)}) custom-call(bf16[96,1024]{1,0:T(8,128)(2,1)S(1)} %collective-permute-done.20.refs_0_, bf16[96,1024]{1,0:T(8,128)(2,1)S(1)} %collective-permute-done.21.refs_1_, ...), custom_call_target="tpu_custom_call", output_to_operand_aliasing={{0}: (6, {}), {1}: (7, {}), {2}: (8, {})} | custom-call | flops 8847360 | bytes 2949120 | tf_op jit(solution)/shard_map/adam_quarter/pallas_call | solution.py:60
  (33 shorter events, 1.4 us)
Async XLA Ops:
  1.9 4.0 %collective-permute-start = (bf16[192,3200]{1,0:T(8,128)(2,1)S(1)}, bf16[192,3200]{1,0:T(8,128)(2,1)S(1)}, u32[]{:S(2)}, u32[]{:S(2)}) collective-permute-start(bf16[192,3200]{1,0:T(8,128)(2,1)S(1)} %get-tuple-element.69), channel_id=1, source_target_pairs={{0,8},{8,0},{16,24},{24,16},{32,40},{40,32},{48,56},{56,48},{64,72... | collective-permute-start | bytes 3686408 | tf_op jit(solution)/shard_map/ppermute | solution.py:29
  3.4 3.3 %copy-start.3 = (bf16[1,192,3072]{2,1,0:T(8,128)(2,1)S(1)}, bf16[1,192,3072]{2,1,0:T(8,128)(2,1)}, u32[]{:S(2)}) copy-start(bf16[1,192,3072]{2,1,0:T(8,128)(2,1)} %param.9) | copy-start | bytes 3538948
  3.4 3.7 %copy-start.2 = (bf16[192,3072]{1,0:T(8,128)(2,1)S(1)}, bf16[192,3072]{1,0:T(8,128)(2,1)}, u32[]{:S(2)}) copy-start(bf16[192,3072]{1,0:T(8,128)(2,1)} %refs_3_.3) | copy-start | bytes 3538948
  6.0 11.7 %copy-start = (f32[192,3072]{1,0:T(8,128)S(1)}, f32[192,3072]{1,0:T(8,128)}, u32[]{:S(2)}) copy-start(f32[192,3072]{1,0:T(8,128)} %refs_4_.3) | copy-start | bytes 7077892
  6.0 13.6 %copy-start.1 = (f32[192,3072]{1,0:T(8,128)S(1)}, f32[192,3072]{1,0:T(8,128)}, u32[]{:S(2)}) copy-start(f32[192,3072]{1,0:T(8,128)} %refs_5_.3) | copy-start | bytes 7077892
  6.7 10.9 %collective-permute-start.4 = (bf16[192,3072]{1,0:T(8,128)(2,1)S(1)}, bf16[192,3072]{1,0:T(8,128)(2,1)S(1)}, u32[]{:S(2)}, u32[]{:S(2)}) collective-permute-start(bf16[192,3072]{1,0:T(8,128)(2,1)S(1)} %bitcast.17), channel_id=1, source_target_pairs={{0,8},{8,0},{16,24},{24,16},{32,40},{40,32},{48,56},{56,48},{64,72... | collective-permute-start | bytes 3538952 | tf_op jit(solution)/shard_map/ppermute | solution.py:29
  7.2 10.4 %collective-permute-start.5 = (bf16[192,3072]{1,0:T(8,128)(2,1)S(1)}, bf16[192,3072]{1,0:T(8,128)(2,1)S(1)}, u32[]{:S(2)}, u32[]{:S(2)}) collective-permute-start(bf16[192,3072]{1,0:T(8,128)(2,1)S(1)} %copy-done.2), channel_id=1, source_target_pairs={{0,8},{8,0},{16,24},{24,16},{32,40},{40,32},{48,56},{56,48},{64,72... | collective-permute-start | bytes 3538952 | tf_op jit(solution)/shard_map/ppermute | solution.py:29
  7.3 6.1 %collective-permute-start.1 = (bf16[96,1024]{1,0:T(8,128)(2,1)S(1)}, bf16[96,1024]{1,0:T(8,128)(2,1)S(1)}, u32[]{:S(2)}, u32[]{:S(2)}) collective-permute-start(bf16[96,1024]{1,0:T(8,128)(2,1)S(1)} %get-tuple-element.76), channel_id=1, source_target_pairs={{0,2},{1,3},{2,0},{3,1},{4,6},{5,7},{6,4},{7,5},{8,10},{9,11},{10,... | collective-permute-start | bytes 589832 | tf_op jit(solution)/shard_map/ppermute | solution.py:40
  8.7 7.0 %collective-permute-start.2 = (bf16[96,1024]{1,0:T(8,128)(2,1)S(1)}, bf16[96,1024]{1,0:T(8,128)(2,1)S(1)}, u32[]{:S(2)}, u32[]{:S(2)}) collective-permute-start(bf16[96,1024]{1,0:T(8,128)(2,1)S(1)} %get-tuple-element.77), channel_id=1, source_target_pairs={{0,6},{1,7},{2,4},{3,5},{4,2},{5,3},{6,0},{7,1},{8,14},{9,15},{10,... | collective-permute-start | bytes 589832 | tf_op jit(solution)/shard_map/ppermute | solution.py:40
  10.6 7.0 %collective-permute-start.3 = (bf16[96,1024]{1,0:T(8,128)(2,1)S(1)}, bf16[96,1024]{1,0:T(8,128)(2,1)S(1)}, u32[]{:S(2)}, u32[]{:S(2)}) collective-permute-start(bf16[96,1024]{1,0:T(8,128)(2,1)S(1)} %get-tuple-element.78), channel_id=1, source_target_pairs={{0,1},{1,0},{2,3},{3,2},{4,5},{5,4},{6,7},{7,6},{8,9},{9,8},{10,11... | collective-permute-start | bytes 589832 | tf_op jit(solution)/shard_map/ppermute | solution.py:40
  17.7 11.0 %collective-permute-start.9 = (f32[192,3072]{1,0:T(8,128)S(1)}, f32[192,3072]{1,0:T(8,128)S(1)}, u32[]{:S(2)}, u32[]{:S(2)}) collective-permute-start(f32[192,3072]{1,0:T(8,128)S(1)} %copy-done), channel_id=1, source_target_pairs={{0,8},{8,0},{16,24},{24,16},{32,40},{40,32},{48,56},{56,48},{64,72... | collective-permute-start | bytes 7077896 | tf_op jit(solution)/shard_map/ppermute | solution.py:29
  19.6 9.1 %collective-permute-start.10 = (f32[192,3072]{1,0:T(8,128)S(1)}, f32[192,3072]{1,0:T(8,128)S(1)}, u32[]{:S(2)}, u32[]{:S(2)}) collective-permute-start(f32[192,3072]{1,0:T(8,128)S(1)} %copy-done.1), channel_id=1, source_target_pairs={{0,8},{8,0},{16,24},{24,16},{32,40},{40,32},{48,56},{56,48},{64,72... | collective-permute-start | bytes 7077896 | tf_op jit(solution)/shard_map/ppermute | solution.py:29
  19.7 7.3 %collective-permute-start.6 = (bf16[96,1024]{1,0:T(8,128)(2,1)S(1)}, bf16[96,1024]{1,0:T(8,128)(2,1)S(1)}, u32[]{:S(2)}, u32[]{:S(2)}) collective-permute-start(bf16[96,1024]{1,0:T(8,128)(2,1)S(1)} %get-tuple-element.88.refs_0_), channel_id=1, source_target_pairs={{0,6},{1,7},{2,4},{3,5},{4,2},{5,3},{6,0},{7,1},{8,14},{9,15},{10,... | collective-permute-start | bytes 589832 | tf_op jit(solution)/shard_map/ppermute | solution.py:40
  20.5 7.3 %collective-permute-start.7 = (bf16[96,1024]{1,0:T(8,128)(2,1)S(1)}, bf16[96,1024]{1,0:T(8,128)(2,1)S(1)}, u32[]{:S(2)}, u32[]{:S(2)}) collective-permute-start(bf16[96,1024]{1,0:T(8,128)(2,1)S(1)} %get-tuple-element.89.refs_1_), channel_id=1, source_target_pairs={{0,1},{1,0},{2,3},{3,2},{4,5},{5,4},{6,7},{7,6},{8,9},{9,8},{10,11... | collective-permute-start | bytes 589832 | tf_op jit(solution)/shard_map/ppermute | solution.py:40
  23.2 5.4 %collective-permute-start.8 = (bf16[96,1024]{1,0:T(8,128)(2,1)S(1)}, bf16[96,1024]{1,0:T(8,128)(2,1)S(1)}, u32[]{:S(2)}, u32[]{:S(2)}) collective-permute-start(bf16[96,1024]{1,0:T(8,128)(2,1)S(1)} %get-tuple-element.90.refs_2_), channel_id=1, source_target_pairs={{0,2},{1,3},{2,0},{3,1},{4,6},{5,7},{6,4},{7,5},{8,10},{9,11},{10,... | collective-permute-start | bytes 589832 | tf_op jit(solution)/shard_map/ppermute | solution.py:40
  28.7 6.1 %collective-permute-start.11 = (bf16[96,1024]{1,0:T(8,128)(2,1)S(1)}, bf16[96,1024]{1,0:T(8,128)(2,1)S(1)}, u32[]{:S(2)}, u32[]{:S(2)}) collective-permute-start(bf16[96,1024]{1,0:T(8,128)(2,1)S(1)} %get-tuple-element.97.refs_0_), channel_id=1, source_target_pairs={{0,1},{1,0},{2,3},{3,2},{4,5},{5,4},{6,7},{7,6},{8,9},{9,8},{10,11... | collective-permute-start | bytes 589832 | tf_op jit(solution)/shard_map/ppermute | solution.py:40
  30.6 4.8 %collective-permute-start.12 = (bf16[96,1024]{1,0:T(8,128)(2,1)S(1)}, bf16[96,1024]{1,0:T(8,128)(2,1)S(1)}, u32[]{:S(2)}, u32[]{:S(2)}) collective-permute-start(bf16[96,1024]{1,0:T(8,128)(2,1)S(1)} %get-tuple-element.98.refs_1_), channel_id=1, source_target_pairs={{0,2},{1,3},{2,0},{3,1},{4,6},{5,7},{6,4},{7,5},{8,10},{9,11},{10,... | collective-permute-start | bytes 589832 | tf_op jit(solution)/shard_map/ppermute | solution.py:40
  30.6 6.0 %collective-permute-start.13 = (bf16[96,1024]{1,0:T(8,128)(2,1)S(1)}, bf16[96,1024]{1,0:T(8,128)(2,1)S(1)}, u32[]{:S(2)}, u32[]{:S(2)}) collective-permute-start(bf16[96,1024]{1,0:T(8,128)(2,1)S(1)} %get-tuple-element.99.refs_2_), channel_id=1, source_target_pairs={{0,6},{1,7},{2,4},{3,5},{4,2},{5,3},{6,0},{7,1},{8,14},{9,15},{10,... | collective-permute-start | bytes 589832 | tf_op jit(solution)/shard_map/ppermute | solution.py:40
  36.7 5.7 %collective-permute-start.17 = (bf16[96,1024]{1,0:T(8,128)(2,1)S(1)}, bf16[96,1024]{1,0:T(8,128)(2,1)S(1)}, u32[]{:S(2)}, u32[]{:S(2)}) collective-permute-start(bf16[96,1024]{1,0:T(8,128)(2,1)S(1)} %get-tuple-element.103.refs_0_), channel_id=1, source_target_pairs={{0,8},{8,0},{16,24},{24,16},{32,40},{40,32},{48,56},{56,48},{64,72... | collective-permute-start | bytes 589832 | tf_op jit(solution)/shard_map/ppermute | solution.py:29
  39.5 6.4 %collective-permute-start.18 = (bf16[96,1024]{1,0:T(8,128)(2,1)S(1)}, bf16[96,1024]{1,0:T(8,128)(2,1)S(1)}, u32[]{:S(2)}, u32[]{:S(2)}) collective-permute-start(bf16[96,1024]{1,0:T(8,128)(2,1)S(1)} %get-tuple-element.104.refs_1_), channel_id=1, source_target_pairs={{0,8},{8,0},{16,24},{24,16},{32,40},{40,32},{48,56},{56,48},{64,72... | collective-permute-start | bytes 589832 | tf_op jit(solution)/shard_map/ppermute | solution.py:29
  39.6 6.3 %collective-permute-start.19 = (bf16[96,1024]{1,0:T(8,128)(2,1)S(1)}, bf16[96,1024]{1,0:T(8,128)(2,1)S(1)}, u32[]{:S(2)}, u32[]{:S(2)}) collective-permute-start(bf16[96,1024]{1,0:T(8,128)(2,1)S(1)} %get-tuple-element.105.refs_2_), channel_id=1, source_target_pairs={{0,8},{8,0},{16,24},{24,16},{32,40},{40,32},{48,56},{56,48},{64,72... | collective-permute-start | bytes 589832 | tf_op jit(solution)/shard_map/ppermute | solution.py:29
  40.0 7.9 %collective-permute-start.14 = (bf16[96,1024]{1,0:T(8,128)(2,1)S(1)}, bf16[96,1024]{1,0:T(8,128)(2,1)S(1)}, u32[]{:S(2)}, u32[]{:S(2)}) collective-permute-start(bf16[96,1024]{1,0:T(8,128)(2,1)S(1)} %get-tuple-element.103.refs_0_), channel_id=1, source_target_pairs={{0,2},{1,3},{2,0},{3,1},{4,6},{5,7},{6,4},{7,5},{8,10},{9,11},{10,... | collective-permute-start | bytes 589832 | tf_op jit(solution)/shard_map/ppermute | solution.py:40
  40.6 7.4 %collective-permute-start.15 = (bf16[96,1024]{1,0:T(8,128)(2,1)S(1)}, bf16[96,1024]{1,0:T(8,128)(2,1)S(1)}, u32[]{:S(2)}, u32[]{:S(2)}) collective-permute-start(bf16[96,1024]{1,0:T(8,128)(2,1)S(1)} %get-tuple-element.104.refs_1_), channel_id=1, source_target_pairs={{0,6},{1,7},{2,4},{3,5},{4,2},{5,3},{6,0},{7,1},{8,14},{9,15},{10,... | collective-permute-start | bytes 589832 | tf_op jit(solution)/shard_map/ppermute | solution.py:40
  42.5 7.3 %collective-permute-start.16 = (bf16[96,1024]{1,0:T(8,128)(2,1)S(1)}, bf16[96,1024]{1,0:T(8,128)(2,1)S(1)}, u32[]{:S(2)}, u32[]{:S(2)}) collective-permute-start(bf16[96,1024]{1,0:T(8,128)(2,1)S(1)} %get-tuple-element.105.refs_2_), channel_id=1, source_target_pairs={{0,1},{1,0},{2,3},{3,2},{4,5},{5,4},{6,7},{7,6},{8,9},{9,8},{10,11... | collective-permute-start | bytes 589832 | tf_op jit(solution)/shard_map/ppermute | solution.py:40
  49.8 4.0 %collective-permute-start.20 = (bf16[96,1024]{1,0:T(8,128)(2,1)S(1)}, bf16[96,1024]{1,0:T(8,128)(2,1)S(1)}, u32[]{:S(2)}, u32[]{:S(2)}) collective-permute-start(bf16[96,1024]{1,0:T(8,128)(2,1)S(1)} %collective-permute-done.14.refs_0_), channel_id=1, source_target_pairs={{0,8},{8,0},{16,24},{24,16},{32,40},{40,32},{48,56},{56,48},{64,72... | collective-permute-start | bytes 589832 | tf_op jit(solution)/shard_map/ppermute | solution.py:29
  51.3 2.5 %collective-permute-start.21 = (bf16[96,1024]{1,0:T(8,128)(2,1)S(1)}, bf16[96,1024]{1,0:T(8,128)(2,1)S(1)}, u32[]{:S(2)}, u32[]{:S(2)}) collective-permute-start(bf16[96,1024]{1,0:T(8,128)(2,1)S(1)} %collective-permute-done.15.refs_1_), channel_id=1, source_target_pairs={{0,8},{8,0},{16,24},{24,16},{32,40},{40,32},{48,56},{56,48},{64,72... | collective-permute-start | bytes 589832 | tf_op jit(solution)/shard_map/ppermute | solution.py:29
  51.3 2.5 %collective-permute-start.22 = (bf16[96,1024]{1,0:T(8,128)(2,1)S(1)}, bf16[96,1024]{1,0:T(8,128)(2,1)S(1)}, u32[]{:S(2)}, u32[]{:S(2)}) collective-permute-start(bf16[96,1024]{1,0:T(8,128)(2,1)S(1)} %collective-permute-done.16.refs_2_), channel_id=1, source_target_pairs={{0,8},{8,0},{16,24},{24,16},{32,40},{40,32},{48,56},{56,48},{64,72... | collective-permute-start | bytes 589832 | tf_op jit(solution)/shard_map/ppermute | solution.py:29

commit v3 on v2

--- a/solution.py
+++ b/solution.py
@@ -14,7 +14,9 @@
 BIAS_ONE = 1.0 - 0.9**10
 BIAS_TWO = 1.0 - 0.95**10
 BLOCK = 256
-PIECES = 3
+WIDTHS = (1280, 1024, 768)
+STARTS = (0, 1280, 2304)
+PIECES = len(WIDTHS)
 LANES = 128
 OWN_STEPS = 4
 VMEM_LIMIT = 12 * 2**20
@@ -167,15 +169,15 @@
 
 def pair_kernel(clipped, residual, message, *outs):
     rows, columns = residual.shape
-    half, width = rows // 2, columns // PIECES
-    for piece in range(PIECES):
-        bit = cube_bits()[piece]
-        for out, start in ((outs[piece], 1 - bit), (outs[PIECES + piece], bit)):
+    half = rows // 2
+    bits = cube_bits()
+    for piece, (first, width) in enumerate(zip(STARTS, WIDTHS)):
+        for out, start in ((outs[piece], 1 - bits[piece]), (outs[PIECES + piece], bits[piece])):
             here = aligned(start * half, half)
             scale = message[here, columns:]
-            for block in range(piece * width // BLOCK, (piece + 1) * width // BLOCK):
+            for block in range(first // BLOCK, (first + width) // BLOCK):
                 at = slice(block * BLOCK, (block + 1) * BLOCK)
-                to = slice(block * BLOCK - piece * width, (block + 1) * BLOCK - piece * width)
+                to = slice(block * BLOCK - first, (block + 1) * BLOCK - first)
                 limit = scale[:, block : block + 1]
                 partner = jnp.clip(message[here, at] + residual[here, at], -limit, limit)
                 out[:, to] = clipped[here, at] + partner
@@ -186,7 +188,7 @@
     size = rows * columns
     outs = call(
         pair_kernel,
-        [((rows // 2, columns // PIECES), BF16)] * (2 * PIECES),
+        [((rows // 2, width), BF16) for width in WIDTHS] * 2,
         [clipped, residual, message],
         5 * size,
         size,
@@ -196,125 +198,119 @@
 
 
 def add_kernel(*refs):
-    for mine, theirs, out in zip(refs[:PIECES], refs[PIECES : 2 * PIECES], refs[2 * PIECES :]):
-        out[...] = mine[...] + theirs[...]
-
-
-def added(mine, theirs):
+    packed = refs[3 * PIECES :]
+    for piece, (first, width) in enumerate(zip(STARTS, WIDTHS)):
+        total = refs[piece][...] + refs[PIECES + piece][...]
+        refs[2 * PIECES + piece][...] = total
+        for out in packed:
+            out[:, first : first + width] = total
+
+
+def added(mine, theirs, packed=False):
     outs = [(value.shape, BF16) for value in mine]
-    return call(add_kernel, outs, [*mine, *theirs], 3 * mine[0].size, 0, "added")
-
-
-def residual_kernel(scales, residual, partner_residual, grads, out, held, read, sems):
+    if packed:
+        outs.append(((mine[0].shape[0], sum(WIDTHS)), BF16))
+    return call(add_kernel, outs, [*mine, *theirs], sum(value.size for value in mine), 0, "added")
+
+
+def residual_kernel(flip_core, scales, residual, grads, *refs):
+    out, held, read, sems = refs[-4:]
     rows, columns = residual.shape
     part = rows // OWN_STEPS
     parity = core_parity()
+    base = (1 - parity if flip_core else parity) * rows
     work = []
-    for side, source in ((0, residual), (1, partner_residual)):
-        base = (parity if side == 0 else 1 - parity) * rows
-        for step in range(OWN_STEPS):
-            here = pl.ds(step * part, part)
-            there = aligned(base + step * part, part)
-            work.append(
-                (
-                    pltpu.make_async_copy(
-                        grads.at[there], read.at[side, here], sems.at[0, side, step]
-                    ),
-                    pltpu.make_async_copy(
-                        held.at[side, here], out.at[there], sems.at[1, side, step]
-                    ),
-                    side,
-                    source,
-                    here,
-                    there,
-                )
-            )
-            work[-1][0].start()
-    for arrive, leave, side, source, here, there in work:
+    for step in range(OWN_STEPS):
+        here = pl.ds(step * part, part)
+        there = aligned(base + step * part, part)
+        arrive = pltpu.make_async_copy(grads.at[there], read.at[here], sems.at[0, step])
+        leave = pltpu.make_async_copy(held.at[here], out.at[there], sems.at[1, step])
+        work.append((arrive, leave, here, there))
+        arrive.start()
+    for arrive, leave, here, there in work:
         arrive.wait()
         scale = scales[there, :]
         for block in range(columns // BLOCK):
             at = slice(block * BLOCK, (block + 1) * BLOCK)
             limit = scale[:, block : block + 1]
-            summand = read[side, here, at].astype(F32) + source[here, at].astype(F32)
+            summand = read[here, at].astype(F32) + residual[here, at].astype(F32)
             kept = jnp.clip(summand.astype(BF16), -limit, limit)
-            held[side, here, at] = (summand - kept.astype(F32)).astype(BF16)
+            held[here, at] = (summand - kept.astype(F32)).astype(BF16)
         leave.start()
-    for arrive, leave, *_ in work:
+    for _, leave, _, _ in work:
         leave.wait()
 
 
-def new_residual(scales, residual, partner_residual, grads):
+def residual_half(flip_core, scales, residual, grads, filled):
     rows, columns = residual.shape
     size = rows * columns
     return call(
-        residual_kernel,
+        functools.partial(residual_kernel, flip_core),
         [HbmOut((grads.shape, BF16))],
-        [scales, residual, partner_residual, grads],
-        12 * size,
-        12 * size,
-        "new_residual",
+        [scales, residual, grads, *filled],
+        6 * size,
+        4 * size,
+        "residual_half",
         scratch=[
-            pltpu.VMEM((2, rows, columns), BF16),
-            pltpu.VMEM((2, rows, columns), BF16),
-            pltpu.SemaphoreType.DMA((2, 2, OWN_STEPS)),
+            pltpu.VMEM((rows, columns), BF16),
+            pltpu.VMEM((rows, columns), BF16),
+            pltpu.SemaphoreType.DMA((2, OWN_STEPS)),
         ],
-        in_hbm=1,
-    )[0]
-
-
-def adam_kernel(flip_core, flip_cube, *refs):
-    summed = refs[:PIECES]
-    weight, moment_one, moment_two = refs[PIECES : PIECES + 3]
-    outs = refs[-7:-4]
-    held, sems = refs[-4:-1], refs[-1]
-    _, half, width = held[0].shape
+        aliases={3: 0} if filled else {},
+        in_hbm=1 + len(filled),
+    )
+
+
+def adam_kernel(flip_core, flip_cube, count, *refs):
+    summed = refs[:count]
+    weight, moment_one, moment_two = refs[count : count + 3]
+    outs, held, sems = refs[-7:-4], refs[-4:-1], refs[-1]
+    half = held[0].shape[0]
     parity = core_parity()
     parity = 1 - parity if flip_core else parity
+    bits = cube_bits()
     copies = []
-    for piece in range(PIECES):
-        bit = cube_bits()[piece]
-        start = (1 - bit if flip_cube else bit) * half
+    for piece, (first, width) in enumerate(zip(STARTS, WIDTHS)):
+        start = (1 - bits[piece] if flip_cube else bits[piece]) * half
         here = aligned(start, half)
         there = aligned(parity * 2 * half + start, half)
         for block in range(width // BLOCK):
             to = slice(block * BLOCK, (block + 1) * BLOCK)
-            at = slice(piece * width + block * BLOCK, piece * width + (block + 1) * BLOCK)
-            averaged = summed[piece][:, to].astype(F32) * (1.0 / 16.0)
+            at = slice(first + block * BLOCK, first + (block + 1) * BLOCK)
+            total = summed[0][:, at] if count == 1 else summed[piece][:, to]
+            averaged = total.astype(F32) * (1.0 / 16.0)
             moment_a = BETA_ONE * moment_one[here, at] + (1.0 - BETA_ONE) * averaged
             moment_b = BETA_TWO * moment_two[here, at] + (1.0 - BETA_TWO) * averaged * averaged
             update = (LEARN_RATE / BIAS_ONE) * moment_a
             update = update / (jnp.sqrt(moment_b * (1.0 / BIAS_TWO)) + EPSILON)
-            held[0][piece, :, to] = (weight[here, at].astype(F32) - update).astype(BF16)
-            held[1][piece, :, to] = moment_a
-            held[2][piece, :, to] = moment_b
+            held[0][:, at] = (weight[here, at].astype(F32) - update).astype(BF16)
+            held[1][:, at] = moment_a
+            held[2][:, at] = moment_b
+        at = pl.ds(first, width)
         for kind in range(3):
-            copies.append(
-                pltpu.make_async_copy(
-                    held[kind].at[piece],
-                    outs[kind].at[there, pl.ds(piece * width, width)],
-                    sems.at[kind, piece],
-                )
+            copy = pltpu.make_async_copy(
+                held[kind].at[:, at], outs[kind].at[there, at], sems.at[kind, piece]
             )
-            copies[-1].start()
+            copy.start()
+            copies.append(copy)
     for copy in copies:
         copy.wait()
 
 
 def adam_quarter(flip_core, flip_cube, summed, weight, moment_one, moment_two, filled):
     rows, columns = weight.shape
-    half, width = rows // 2, columns // PIECES
+    half = rows // 2
     kinds = (BF16, F32, F32)
     size = half * columns
     given = [*summed, weight, moment_one, moment_two]
     return call(
-        functools.partial(adam_kernel, flip_core, flip_cube),
+        functools.partial(adam_kernel, flip_core, flip_cube, len(summed)),
         [HbmOut(((2 * rows, columns), kind)) for kind in kinds],
         given + list(filled),
         30 * size,
         10 * size,
         "adam_quarter",
-        scratch=[pltpu.VMEM((PIECES, half, width), kind) for kind in kinds]
+        scratch=[pltpu.VMEM((half, columns), kind) for kind in kinds]
         + [pltpu.SemaphoreType.DMA((3, PIECES))],
         aliases={len(given) + at: at for at in range(len(filled))},
         in_hbm=len(filled),
@@ -334,41 +330,43 @@
     message, scales = make_message(exponents, grads, rows)
     partner_message = core_swap(message)
     clipped, carried = clip_own(scales, grads, residual)
+    held, weight = together(carried, weight_old)
+    partner_residual, partner_weight = core_swap(held), core_swap(weight)
     sent, kept = pair_sums(clipped, carried, partner_message)
 
     def cube_step(sent, step):
         return [cube_swap(sent[piece], (piece + step) % 3) for piece in range(PIECES)]
 
-    sent, residual, weight = together(sent, residual, weight_old)
+    sent, carried = together(sent, carried)
     arrived = cube_step(sent, 0)
-    arrived, partner_residual, partner_weight = together(
-        arrived, core_swap(residual), core_swap(weight)
+    left = residual_half(False, scales, carried, grads, ())
+    arrived, left, partner_residual, partner_weight = together(
+        arrived, left, partner_residual, partner_weight
     )
     kept = added(kept, arrived)
 
     kept, one, two, partner_residual = together(kept, moment_one, moment_two, partner_residual)
     arrived = cube_step(kept, 1)
-    left = new_residual(scales, carried, partner_residual, grads)
-    arrived, partner_one, partner_two, left = together(
-        arrived, core_swap(one), core_swap(two), left
+    left = residual_half(True, scales, partner_residual, grads, left)
+    arrived, left, partner_one, partner_two = together(
+        arrived, left, core_swap(one), core_swap(two)
     )
     kept = added(kept, arrived)
 
-    arrived = cube_step(kept, 2)
-    arrived = together(*arrived)
-    kept = added(kept, arrived)
+    arrived = together(*cube_step(kept, 2))
+    *kept, packed = added(kept, arrived, packed=True)
 
     own_old = (weight_old, moment_one, moment_two)
     partner_old = (partner_weight, partner_one, partner_two)
     gathered = cube_step(kept, 0)
-    partner_kept = [core_swap(value) for value in kept]
+    partner_packed = core_swap(packed)
     filled = adam_quarter(False, False, kept, *own_old, ())
-    filled = adam_quarter(True, False, partner_kept, *partner_old, filled)
+    filled = adam_quarter(True, False, [partner_packed], *partner_old, filled)
     gathered, filled = together(gathered, filled)
     partner_gathered = [core_swap(value) for value in gathered]
     filled = adam_quarter(False, True, gathered, *own_old, filled)
     filled = adam_quarter(True, True, partner_gathered, *partner_old, filled)
-    return (filled[0][None], filled[1][None], filled[2][None], left[None, None])
+    return (filled[0][None], filled[1][None], filled[2][None], left[0][None, None])
 
 
 def solution(mesh):

time: 56 us -> 52.7 us (0.941)
  waiting for transfers between devices: 12.1 us -> 7.56 us
  Pallas kernels: 16.2 us -> 18.1 us
  starting transfers between devices: 26.7 us -> 26.1 us
    ppermute x12, waiting for transfers between devices: 11.8 us -> 7.54 us  [cube_swap(): return lax.ppermute(value, 'dp', pairs)]
    pallas_call x11 -> x12, Pallas kernels: 16.2 us -> 18.1 us  [call(): pl.pallas_call(body, in_specs=[IN_VMEM] * len(near) + [IN_HBM] * in_hbm,...]
    ppermute x11 -> x9, starting transfers between devices: 9.42 us -> 8.44 us  [core_swap(): return lax.ppermute(value, 'section', pairs)]
  transfers between devices with their start and end apart: 23 -> 21, of which waited for: 10 -> 6; matrix products, arithmetic and copies ran while one was open for 0% -> 0% of each run, Pallas kernels for 22% -> 28%
where the time goes in v3:
time: 52.7 us; the launch traced here: 52.5 us
  starting transfers between devices  26.1 us (50%)
  Pallas kernels  18.1 us (34%)
  waiting for transfers between devices  7.56 us (14%)
  between operations  0.81 us (2%)
    pallas_call x12, Pallas kernels, call(): pl.pallas_call(body, in_specs=[IN_VMEM] * len(near) + [IN_HBM] * in_hbm,...  18.1 us
    ppermute x12, starting transfers between devices, cube_swap(): return lax.ppermute(value, 'dp', pairs)  17.6 us
    ppermute x9, starting transfers between devices, core_swap(): return lax.ppermute(value, 'section', pairs)  8.44 us
    ppermute x12, waiting for transfers between devices, cube_swap(): return lax.ppermute(value, 'dp', pairs)  7.54 us
  transfers between devices with their start and end apart: 21, of which 6 were waited for; matrix products, arithmetic and copies ran while one was open for 0% of the time, Pallas kernels for 28%

profile of v3, /device:TPU:1, one launch (start us, length us, event | category | flops | bytes accessed | tf_op | source)
XLA Modules:
  0.0 52.5 jit_solution(8220045651491859539)
XLA Ops:
  0.6 1.3 %make_message.1 = (bf16[192,3200]{1,0:T(8,128)(2,1)S(1)}, bf16[384,128]{1,0:T(8,128)(2,1)S(1)}) custom-call(s32[12,1,384]{2,1,0:T(1,128)} %bitcast.18, bf16[384,3072]{1,0:T(8,128)(2,1)} %bitcast.11), custom_call_target="tpu_custom_call" | custom-call | bytes 1179648 | tf_op jit(solution)/shard_map/make_message/pallas_call | solution.py:62
  1.9 1.5 %collective-permute-start = (bf16[192,3200]{1,0:T(8,128)(2,1)S(1)}, bf16[192,3200]{1,0:T(8,128)(2,1)S(1)}, u32[]{:S(2)}, u32[]{:S(2)}) collective-permute-start(bf16[192,3200]{1,0:T(8,128)(2,1)S(1)} %get-tuple-element.72), channel_id=1, source_target_pairs={{0,8},{8,0},{16,24},{24,16},{32,40},{40,32},{48,56},{56,48},{64,72... | collective-permute-start | bytes 3686408 | tf_op jit(solution)/shard_map/ppermute | solution.py:31
  3.4 2.1 %clip_own.1 = (bf16[192,3072]{1,0:T(8,128)(2,1)S(1)}, bf16[192,3072]{1,0:T(8,128)(2,1)S(1)}) custom-call(bf16[384,128]{1,0:T(8,128)(2,1)S(1)} %get-tuple-element.69.scales, bf16[384,3072]{1,0:T(8,128)(2,1)} %bitcast.12, bf16[192,3072]{1,0:T(8,128)(2,1)} %bitcast.17), custom_call_target="tpu_custom_call" | custom-call | flops 2359296 | bytes 2359296 | tf_op jit(solution)/shard_map/clip_own/pallas_call | solution.py:62
  5.5 0.2 collective-permute-start.4
  5.7 0.4 collective-permute-start.5
  6.1 0.7 %pair_sums.1 = (bf16[96,1280]{1,0:T(8,128)(2,1)S(1)}, bf16[96,1024]{1,0:T(8,128)(2,1)S(1)}, bf16[96,768]{1,0:T(8,128)(2,1)S(1)}, bf16[96,1280]{1,0:T(8,128)(2,1)...) custom-call(bf16[192,3072]{1,0:T(8,128)(2,1)S(1)} %get-tuple-element.70.clipped, ...), custom_call_target="tpu_custom_call" | custom-call | flops 2949120 | bytes 589824 | tf_op jit(solution)/shard_map/pair_sums/pallas_call | solution.py:62
  6.9 1.5 %collective-permute-start.1 = (bf16[96,1280]{1,0:T(8,128)(2,1)S(1)}, bf16[96,1280]{1,0:T(8,128)(2,1)S(1)}, u32[]{:S(2)}, u32[]{:S(2)}) collective-permute-start(bf16[96,1280]{1,0:T(8,128)(2,1)S(1)} %get-tuple-element.79), channel_id=1, source_target_pairs={{0,2},{1,3},{2,0},{3,1},{4,6},{5,7},{6,4},{7,5},{8,10},{9,11},{10,... | collective-permute-start | bytes 737288 | tf_op jit(solution)/shard_map/ppermute | solution.py:42
  8.4 1.9 %collective-permute-start.2 = (bf16[96,1024]{1,0:T(8,128)(2,1)S(1)}, bf16[96,1024]{1,0:T(8,128)(2,1)S(1)}, u32[]{:S(2)}, u32[]{:S(2)}) collective-permute-start(bf16[96,1024]{1,0:T(8,128)(2,1)S(1)} %get-tuple-element.80), channel_id=1, source_target_pairs={{0,6},{1,7},{2,4},{3,5},{4,2},{5,3},{6,0},{7,1},{8,14},{9,15},{10,... | collective-permute-start | bytes 589832 | tf_op jit(solution)/shard_map/ppermute | solution.py:42
  10.3 2.7 %collective-permute-start.3 = (bf16[96,768]{1,0:T(8,128)(2,1)S(1)}, bf16[96,768]{1,0:T(8,128)(2,1)S(1)}, u32[]{:S(2)}, u32[]{:S(2)}) collective-permute-start(bf16[96,768]{1,0:T(8,128)(2,1)S(1)} %get-tuple-element.81), channel_id=1, source_target_pairs={{0,1},{1,0},{2,3},{3,2},{4,5},{5,4},{6,7},{7,6},{8,9},{9,8},{10,11... | collective-permute-start | bytes 442376 | tf_op jit(solution)/shard_map/ppermute | solution.py:42
  13.0 2.7 %residual_half.2.refs_0_ = bf16[384,3072]{1,0:T(8,128)(2,1)} custom-call(bf16[384,128]{1,0:T(8,128)(2,1)S(1)} %get-tuple-element.69.scales, bf16[192,3072]{1,0:T(8,128)(2,1)S(1)} %get-tuple-element.83.residual, bf16[384,3072]{1,0:T(8,128)(2,1)} %bitcast.13), custom_call_target="tpu_custom_call" | custom-call | flops 3538944 | bytes 2359296 | tf_op jit(solution)/shard_map/residual_half/pallas_call | solution.py:62
  15.8 0.6 %collective-permute-done.3.refs_5_ = bf16[96,768]{1,0:T(8,128)(2,1)S(1)} collective-permute-done((bf16[96,768]{1,0:T(8,128)(2,1)S(1)}, bf16[96,768]{1,0:T(8,128)(2,1)S(1)}, u32[]{:S(2)}, u32[]{:S(2)}) %collective-permute-start.3) | collective-permute-done | bytes 147488 | tf_op jit(solution)/shard_map/ppermute | solution.py:42
  16.4 1.7 %collective-permute-start.9 = (f32[192,3072]{1,0:T(8,128)S(1)}, f32[192,3072]{1,0:T(8,128)S(1)}, u32[]{:S(2)}, u32[]{:S(2)}) collective-permute-start(f32[192,3072]{1,0:T(8,128)S(1)} %copy-done), channel_id=1, source_target_pairs={{0,8},{8,0},{16,24},{24,16},{32,40},{40,32},{48,56},{56,48},{64,72... | collective-permute-start | bytes 7077896 | tf_op jit(solution)/shard_map/ppermute | solution.py:31
  18.3 0.8 %collective-permute-start.6 = (bf16[96,1280]{1,0:T(8,128)(2,1)S(1)}, bf16[96,1280]{1,0:T(8,128)(2,1)S(1)}, u32[]{:S(2)}, u32[]{:S(2)}) collective-permute-start(bf16[96,1280]{1,0:T(8,128)(2,1)S(1)} %get-tuple-element.92.refs_0_), channel_id=1, source_target_pairs={{0,6},{1,7},{2,4},{3,5},{4,2},{5,3},{6,0},{7,1},{8,14},{9,15},{10,... | collective-permute-start | bytes 737288 | tf_op jit(solution)/shard_map/ppermute | solution.py:42
  19.1 2.7 %collective-permute-start.7 = (bf16[96,1024]{1,0:T(8,128)(2,1)S(1)}, bf16[96,1024]{1,0:T(8,128)(2,1)S(1)}, u32[]{:S(2)}, u32[]{:S(2)}) collective-permute-start(bf16[96,1024]{1,0:T(8,128)(2,1)S(1)} %get-tuple-element.93.refs_1_), channel_id=1, source_target_pairs={{0,1},{1,0},{2,3},{3,2},{4,5},{5,4},{6,7},{7,6},{8,9},{9,8},{10,11... | collective-permute-start | bytes 589832 | tf_op jit(solution)/shard_map/ppermute | solution.py:42
  21.8 2.7 %residual_half.3 = bf16[384,3072]{1,0:T(8,128)(2,1)} custom-call(bf16[384,128]{1,0:T(8,128)(2,1)S(1)} %get-tuple-element.69.scales, bf16[192,3072]{1,0:T(8,128)(2,1)S(1)} %collective-permute-done.4.residual, bf16[384,3072]{1,0:T(8,128)(2,1)} %bitcast.14, bf16[384,3072]{1,0:T(8,128)(2,1)} %residual_half.2.refs_0_), custom_call_target="tpu_custom_call", output_to_operand_aliasing={{}: (3, {})} | custom-call | flops 3538944 | bytes 2359296 | tf_op jit(solution)/shard_map/residual_half/pallas_call | solution.py:62
  24.6 1.6 %collective-permute-done.8.refs_5_ = bf16[96,768]{1,0:T(8,128)(2,1)S(1)} collective-permute-done((bf16[96,768]{1,0:T(8,128)(2,1)S(1)}, bf16[96,768]{1,0:T(8,128)(2,1)S(1)}, u32[]{:S(2)}, u32[]{:S(2)}) %collective-permute-start.8) | collective-permute-done | bytes 147488 | tf_op jit(solution)/shard_map/ppermute | solution.py:42
  26.2 0.1 collective-permute-done.7.refs_4_
  26.3 0.3 collective-permute-done.6.refs_3_
  26.7 2.8 %collective-permute-start.11 = (bf16[96,1280]{1,0:T(8,128)(2,1)S(1)}, bf16[96,1280]{1,0:T(8,128)(2,1)S(1)}, u32[]{:S(2)}, u32[]{:S(2)}) collective-permute-start(bf16[96,1280]{1,0:T(8,128)(2,1)S(1)} %get-tuple-element.102.refs_0_), channel_id=1, source_target_pairs={{0,1},{1,0},{2,3},{3,2},{4,5},{5,4},{6,7},{7,6},{8,9},{9,8},{10,11... | collective-permute-start | bytes 737288 | tf_op jit(solution)/shard_map/ppermute | solution.py:42
  29.5 1.6 %collective-permute-start.13 = (bf16[96,768]{1,0:T(8,128)(2,1)S(1)}, bf16[96,768]{1,0:T(8,128)(2,1)S(1)}, u32[]{:S(2)}, u32[]{:S(2)}) collective-permute-start(bf16[96,768]{1,0:T(8,128)(2,1)S(1)} %get-tuple-element.104.refs_2_), channel_id=1, source_target_pairs={{0,6},{1,7},{2,4},{3,5},{4,2},{5,3},{6,0},{7,1},{8,14},{9,15},{10,... | collective-permute-start | bytes 442376 | tf_op jit(solution)/shard_map/ppermute | solution.py:42
  31.1 3.9 %collective-permute-done.13.refs_5_ = bf16[96,768]{1,0:T(8,128)(2,1)S(1)} collective-permute-done((bf16[96,768]{1,0:T(8,128)(2,1)S(1)}, bf16[96,768]{1,0:T(8,128)(2,1)S(1)}, u32[]{:S(2)}, u32[]{:S(2)}) %collective-permute-start.13) | collective-permute-done | bytes 147488 | tf_op jit(solution)/shard_map/ppermute | solution.py:42
  35.1 2.5 %collective-permute-start.17 = (bf16[96,3072]{1,0:T(8,128)(2,1)S(1)}, bf16[96,3072]{1,0:T(8,128)(2,1)S(1)}, u32[]{:S(2)}, u32[]{:S(2)}) collective-permute-start(bf16[96,3072]{1,0:T(8,128)(2,1)S(1)} %get-tuple-element.111), channel_id=1, source_target_pairs={{0,8},{8,0},{16,24},{24,16},{32,40},{40,32},{48,56},{56,48},{64,72... | collective-permute-start | bytes 1769480 | tf_op jit(solution)/shard_map/ppermute | solution.py:31
  37.6 0.5 %collective-permute-start.14 = (bf16[96,1280]{1,0:T(8,128)(2,1)S(1)}, bf16[96,1280]{1,0:T(8,128)(2,1)S(1)}, u32[]{:S(2)}, u32[]{:S(2)}) collective-permute-start(bf16[96,1280]{1,0:T(8,128)(2,1)S(1)} %get-tuple-element.108.refs_0_), channel_id=1, source_target_pairs={{0,2},{1,3},{2,0},{3,1},{4,6},{5,7},{6,4},{7,5},{8,10},{9,11},{10,... | collective-permute-start | bytes 737288 | tf_op jit(solution)/shard_map/ppermute | solution.py:42
  38.2 1.9 %collective-permute-start.15 = (bf16[96,1024]{1,0:T(8,128)(2,1)S(1)}, bf16[96,1024]{1,0:T(8,128)(2,1)S(1)}, u32[]{:S(2)}, u32[]{:S(2)}) collective-permute-start(bf16[96,1024]{1,0:T(8,128)(2,1)S(1)} %get-tuple-element.109.refs_1_), channel_id=1, source_target_pairs={{0,6},{1,7},{2,4},{3,5},{4,2},{5,3},{6,0},{7,1},{8,14},{9,15},{10,... | collective-permute-start | bytes 589832 | tf_op jit(solution)/shard_map/ppermute | solution.py:42
  40.1 1.1 %collective-permute-start.16 = (bf16[96,768]{1,0:T(8,128)(2,1)S(1)}, bf16[96,768]{1,0:T(8,128)(2,1)S(1)}, u32[]{:S(2)}, u32[]{:S(2)}) collective-permute-start(bf16[96,768]{1,0:T(8,128)(2,1)S(1)} %get-tuple-element.110.refs_2_), channel_id=1, source_target_pairs={{0,1},{1,0},{2,3},{3,2},{4,5},{5,4},{6,7},{7,6},{8,9},{9,8},{10,11... | collective-permute-start | bytes 442376 | tf_op jit(solution)/shard_map/ppermute | solution.py:42
  41.2 2.1 %adam_quarter.4 = (bf16[384,3072]{1,0:T(8,128)(2,1)}, f32[384,3072]{1,0:T(8,128)}, f32[384,3072]{1,0:T(8,128)}) custom-call(bf16[96,1280]{1,0:T(8,128)(2,1)S(1)} %get-tuple-element.108.refs_0_, bf16[96,1024]{1,0:T(8,128)(2,1)S(1)} %get-tuple-element.109.refs_1_, bf16[96,768]{1,0:T(8,128)(2,1)S(1)} %get-tuple-element.110.refs_2_, ...), custom_call_target="tpu_custom_call" | custom-call | flops 8847360 | bytes 2949120 | tf_op jit(solution)/shard_map/adam_quarter/pallas_call | solution.py:62
  43.3 2.1 %adam_quarter.5 = (bf16[384,3072]{1,0:T(8,128)(2,1)}, f32[384,3072]{1,0:T(8,128)}, f32[384,3072]{1,0:T(8,128)}) custom-call(bf16[96,3072]{1,0:T(8,128)(2,1)S(1)} %collective-permute-done.17.refs_0_, bf16[192,3072]{1,0:T(8,128)(2,1)S(1)} %collective-permute-done.5.refs_1_.refs_3_, ...), custom_call_target="tpu_custom_call", output_to_operand_aliasing={{0}: (4, {}), {1}: (5, {}), {2}: (6, {})} | custom-call | flops 8847360 | bytes 2949120 | tf_op jit(solution)/shard_map/adam_quarter/pallas_call | solution.py:62
  45.4 1.0 %collective-permute-done.16.refs_2_ = bf16[96,768]{1,0:T(8,128)(2,1)S(1)} collective-permute-done((bf16[96,768]{1,0:T(8,128)(2,1)S(1)}, bf16[96,768]{1,0:T(8,128)(2,1)S(1)}, u32[]{:S(2)}, u32[]{:S(2)}) %collective-permute-start.16) | collective-permute-done | bytes 147488 | tf_op jit(solution)/shard_map/ppermute | solution.py:42
  46.3 1.5 %collective-permute-start.18 = (bf16[96,1280]{1,0:T(8,128)(2,1)S(1)}, bf16[96,1280]{1,0:T(8,128)(2,1)S(1)}, u32[]{:S(2)}, u32[]{:S(2)}) collective-permute-start(bf16[96,1280]{1,0:T(8,128)(2,1)S(1)} %collective-permute-done.14.refs_0_), channel_id=1, source_target_pairs={{0,8},{8,0},{16,24},{24,16},{32,40},{40,32},{48,56},{56,48},{64,72... | collective-permute-start | bytes 737288 | tf_op jit(solution)/shard_map/ppermute | solution.py:31
  47.9 0.4 collective-permute-start.20
  48.4 2.1 %adam_quarter.6 = (bf16[384,3072]{1,0:T(8,128)(2,1)}, f32[384,3072]{1,0:T(8,128)}, f32[384,3072]{1,0:T(8,128)}) custom-call(bf16[96,1280]{1,0:T(8,128)(2,1)S(1)} %collective-permute-done.14.refs_0_, bf16[96,1024]{1,0:T(8,128)(2,1)S(1)} %collective-permute-done.15.refs_1_, ...), custom_call_target="tpu_custom_call", output_to_operand_aliasing={{0}: (6, {}), {1}: (7, {}), {2}: (8, {})} | custom-call | flops 8847360 | bytes 2949120 | tf_op jit(solution)/shard_map/adam_quarter/pallas_call | solution.py:62
  50.5 2.1 %adam_quarter.7 = (bf16[384,3072]{1,0:T(8,128)(2,1)}, f32[384,3072]{1,0:T(8,128)}, f32[384,3072]{1,0:T(8,128)}) custom-call(bf16[96,1280]{1,0:T(8,128)(2,1)S(1)} %collective-permute-done.18.refs_0_, bf16[96,1024]{1,0:T(8,128)(2,1)S(1)} %collective-permute-done.19.refs_1_, ...), custom_call_target="tpu_custom_call", output_to_operand_aliasing={{0}: (6, {}), {1}: (7, {}), {2}: (8, {})} | custom-call | flops 8847360 | bytes 2949120 | tf_op jit(solution)/shard_map/adam_quarter/pallas_call | solution.py:62
  (28 shorter events, 0.5 us)
Async XLA Ops:
  1.9 3.8 %copy-start.2 = (bf16[192,3072]{1,0:T(8,128)(2,1)S(1)}, bf16[192,3072]{1,0:T(8,128)(2,1)}, u32[]{:S(2)}) copy-start(bf16[192,3072]{1,0:T(8,128)(2,1)} %refs_3_.3) | copy-start | bytes 3538948
  1.9 4.2 %collective-permute-start = (bf16[192,3200]{1,0:T(8,128)(2,1)S(1)}, bf16[192,3200]{1,0:T(8,128)(2,1)S(1)}, u32[]{:S(2)}, u32[]{:S(2)}) collective-permute-start(bf16[192,3200]{1,0:T(8,128)(2,1)S(1)} %get-tuple-element.72), channel_id=1, source_target_pairs={{0,8},{8,0},{16,24},{24,16},{32,40},{40,32},{48,56},{56,48},{64,72... | collective-permute-start | bytes 3686408 | tf_op jit(solution)/shard_map/ppermute | solution.py:31
  5.5 10.2 %collective-permute-start.4 = (bf16[192,3072]{1,0:T(8,128)(2,1)S(1)}, bf16[192,3072]{1,0:T(8,128)(2,1)S(1)}, u32[]{:S(2)}, u32[]{:S(2)}) collective-permute-start(bf16[192,3072]{1,0:T(8,128)(2,1)S(1)} %get-tuple-element.83.residual), channel_id=1, source_target_pairs={{0,8},{8,0},{16,24},{24,16},{32,40},{40,32},{48,56},{56,48},{64,72... | collective-permute-start | bytes 3538952 | tf_op jit(solution)/shard_map/ppermute | solution.py:31
  5.7 10.0 %collective-permute-start.5 = (bf16[192,3072]{1,0:T(8,128)(2,1)S(1)}, bf16[192,3072]{1,0:T(8,128)(2,1)S(1)}, u32[]{:S(2)}, u32[]{:S(2)}) collective-permute-start(bf16[192,3072]{1,0:T(8,128)(2,1)S(1)} %copy-done.2), channel_id=1, source_target_pairs={{0,8},{8,0},{16,24},{24,16},{32,40},{40,32},{48,56},{56,48},{64,72... | collective-permute-start | bytes 3538952 | tf_op jit(solution)/shard_map/ppermute | solution.py:31
  6.9 9.6 %copy-start = (f32[192,3072]{1,0:T(8,128)S(1)}, f32[192,3072]{1,0:T(8,128)}, u32[]{:S(2)}) copy-start(f32[192,3072]{1,0:T(8,128)} %refs_4_.3) | copy-start | bytes 7077892
  6.9 11.3 %copy-start.1 = (f32[192,3072]{1,0:T(8,128)S(1)}, f32[192,3072]{1,0:T(8,128)}, u32[]{:S(2)}) copy-start(f32[192,3072]{1,0:T(8,128)} %refs_5_.3) | copy-start | bytes 7077892
  6.9 9.5 %collective-permute-start.1 = (bf16[96,1280]{1,0:T(8,128)(2,1)S(1)}, bf16[96,1280]{1,0:T(8,128)(2,1)S(1)}, u32[]{:S(2)}, u32[]{:S(2)}) collective-permute-start(bf16[96,1280]{1,0:T(8,128)(2,1)S(1)} %get-tuple-element.79), channel_id=1, source_target_pairs={{0,2},{1,3},{2,0},{3,1},{4,6},{5,7},{6,4},{7,5},{8,10},{9,11},{10,... | collective-permute-start | bytes 737288 | tf_op jit(solution)/shard_map/ppermute | solution.py:42
  8.4 8.0 %collective-permute-start.2 = (bf16[96,1024]{1,0:T(8,128)(2,1)S(1)}, bf16[96,1024]{1,0:T(8,128)(2,1)S(1)}, u32[]{:S(2)}, u32[]{:S(2)}) collective-permute-start(bf16[96,1024]{1,0:T(8,128)(2,1)S(1)} %get-tuple-element.80), channel_id=1, source_target_pairs={{0,6},{1,7},{2,4},{3,5},{4,2},{5,3},{6,0},{7,1},{8,14},{9,15},{10,... | collective-permute-start | bytes 589832 | tf_op jit(solution)/shard_map/ppermute | solution.py:42
  10.3 6.1 %collective-permute-start.3 = (bf16[96,768]{1,0:T(8,128)(2,1)S(1)}, bf16[96,768]{1,0:T(8,128)(2,1)S(1)}, u32[]{:S(2)}, u32[]{:S(2)}) collective-permute-start(bf16[96,768]{1,0:T(8,128)(2,1)S(1)} %get-tuple-element.81), channel_id=1, source_target_pairs={{0,1},{1,0},{2,3},{3,2},{4,5},{5,4},{6,7},{7,6},{8,9},{9,8},{10,11... | collective-permute-start | bytes 442376 | tf_op jit(solution)/shard_map/ppermute | solution.py:42
  16.4 10.2 %collective-permute-start.9 = (f32[192,3072]{1,0:T(8,128)S(1)}, f32[192,3072]{1,0:T(8,128)S(1)}, u32[]{:S(2)}, u32[]{:S(2)}) collective-permute-start(f32[192,3072]{1,0:T(8,128)S(1)} %copy-done), channel_id=1, source_target_pairs={{0,8},{8,0},{16,24},{24,16},{32,40},{40,32},{48,56},{56,48},{64,72... | collective-permute-start | bytes 7077896 | tf_op jit(solution)/shard_map/ppermute | solution.py:31
  18.2 8.4 %collective-permute-start.10 = (f32[192,3072]{1,0:T(8,128)S(1)}, f32[192,3072]{1,0:T(8,128)S(1)}, u32[]{:S(2)}, u32[]{:S(2)}) collective-permute-start(f32[192,3072]{1,0:T(8,128)S(1)} %copy-done.1), channel_id=1, source_target_pairs={{0,8},{8,0},{16,24},{24,16},{32,40},{40,32},{48,56},{56,48},{64,72... | collective-permute-start | bytes 7077896 | tf_op jit(solution)/shard_map/ppermute | solution.py:31
  18.3 8.3 %collective-permute-start.6 = (bf16[96,1280]{1,0:T(8,128)(2,1)S(1)}, bf16[96,1280]{1,0:T(8,128)(2,1)S(1)}, u32[]{:S(2)}, u32[]{:S(2)}) collective-permute-start(bf16[96,1280]{1,0:T(8,128)(2,1)S(1)} %get-tuple-element.92.refs_0_), channel_id=1, source_target_pairs={{0,6},{1,7},{2,4},{3,5},{4,2},{5,3},{6,0},{7,1},{8,14},{9,15},{10,... | collective-permute-start | bytes 737288 | tf_op jit(solution)/shard_map/ppermute | solution.py:42
  19.1 7.3 %collective-permute-start.7 = (bf16[96,1024]{1,0:T(8,128)(2,1)S(1)}, bf16[96,1024]{1,0:T(8,128)(2,1)S(1)}, u32[]{:S(2)}, u32[]{:S(2)}) collective-permute-start(bf16[96,1024]{1,0:T(8,128)(2,1)S(1)} %get-tuple-element.93.refs_1_), channel_id=1, source_target_pairs={{0,1},{1,0},{2,3},{3,2},{4,5},{5,4},{6,7},{7,6},{8,9},{9,8},{10,11... | collective-permute-start | bytes 589832 | tf_op jit(solution)/shard_map/ppermute | solution.py:42
  21.8 4.4 %collective-permute-start.8 = (bf16[96,768]{1,0:T(8,128)(2,1)S(1)}, bf16[96,768]{1,0:T(8,128)(2,1)S(1)}, u32[]{:S(2)}, u32[]{:S(2)}) collective-permute-start(bf16[96,768]{1,0:T(8,128)(2,1)S(1)} %get-tuple-element.94.refs_2_), channel_id=1, source_target_pairs={{0,2},{1,3},{2,0},{3,1},{4,6},{5,7},{6,4},{7,5},{8,10},{9,11},{10,... | collective-permute-start | bytes 442376 | tf_op jit(solution)/shard_map/ppermute | solution.py:42
  26.7 8.3 %collective-permute-start.11 = (bf16[96,1280]{1,0:T(8,128)(2,1)S(1)}, bf16[96,1280]{1,0:T(8,128)(2,1)S(1)}, u32[]{:S(2)}, u32[]{:S(2)}) collective-permute-start(bf16[96,1280]{1,0:T(8,128)(2,1)S(1)} %get-tuple-element.102.refs_0_), channel_id=1, source_target_pairs={{0,1},{1,0},{2,3},{3,2},{4,5},{5,4},{6,7},{7,6},{8,9},{9,8},{10,11... | collective-permute-start | bytes 737288 | tf_op jit(solution)/shard_map/ppermute | solution.py:42
  29.5 5.5 %collective-permute-start.12 = (bf16[96,1024]{1,0:T(8,128)(2,1)S(1)}, bf16[96,1024]{1,0:T(8,128)(2,1)S(1)}, u32[]{:S(2)}, u32[]{:S(2)}) collective-permute-start(bf16[96,1024]{1,0:T(8,128)(2,1)S(1)} %get-tuple-element.103.refs_1_), channel_id=1, source_target_pairs={{0,2},{1,3},{2,0},{3,1},{4,6},{5,7},{6,4},{7,5},{8,10},{9,11},{10,... | collective-permute-start | bytes 589832 | tf_op jit(solution)/shard_map/ppermute | solution.py:42
  29.5 5.5 %collective-permute-start.13 = (bf16[96,768]{1,0:T(8,128)(2,1)S(1)}, bf16[96,768]{1,0:T(8,128)(2,1)S(1)}, u32[]{:S(2)}, u32[]{:S(2)}) collective-permute-start(bf16[96,768]{1,0:T(8,128)(2,1)S(1)} %get-tuple-element.104.refs_2_), channel_id=1, source_target_pairs={{0,6},{1,7},{2,4},{3,5},{4,2},{5,3},{6,0},{7,1},{8,14},{9,15},{10,... | collective-permute-start | bytes 442376 | tf_op jit(solution)/shard_map/ppermute | solution.py:42
  35.1 8.1 %collective-permute-start.17 = (bf16[96,3072]{1,0:T(8,128)(2,1)S(1)}, bf16[96,3072]{1,0:T(8,128)(2,1)S(1)}, u32[]{:S(2)}, u32[]{:S(2)}) collective-permute-start(bf16[96,3072]{1,0:T(8,128)(2,1)S(1)} %get-tuple-element.111), channel_id=1, source_target_pairs={{0,8},{8,0},{16,24},{24,16},{32,40},{40,32},{48,56},{56,48},{64,72... | collective-permute-start | bytes 1769480 | tf_op jit(solution)/shard_map/ppermute | solution.py:31
  37.6 8.7 %collective-permute-start.14 = (bf16[96,1280]{1,0:T(8,128)(2,1)S(1)}, bf16[96,1280]{1,0:T(8,128)(2,1)S(1)}, u32[]{:S(2)}, u32[]{:S(2)}) collective-permute-start(bf16[96,1280]{1,0:T(8,128)(2,1)S(1)} %get-tuple-element.108.refs_0_), channel_id=1, source_target_pairs={{0,2},{1,3},{2,0},{3,1},{4,6},{5,7},{6,4},{7,5},{8,10},{9,11},{10,... | collective-permute-start | bytes 737288 | tf_op jit(solution)/shard_map/ppermute | solution.py:42
  38.2 8.2 %collective-permute-start.15 = (bf16[96,1024]{1,0:T(8,128)(2,1)S(1)}, bf16[96,1024]{1,0:T(8,128)(2,1)S(1)}, u32[]{:S(2)}, u32[]{:S(2)}) collective-permute-start(bf16[96,1024]{1,0:T(8,128)(2,1)S(1)} %get-tuple-element.109.refs_1_), channel_id=1, source_target_pairs={{0,6},{1,7},{2,4},{3,5},{4,2},{5,3},{6,0},{7,1},{8,14},{9,15},{10,... | collective-permute-start | bytes 589832 | tf_op jit(solution)/shard_map/ppermute | solution.py:42
  40.1 6.3 %collective-permute-start.16 = (bf16[96,768]{1,0:T(8,128)(2,1)S(1)}, bf16[96,768]{1,0:T(8,128)(2,1)S(1)}, u32[]{:S(2)}, u32[]{:S(2)}) collective-permute-start(bf16[96,768]{1,0:T(8,128)(2,1)S(1)} %get-tuple-element.110.refs_2_), channel_id=1, source_target_pairs={{0,1},{1,0},{2,3},{3,2},{4,5},{5,4},{6,7},{7,6},{8,9},{9,8},{10,11... | collective-permute-start | bytes 442376 | tf_op jit(solution)/shard_map/ppermute | solution.py:42
  46.3 4.1 %collective-permute-start.18 = (bf16[96,1280]{1,0:T(8,128)(2,1)S(1)}, bf16[96,1280]{1,0:T(8,128)(2,1)S(1)}, u32[]{:S(2)}, u32[]{:S(2)}) collective-permute-start(bf16[96,1280]{1,0:T(8,128)(2,1)S(1)} %collective-permute-done.14.refs_0_), channel_id=1, source_target_pairs={{0,8},{8,0},{16,24},{24,16},{32,40},{40,32},{48,56},{56,48},{64,72... | collective-permute-start | bytes 737288 | tf_op jit(solution)/shard_map/ppermute | solution.py:31
  47.8 2.6 %collective-permute-start.19 = (bf16[96,1024]{1,0:T(8,128)(2,1)S(1)}, bf16[96,1024]{1,0:T(8,128)(2,1)S(1)}, u32[]{:S(2)}, u32[]{:S(2)}) collective-permute-start(bf16[96,1024]{1,0:T(8,128)(2,1)S(1)} %collective-permute-done.15.refs_1_), channel_id=1, source_target_pairs={{0,8},{8,0},{16,24},{24,16},{32,40},{40,32},{48,56},{56,48},{64,72... | collective-permute-start | bytes 589832 | tf_op jit(solution)/shard_map/ppermute | solution.py:31
  47.9 2.5 %collective-permute-start.20 = (bf16[96,768]{1,0:T(8,128)(2,1)S(1)}, bf16[96,768]{1,0:T(8,128)(2,1)S(1)}, u32[]{:S(2)}, u32[]{:S(2)}) collective-permute-start(bf16[96,768]{1,0:T(8,128)(2,1)S(1)} %collective-permute-done.16.refs_2_), channel_id=1, source_target_pairs={{0,8},{8,0},{16,24},{24,16},{32,40},{40,32},{48,56},{56,48},{64,72... | collective-permute-start | bytes 442376 | tf_op jit(solution)/shard_map/ppermute | solution.py:31

commit v4 on v3

--- a/solution.py
+++ b/solution.py
@@ -14,8 +14,8 @@
 BIAS_ONE = 1.0 - 0.9**10
 BIAS_TWO = 1.0 - 0.95**10
 BLOCK = 256
-WIDTHS = (1280, 1024, 768)
-STARTS = (0, 1280, 2304)
+WIDTHS = (1024, 1024, 1024)
+STARTS = (0, 1024, 2048)
 PIECES = len(WIDTHS)
 LANES = 128
 OWN_STEPS = 4
@@ -31,25 +31,40 @@
     return lax.ppermute(value, "section", pairs)
 
 
+def cube_partner(replica, dim):
+    if dim == 0:
+        return replica ^ 2
+    if dim == 1:
+        return (3 - replica // 2) * 2 + replica % 2
+    return replica ^ 1
+
+
+def core_dim(dim, parity):
+    return (dim + 2 * parity) % 3
+
+
 def cube_swap(value, dim):
-    count = lax.axis_size("dp")
-    if dim == 0:
-        pairs = [(source, source ^ 2) for source in range(count)]
-    elif dim == 1:
-        pairs = [(source, (3 - source // 2) * 2 + source % 2) for source in range(count)]
-    else:
-        pairs = [(source, source ^ 1) for source in range(count)]
-    return lax.ppermute(value, "dp", pairs)
+    replicas = lax.axis_size("dp")
+    pairs = []
+    for section in range(lax.axis_size("section")):
+        for replica in range(replicas):
+            to = cube_partner(replica, core_dim(dim, section % 2))
+            pairs.append((section * replicas + replica, section * replicas + to))
+    return lax.ppermute(value, ("section", "dp"), pairs)
 
 
 def core_parity():
     return lax.axis_index("section").astype(jnp.int32) % 2
 
 
-def cube_bits():
+def cube_bits(parity):
     replica = lax.axis_index("dp").astype(jnp.int32)
     y = replica // 2
-    return [((y + 1) // 2) % 2, y // 2, replica % 2]
+    bits = [((y + 1) // 2) % 2, y // 2, replica % 2]
+    return [
+        jnp.where(parity == 0, bits[core_dim(piece, 0)], bits[core_dim(piece, 1)])
+        for piece in range(PIECES)
+    ]
 
 
 class HbmOut(tuple):
@@ -167,50 +182,50 @@
     )
 
 
-def pair_kernel(clipped, residual, message, *outs):
+def pair_kernel(flip_cube, clipped, residual, message, *outs):
     rows, columns = residual.shape
     half = rows // 2
-    bits = cube_bits()
-    for piece, (first, width) in enumerate(zip(STARTS, WIDTHS)):
-        for out, start in ((outs[piece], 1 - bits[piece]), (outs[PIECES + piece], bits[piece])):
-            here = aligned(start * half, half)
-            scale = message[here, columns:]
-            for block in range(first // BLOCK, (first + width) // BLOCK):
-                at = slice(block * BLOCK, (block + 1) * BLOCK)
-                to = slice(block * BLOCK - first, (block + 1) * BLOCK - first)
-                limit = scale[:, block : block + 1]
-                partner = jnp.clip(message[here, at] + residual[here, at], -limit, limit)
-                out[:, to] = clipped[here, at] + partner
-
-
-def pair_sums(clipped, residual, message):
-    rows, columns = residual.shape
-    size = rows * columns
-    outs = call(
-        pair_kernel,
-        [((rows // 2, width), BF16) for width in WIDTHS] * 2,
+    bits = cube_bits(core_parity())
+    for out, bit, first, width in zip(outs, bits, STARTS, WIDTHS):
+        here = aligned((1 - bit if flip_cube else bit) * half, half)
+        scale = message[here, columns:]
+        for block in range(first // BLOCK, (first + width) // BLOCK):
+            at = slice(block * BLOCK, (block + 1) * BLOCK)
+            to = slice(block * BLOCK - first, (block + 1) * BLOCK - first)
+            limit = scale[:, block : block + 1]
+            partner = jnp.clip(message[here, at] + residual[here, at], -limit, limit)
+            out[:, to] = clipped[here, at] + partner
+
+
+def pair_sums(flip_cube, clipped, residual, message):
+    rows, columns = residual.shape
+    size = rows * columns // 2
+    return call(
+        functools.partial(pair_kernel, flip_cube),
+        [((rows // 2, width), BF16) for width in WIDTHS],
         [clipped, residual, message],
         5 * size,
         size,
         "pair_sums",
     )
-    return outs[:PIECES], outs[PIECES:]
-
-
-def add_kernel(*refs):
-    packed = refs[3 * PIECES :]
-    for piece, (first, width) in enumerate(zip(STARTS, WIDTHS)):
-        total = refs[piece][...] + refs[PIECES + piece][...]
-        refs[2 * PIECES + piece][...] = total
-        for out in packed:
-            out[:, first : first + width] = total
-
-
-def added(mine, theirs, packed=False):
-    outs = [(value.shape, BF16) for value in mine]
-    if packed:
-        outs.append(((mine[0].shape[0], sum(WIDTHS)), BF16))
-    return call(add_kernel, outs, [*mine, *theirs], sum(value.size for value in mine), 0, "added")
+
+
+def pack_kernel(*refs):
+    for part, first, width in zip(refs, STARTS, WIDTHS):
+        refs[-1][:, first : first + width] = part[...]
+
+
+def packed_pieces(parts):
+    shape = (parts[0].shape[0], sum(WIDTHS))
+    return call(pack_kernel, [(shape, BF16)], parts, 0, 0, "pack")[0]
+
+
+def add_kernel(mine, theirs, out):
+    out[...] = mine[...] + theirs[...]
+
+
+def added(mine, theirs):
+    return call(add_kernel, [(mine.shape, BF16)], [mine, theirs], mine.size, 0, "added")[0]
 
 
 def residual_kernel(flip_core, scales, residual, grads, *refs):
@@ -261,57 +276,61 @@
     )
 
 
-def adam_kernel(flip_core, flip_cube, count, *refs):
-    summed = refs[:count]
-    weight, moment_one, moment_two = refs[count : count + 3]
+def adam_kernel(jobs, *refs):
     outs, held, sems = refs[-7:-4], refs[-4:-1], refs[-1]
-    half = held[0].shape[0]
-    parity = core_parity()
-    parity = 1 - parity if flip_core else parity
-    bits = cube_bits()
+    half = held[0].shape[1]
     copies = []
-    for piece, (first, width) in enumerate(zip(STARTS, WIDTHS)):
-        start = (1 - bits[piece] if flip_cube else bits[piece]) * half
-        here = aligned(start, half)
-        there = aligned(parity * 2 * half + start, half)
-        for block in range(width // BLOCK):
-            to = slice(block * BLOCK, (block + 1) * BLOCK)
-            at = slice(first + block * BLOCK, first + (block + 1) * BLOCK)
-            total = summed[0][:, at] if count == 1 else summed[piece][:, to]
-            averaged = total.astype(F32) * (1.0 / 16.0)
-            moment_a = BETA_ONE * moment_one[here, at] + (1.0 - BETA_ONE) * averaged
-            moment_b = BETA_TWO * moment_two[here, at] + (1.0 - BETA_TWO) * averaged * averaged
-            update = (LEARN_RATE / BIAS_ONE) * moment_a
-            update = update / (jnp.sqrt(moment_b * (1.0 / BIAS_TWO)) + EPSILON)
-            held[0][:, at] = (weight[here, at].astype(F32) - update).astype(BF16)
-            held[1][:, at] = moment_a
-            held[2][:, at] = moment_b
-        at = pl.ds(first, width)
-        for kind in range(3):
-            copy = pltpu.make_async_copy(
-                held[kind].at[:, at], outs[kind].at[there, at], sems.at[kind, piece]
-            )
-            copy.start()
-            copies.append(copy)
+    used = 0
+    for job, (flip_core, flip_cube, count) in enumerate(jobs):
+        summed = refs[used : used + count]
+        weight, moment_one, moment_two = refs[used + count : used + count + 3]
+        used += count + 3
+        parity = core_parity()
+        parity = 1 - parity if flip_core else parity
+        bits = cube_bits(parity)
+        for piece, (first, width) in enumerate(zip(STARTS, WIDTHS)):
+            start = (1 - bits[piece] if flip_cube else bits[piece]) * half
+            here = aligned(start, half)
+            there = aligned(parity * 2 * half + start, half)
+            for block in range(width // BLOCK):
+                to = slice(block * BLOCK, (block + 1) * BLOCK)
+                at = slice(first + block * BLOCK, first + (block + 1) * BLOCK)
+                total = summed[0][:, at] if count == 1 else summed[piece][:, to]
+                averaged = total.astype(F32) * (1.0 / 16.0)
+                moment_a = BETA_ONE * moment_one[here, at] + (1.0 - BETA_ONE) * averaged
+                moment_b = BETA_TWO * moment_two[here, at]
+                moment_b = moment_b + (1.0 - BETA_TWO) * averaged * averaged
+                update = (LEARN_RATE / BIAS_ONE) * moment_a
+                update = update / (jnp.sqrt(moment_b * (1.0 / BIAS_TWO)) + EPSILON)
+                held[0][job, :, at] = (weight[here, at].astype(F32) - update).astype(BF16)
+                held[1][job, :, at] = moment_a
+                held[2][job, :, at] = moment_b
+            at = pl.ds(first, width)
+            for kind in range(3):
+                copy = pltpu.make_async_copy(
+                    held[kind].at[job, :, at], outs[kind].at[there, at], sems.at[job, kind, piece]
+                )
+                copy.start()
+                copies.append(copy)
     for copy in copies:
         copy.wait()
 
 
-def adam_quarter(flip_core, flip_cube, summed, weight, moment_one, moment_two, filled):
-    rows, columns = weight.shape
+def adam(jobs, filled):
+    rows, columns = jobs[0][3][0].shape
     half = rows // 2
     kinds = (BF16, F32, F32)
-    size = half * columns
-    given = [*summed, weight, moment_one, moment_two]
+    size = len(jobs) * half * columns
+    given = [value for _, _, summed, old in jobs for value in (*summed, *old)]
     return call(
-        functools.partial(adam_kernel, flip_core, flip_cube, len(summed)),
+        functools.partial(adam_kernel, [(core, cube, len(sums)) for core, cube, sums, _ in jobs]),
         [HbmOut(((2 * rows, columns), kind)) for kind in kinds],
         given + list(filled),
         30 * size,
         10 * size,
-        "adam_quarter",
-        scratch=[pltpu.VMEM((half, columns), kind) for kind in kinds]
-        + [pltpu.SemaphoreType.DMA((3, PIECES))],
+        "adam",
+        scratch=[pltpu.VMEM((len(jobs), half, columns), kind) for kind in kinds]
+        + [pltpu.SemaphoreType.DMA((len(jobs), 3, PIECES))],
         aliases={len(given) + at: at for at in range(len(filled))},
         in_hbm=len(filled),
     )
@@ -332,40 +351,38 @@
     clipped, carried = clip_own(scales, grads, residual)
     held, weight = together(carried, weight_old)
     partner_residual, partner_weight = core_swap(held), core_swap(weight)
-    sent, kept = pair_sums(clipped, carried, partner_message)
-
-    def cube_step(sent, step):
-        return [cube_swap(sent[piece], (piece + step) % 3) for piece in range(PIECES)]
-
-    sent, carried = together(sent, carried)
-    arrived = cube_step(sent, 0)
+    sent = pair_sums(True, clipped, carried, partner_message)
+    sent, carried, clipped = together(sent, carried, clipped)
+    kept = list(pair_sums(False, clipped, carried, partner_message))
     left = residual_half(False, scales, carried, grads, ())
-    arrived, left, partner_residual, partner_weight = together(
-        arrived, left, partner_residual, partner_weight
-    )
-    kept = added(kept, arrived)
-
+    sent = list(sent)
+    last = PIECES - 1
+    arrived = [cube_swap(sent[piece], piece) for piece in range(PIECES)]
+    arrived, kept, left, partner_residual, partner_weight = together(
+        arrived, kept, left, partner_residual, partner_weight
+    )
+    kept = [added(*pair) for pair in zip(kept, arrived)]
     kept, one, two, partner_residual = together(kept, moment_one, moment_two, partner_residual)
-    arrived = cube_step(kept, 1)
+    partner_one, partner_two = core_swap(one), core_swap(two)
     left = residual_half(True, scales, partner_residual, grads, left)
-    arrived, left, partner_one, partner_two = together(
-        arrived, left, core_swap(one), core_swap(two)
-    )
-    kept = added(kept, arrived)
-
-    arrived = together(*cube_step(kept, 2))
-    *kept, packed = added(kept, arrived, packed=True)
+    arrived = [cube_swap(kept[piece], piece + 1) for piece in range(PIECES)]
+    arrived[last], left = together(arrived[last], left)
+    kept = [added(*pair) for pair in zip(kept, arrived)]
+    arrived = [cube_swap(kept[piece], piece + 2) for piece in range(PIECES)]
+    arrived[last], partner_one, partner_two = together(arrived[last], partner_one, partner_two)
+    kept = [added(*pair) for pair in zip(kept, arrived)]
 
     own_old = (weight_old, moment_one, moment_two)
     partner_old = (partner_weight, partner_one, partner_two)
-    gathered = cube_step(kept, 0)
-    partner_packed = core_swap(packed)
-    filled = adam_quarter(False, False, kept, *own_old, ())
-    filled = adam_quarter(True, False, [partner_packed], *partner_old, filled)
+    gathered = [cube_swap(kept[piece], piece) for piece in range(PIECES)]
+    partner_packed = core_swap(packed_pieces(kept))
+    filled = adam([(False, False, kept, own_old)], ())
     gathered, filled = together(gathered, filled)
-    partner_gathered = [core_swap(value) for value in gathered]
-    filled = adam_quarter(False, True, gathered, *own_old, filled)
-    filled = adam_quarter(True, True, partner_gathered, *partner_old, filled)
+    partner_gathered = core_swap(packed_pieces(gathered))
+    filled = adam([(True, False, [partner_packed], partner_old)], filled)
+    filled = adam(
+        [(False, True, gathered, own_old), (True, True, [partner_gathered], partner_old)], filled
+    )
     return (filled[0][None], filled[1][None], filled[2][None], left[0][None, None])
 
 

time: 52.7 us -> 50.3 us (0.954)
  waiting for transfers between devices: 7.56 us -> 5.23 us
  Pallas kernels: 18.1 us -> 17.1 us
  starting transfers between devices: 26.1 us -> 26.7 us
    ppermute x9 -> x7, starting transfers between devices: 8.44 us -> 10.9 us  [core_swap(): return lax.ppermute(value, 'section', pairs)]
    ppermute x12, waiting for transfers between devices: 7.54 us -> 5.21 us  [cube_swap(): return lax.ppermute(value, ('section', 'dp'), pairs)]
    ppermute x12, starting transfers between devices: 17.6 us -> 15.8 us  [cube_swap(): return lax.ppermute(value, ('section', 'dp'), pairs)]
    pallas_call x12 -> x20, Pallas kernels: 18.1 us -> 17.1 us  [call(): pl.pallas_call(body, in_specs=[IN_VMEM] * len(near) + [IN_HBM] * in_hbm,...]
  transfers between devices with their start and end apart: 21 -> 19, of which waited for: 6 -> 3; matrix products, arithmetic and copies ran while one was open for 0% -> 0% of each run, Pallas kernels for 28% -> 25%
where the time goes in v4:
time: 50.3 us; the launch traced here: 50.1 us
  starting transfers between devices  26.7 us (53%)
  Pallas kernels  17.1 us (34%)
  waiting for transfers between devices  5.23 us (10%)
  between operations  1.07 us (2%)
    pallas_call x20, Pallas kernels, call(): pl.pallas_call(body, in_specs=[IN_VMEM] * len(near) + [IN_HBM] * in_hbm,...  17.1 us
    ppermute x12, starting transfers between devices, cube_swap(): return lax.ppermute(value, ('section', 'dp'), pairs)  15.8 us
    ppermute x7, starting transfers between devices, core_swap(): return lax.ppermute(value, 'section', pairs)  10.9 us
    ppermute x12, waiting for transfers between devices, cube_swap(): return lax.ppermute(value, ('section', 'dp'), pairs)  5.21 us
  transfers between devices with their start and end apart: 19, of which 3 were waited for; matrix products, arithmetic and copies ran while one was open for 0% of the time, Pallas kernels for 25%

profile of v4, /device:TPU:1, one launch (start us, length us, event | category | flops | bytes accessed | tf_op | source)
XLA Modules:
  0.0 50.1 jit_solution(3679899237901293288)
XLA Ops:
  0.6 1.3 %make_message.1 = (bf16[192,3200]{1,0:T(8,128)(2,1)S(1)}, bf16[384,128]{1,0:T(8,128)(2,1)S(1)}) custom-call(s32[12,1,384]{2,1,0:T(1,128)} %bitcast.18, bf16[384,3072]{1,0:T(8,128)(2,1)} %bitcast.9), custom_call_target="tpu_custom_call" | custom-call | bytes 1179648 | tf_op jit(solution)/shard_map/make_message/pallas_call | solution.py:77
  1.9 1.5 %collective-permute-start = (bf16[192,3200]{1,0:T(8,128)(2,1)S(1)}, bf16[192,3200]{1,0:T(8,128)(2,1)S(1)}, u32[]{:S(2)}, u32[]{:S(2)}) collective-permute-start(bf16[192,3200]{1,0:T(8,128)(2,1)S(1)} %get-tuple-element.59), channel_id=1, source_target_pairs={{0,8},{8,0},{16,24},{24,16},{32,40},{40,32},{48,56},{56,48},{64,72... | collective-permute-start | bytes 3686408 | tf_op jit(solution)/shard_map/ppermute | solution.py:31
  3.4 2.1 %clip_own.1 = (bf16[192,3072]{1,0:T(8,128)(2,1)S(1)}, bf16[192,3072]{1,0:T(8,128)(2,1)S(1)}) custom-call(bf16[384,128]{1,0:T(8,128)(2,1)S(1)} %get-tuple-element.56.scales, bf16[384,3072]{1,0:T(8,128)(2,1)} %bitcast.10, bf16[192,3072]{1,0:T(8,128)(2,1)} %bitcast.17), custom_call_target="tpu_custom_call" | custom-call | flops 2359296 | bytes 2359296 | tf_op jit(solution)/shard_map/clip_own/pallas_call | solution.py:77
  5.5 0.2 collective-permute-start.4
  5.7 0.4 collective-permute-start.5
  6.1 0.4 pair_sums.2
  6.6 2.9 %collective-permute-start.1 = (bf16[96,1024]{1,0:T(8,128)(2,1)S(1)}, bf16[96,1024]{1,0:T(8,128)(2,1)S(1)}, u32[]{:S(2)}, u32[]{:S(2)}) collective-permute-start(bf16[96,1024]{1,0:T(8,128)(2,1)S(1)} %get-tuple-element.63), channel_id=1, source_target_pairs={{0,2},{1,3},{2,0},{3,1},{4,6},{5,7},{6,4},{7,5},{8,9},{9,8},{10,11... | collective-permute-start | bytes 589832 | tf_op jit(solution)/shard_map/ppermute | solution.py:53
  9.5 1.3 %collective-permute-start.2 = (bf16[96,1024]{1,0:T(8,128)(2,1)S(1)}, bf16[96,1024]{1,0:T(8,128)(2,1)S(1)}, u32[]{:S(2)}, u32[]{:S(2)}) collective-permute-start(bf16[96,1024]{1,0:T(8,128)(2,1)S(1)} %get-tuple-element.64), channel_id=1, source_target_pairs={{0,6},{1,7},{2,4},{3,5},{4,2},{5,3},{6,0},{7,1},{8,10},{9,11},{10,... | collective-permute-start | bytes 589832 | tf_op jit(solution)/shard_map/ppermute | solution.py:53
  10.7 1.9 %collective-permute-start.3 = (bf16[96,1024]{1,0:T(8,128)(2,1)S(1)}, bf16[96,1024]{1,0:T(8,128)(2,1)S(1)}, u32[]{:S(2)}, u32[]{:S(2)}) collective-permute-start(bf16[96,1024]{1,0:T(8,128)(2,1)S(1)} %get-tuple-element.65), channel_id=1, source_target_pairs={{0,1},{1,0},{2,3},{3,2},{4,5},{5,4},{6,7},{7,6},{8,14},{9,15},{10,... | collective-permute-start | bytes 589832 | tf_op jit(solution)/shard_map/ppermute | solution.py:53
  12.6 0.4 pair_sums.3
  13.0 0.0 copy-start.1
  13.1 2.9 %residual_half.2.refs_0_ = bf16[384,3072]{1,0:T(8,128)(2,1)} custom-call(bf16[384,128]{1,0:T(8,128)(2,1)S(1)} %get-tuple-element.56.scales, bf16[192,3072]{1,0:T(8,128)(2,1)S(1)} %get-tuple-element.71.residual, bf16[384,3072]{1,0:T(8,128)(2,1)} %bitcast.11), custom_call_target="tpu_custom_call" | custom-call | flops 3538944 | bytes 2359296 | tf_op jit(solution)/shard_map/residual_half/pallas_call | solution.py:77
  16.0 1.1 %collective-permute-done.3.theirs = bf16[96,1024]{1,0:T(8,128)(2,1)S(1)} collective-permute-done((bf16[96,1024]{1,0:T(8,128)(2,1)S(1)}, bf16[96,1024]{1,0:T(8,128)(2,1)S(1)}, u32[]{:S(2)}, u32[]{:S(2)}) %collective-permute-start.3) | collective-permute-done | bytes 196640 | tf_op jit(solution)/shard_map/ppermute | solution.py:53
  17.2 0.8 %collective-permute-start.14 = (f32[192,3072]{1,0:T(8,128)S(1)}, f32[192,3072]{1,0:T(8,128)S(1)}, u32[]{:S(2)}, u32[]{:S(2)}) collective-permute-start(f32[192,3072]{1,0:T(8,128)S(1)} %copy-done), channel_id=1, source_target_pairs={{0,8},{8,0},{16,24},{24,16},{32,40},{40,32},{48,56},{56,48},{64,72... | collective-permute-start | bytes 7077896 | tf_op jit(solution)/shard_map/ppermute | solution.py:31
  18.0 0.1 collective-permute-start.15
  18.1 0.4 collective-permute-start.6
  18.5 0.9 %collective-permute-start.9 = (bf16[96,1024]{1,0:T(8,128)(2,1)S(1)}, bf16[96,1024]{1,0:T(8,128)(2,1)S(1)}, u32[]{:S(2)}, u32[]{:S(2)}) collective-permute-start(bf16[96,1024]{1,0:T(8,128)(2,1)S(1)} %added.10.mine), channel_id=1, source_target_pairs={{0,1},{1,0},{2,3},{3,2},{4,5},{5,4},{6,7},{7,6},{8,14},{9,15},{10,... | collective-permute-start | bytes 589832 | tf_op jit(solution)/shard_map/ppermute | solution.py:53
  19.4 2.3 %collective-permute-start.12 = (bf16[96,1024]{1,0:T(8,128)(2,1)S(1)}, bf16[96,1024]{1,0:T(8,128)(2,1)S(1)}, u32[]{:S(2)}, u32[]{:S(2)}) collective-permute-start(bf16[96,1024]{1,0:T(8,128)(2,1)S(1)} %added.11.mine), channel_id=1, source_target_pairs={{0,2},{1,3},{2,0},{3,1},{4,6},{5,7},{6,4},{7,5},{8,9},{9,8},{10,11... | collective-permute-start | bytes 589832 | tf_op jit(solution)/shard_map/ppermute | solution.py:53
  21.7 2.7 %residual_half.3 = bf16[384,3072]{1,0:T(8,128)(2,1)} custom-call(bf16[384,128]{1,0:T(8,128)(2,1)S(1)} %get-tuple-element.56.scales, bf16[192,3072]{1,0:T(8,128)(2,1)S(1)} %collective-permute-done.4.residual, bf16[384,3072]{1,0:T(8,128)(2,1)} %bitcast.12, bf16[384,3072]{1,0:T(8,128)(2,1)} %residual_half.2.refs_0_), custom_call_target="tpu_custom_call", output_to_operand_aliasing={{}: (3, {})} | custom-call | flops 3538944 | bytes 2359296 | tf_op jit(solution)/shard_map/residual_half/pallas_call | solution.py:77
  24.5 2.3 %collective-permute-start.7 = (bf16[96,1024]{1,0:T(8,128)(2,1)S(1)}, bf16[96,1024]{1,0:T(8,128)(2,1)S(1)}, u32[]{:S(2)}, u32[]{:S(2)}) collective-permute-start(bf16[96,1024]{1,0:T(8,128)(2,1)S(1)} %added.12.mine), channel_id=1, source_target_pairs={{0,1},{1,0},{2,3},{3,2},{4,5},{5,4},{6,7},{7,6},{8,14},{9,15},{10,... | collective-permute-start | bytes 589832 | tf_op jit(solution)/shard_map/ppermute | solution.py:53
  26.8 2.3 %collective-permute-start.10 = (bf16[96,1024]{1,0:T(8,128)(2,1)S(1)}, bf16[96,1024]{1,0:T(8,128)(2,1)S(1)}, u32[]{:S(2)}, u32[]{:S(2)}) collective-permute-start(bf16[96,1024]{1,0:T(8,128)(2,1)S(1)} %added.14.mine), channel_id=1, source_target_pairs={{0,2},{1,3},{2,0},{3,1},{4,6},{5,7},{6,4},{7,5},{8,9},{9,8},{10,11... | collective-permute-start | bytes 589832 | tf_op jit(solution)/shard_map/ppermute | solution.py:53
  29.2 0.1 collective-permute-start.13
  29.3 1.0 %collective-permute-done.7.theirs = bf16[96,1024]{1,0:T(8,128)(2,1)S(1)} collective-permute-done((bf16[96,1024]{1,0:T(8,128)(2,1)S(1)}, bf16[96,1024]{1,0:T(8,128)(2,1)S(1)}, u32[]{:S(2)}, u32[]{:S(2)}) %collective-permute-start.7) | collective-permute-done | bytes 196640 | tf_op jit(solution)/shard_map/ppermute | solution.py:53
  30.4 1.3 %collective-permute-start.8 = (bf16[96,1024]{1,0:T(8,128)(2,1)S(1)}, bf16[96,1024]{1,0:T(8,128)(2,1)S(1)}, u32[]{:S(2)}, u32[]{:S(2)}) collective-permute-start(bf16[96,1024]{1,0:T(8,128)(2,1)S(1)} %added.13.refs_0_), channel_id=1, source_target_pairs={{0,2},{1,3},{2,0},{3,1},{4,6},{5,7},{6,4},{7,5},{8,9},{9,8},{10,11... | collective-permute-start | bytes 589832 | tf_op jit(solution)/shard_map/ppermute | solution.py:53
  31.6 3.0 %collective-permute-done.10.theirs = bf16[96,1024]{1,0:T(8,128)(2,1)S(1)} collective-permute-done((bf16[96,1024]{1,0:T(8,128)(2,1)S(1)}, bf16[96,1024]{1,0:T(8,128)(2,1)S(1)}, u32[]{:S(2)}, u32[]{:S(2)}) %collective-permute-start.10) | collective-permute-done | bytes 196640 | tf_op jit(solution)/shard_map/ppermute | solution.py:53
  34.7 0.1 collective-permute-start.11
  34.9 0.1 collective-permute-start.16
  35.0 5.0 %collective-permute-start.18 = (bf16[96,3072]{1,0:T(8,128)(2,1)S(1)}, bf16[96,3072]{1,0:T(8,128)(2,1)S(1)}, u32[]{:S(2)}, u32[]{:S(2)}) collective-permute-start(bf16[96,3072]{1,0:T(8,128)(2,1)S(1)} %pack.3), channel_id=1, source_target_pairs={{0,8},{8,0},{16,24},{24,16},{32,40},{40,32},{48,56},{56,48},{64,72... | collective-permute-start | bytes 1769480 | tf_op jit(solution)/shard_map/ppermute | solution.py:31
  40.0 2.0 %adam.3 = (bf16[384,3072]{1,0:T(8,128)(2,1)}, f32[384,3072]{1,0:T(8,128)}, f32[384,3072]{1,0:T(8,128)}) custom-call(bf16[96,1024]{1,0:T(8,128)(2,1)S(1)} %added.13.refs_0_, bf16[96,1024]{1,0:T(8,128)(2,1)S(1)} %added.15.refs_1_, bf16[96,1024]{1,0:T(8,128)(2,1)S(1)} %added.17.refs_2_, bf16[192,3072]{1,0:T(8,128)(2,1)S(1)} %copy-done.2, ...), custom_call_target="tpu_custom_call" | custom-call | flops 8847360 | bytes 2949120 | tf_op jit(solution)/shard_map/adam/pallas_call | solution.py:77
  42.1 2.8 %collective-permute-start.17 = (bf16[96,3072]{1,0:T(8,128)(2,1)S(1)}, bf16[96,3072]{1,0:T(8,128)(2,1)S(1)}, u32[]{:S(2)}, u32[]{:S(2)}) collective-permute-start(bf16[96,3072]{1,0:T(8,128)(2,1)S(1)} %pack.2), channel_id=1, source_target_pairs={{0,8},{8,0},{16,24},{24,16},{32,40},{40,32},{48,56},{56,48},{64,72... | collective-permute-start | bytes 1769480 | tf_op jit(solution)/shard_map/ppermute | solution.py:31
  44.9 2.0 %adam.4 = (bf16[384,3072]{1,0:T(8,128)(2,1)}, f32[384,3072]{1,0:T(8,128)}, f32[384,3072]{1,0:T(8,128)}) custom-call(bf16[96,3072]{1,0:T(8,128)(2,1)S(1)} %collective-permute-done.18.refs_0_, bf16[192,3072]{1,0:T(8,128)(2,1)S(1)} %collective-permute-done.5.refs_1_.refs_7_, ...), custom_call_target="tpu_custom_call", output_to_operand_aliasing={{0}: (4, {}), {1}: (5, {}), {2}: (6, {})} | custom-call | flops 8847360 | bytes 2949120 | tf_op jit(solution)/shard_map/adam/pallas_call | solution.py:77
  46.9 3.0 %adam.5 = (bf16[384,3072]{1,0:T(8,128)(2,1)}, f32[384,3072]{1,0:T(8,128)}, f32[384,3072]{1,0:T(8,128)}) custom-call(bf16[96,1024]{1,0:T(8,128)(2,1)S(1)} %collective-permute-done.8.refs_0_, bf16[96,1024]{1,0:T(8,128)(2,1)S(1)} %collective-permute-done.11.refs_1_, ...), custom_call_target="tpu_custom_call", output_to_operand_aliasing={{0}: (10, {}), {1}: (11, {}), {2}: (12, {})} | custom-call | flops 17694720 | bytes 5898240 | tf_op jit(solution)/shard_map/adam/pallas_call | solution.py:77
  (32 shorter events, 0.3 us)
Async XLA Ops:
  1.9 3.8 %copy-start.2 = (bf16[192,3072]{1,0:T(8,128)(2,1)S(1)}, bf16[192,3072]{1,0:T(8,128)(2,1)}, u32[]{:S(2)}) copy-start(bf16[192,3072]{1,0:T(8,128)(2,1)} %refs_3_.3) | copy-start | bytes 3538948
  1.9 4.2 %collective-permute-start = (bf16[192,3200]{1,0:T(8,128)(2,1)S(1)}, bf16[192,3200]{1,0:T(8,128)(2,1)S(1)}, u32[]{:S(2)}, u32[]{:S(2)}) collective-permute-start(bf16[192,3200]{1,0:T(8,128)(2,1)S(1)} %get-tuple-element.59), channel_id=1, source_target_pairs={{0,8},{8,0},{16,24},{24,16},{32,40},{40,32},{48,56},{56,48},{64,72... | collective-permute-start | bytes 3686408 | tf_op jit(solution)/shard_map/ppermute | solution.py:31
  5.5 10.4 %collective-permute-start.4 = (bf16[192,3072]{1,0:T(8,128)(2,1)S(1)}, bf16[192,3072]{1,0:T(8,128)(2,1)S(1)}, u32[]{:S(2)}, u32[]{:S(2)}) collective-permute-start(bf16[192,3072]{1,0:T(8,128)(2,1)S(1)} %get-tuple-element.71.residual), channel_id=1, source_target_pairs={{0,8},{8,0},{16,24},{24,16},{32,40},{40,32},{48,56},{56,48},{64,72... | collective-permute-start | bytes 3538952 | tf_op jit(solution)/shard_map/ppermute | solution.py:31
  5.7 10.2 %collective-permute-start.5 = (bf16[192,3072]{1,0:T(8,128)(2,1)S(1)}, bf16[192,3072]{1,0:T(8,128)(2,1)S(1)}, u32[]{:S(2)}, u32[]{:S(2)}) collective-permute-start(bf16[192,3072]{1,0:T(8,128)(2,1)S(1)} %copy-done.2), channel_id=1, source_target_pairs={{0,8},{8,0},{16,24},{24,16},{32,40},{40,32},{48,56},{56,48},{64,72... | collective-permute-start | bytes 3538952 | tf_op jit(solution)/shard_map/ppermute | solution.py:31
  6.6 9.4 %collective-permute-start.1 = (bf16[96,1024]{1,0:T(8,128)(2,1)S(1)}, bf16[96,1024]{1,0:T(8,128)(2,1)S(1)}, u32[]{:S(2)}, u32[]{:S(2)}) collective-permute-start(bf16[96,1024]{1,0:T(8,128)(2,1)S(1)} %get-tuple-element.63), channel_id=1, source_target_pairs={{0,2},{1,3},{2,0},{3,1},{4,6},{5,7},{6,4},{7,5},{8,9},{9,8},{10,11... | collective-permute-start | bytes 589832 | tf_op jit(solution)/shard_map/ppermute | solution.py:53
  9.5 6.5 %collective-permute-start.2 = (bf16[96,1024]{1,0:T(8,128)(2,1)S(1)}, bf16[96,1024]{1,0:T(8,128)(2,1)S(1)}, u32[]{:S(2)}, u32[]{:S(2)}) collective-permute-start(bf16[96,1024]{1,0:T(8,128)(2,1)S(1)} %get-tuple-element.64), channel_id=1, source_target_pairs={{0,6},{1,7},{2,4},{3,5},{4,2},{5,3},{6,0},{7,1},{8,10},{9,11},{10,... | collective-permute-start | bytes 589832 | tf_op jit(solution)/shard_map/ppermute | solution.py:53
  10.7 6.4 %collective-permute-start.3 = (bf16[96,1024]{1,0:T(8,128)(2,1)S(1)}, bf16[96,1024]{1,0:T(8,128)(2,1)S(1)}, u32[]{:S(2)}, u32[]{:S(2)}) collective-permute-start(bf16[96,1024]{1,0:T(8,128)(2,1)S(1)} %get-tuple-element.65), channel_id=1, source_target_pairs={{0,1},{1,0},{2,3},{3,2},{4,5},{5,4},{6,7},{7,6},{8,14},{9,15},{10,... | collective-permute-start | bytes 589832 | tf_op jit(solution)/shard_map/ppermute | solution.py:53
  13.0 4.2 %copy-start = (f32[192,3072]{1,0:T(8,128)S(1)}, f32[192,3072]{1,0:T(8,128)}, u32[]{:S(2)}) copy-start(f32[192,3072]{1,0:T(8,128)} %refs_4_.3) | copy-start | bytes 7077892
  13.0 5.0 %copy-start.1 = (f32[192,3072]{1,0:T(8,128)S(1)}, f32[192,3072]{1,0:T(8,128)}, u32[]{:S(2)}) copy-start(f32[192,3072]{1,0:T(8,128)} %refs_5_.3) | copy-start | bytes 7077892
  17.2 17.6 %collective-permute-start.14 = (f32[192,3072]{1,0:T(8,128)S(1)}, f32[192,3072]{1,0:T(8,128)S(1)}, u32[]{:S(2)}, u32[]{:S(2)}) collective-permute-start(f32[192,3072]{1,0:T(8,128)S(1)} %copy-done), channel_id=1, source_target_pairs={{0,8},{8,0},{16,24},{24,16},{32,40},{40,32},{48,56},{56,48},{64,72... | collective-permute-start | bytes 7077896 | tf_op jit(solution)/shard_map/ppermute | solution.py:31
  18.0 16.8 %collective-permute-start.15 = (f32[192,3072]{1,0:T(8,128)S(1)}, f32[192,3072]{1,0:T(8,128)S(1)}, u32[]{:S(2)}, u32[]{:S(2)}) collective-permute-start(f32[192,3072]{1,0:T(8,128)S(1)} %copy-done.1), channel_id=1, source_target_pairs={{0,8},{8,0},{16,24},{24,16},{32,40},{40,32},{48,56},{56,48},{64,72... | collective-permute-start | bytes 7077896 | tf_op jit(solution)/shard_map/ppermute | solution.py:31
  18.1 6.3 %collective-permute-start.6 = (bf16[96,1024]{1,0:T(8,128)(2,1)S(1)}, bf16[96,1024]{1,0:T(8,128)(2,1)S(1)}, u32[]{:S(2)}, u32[]{:S(2)}) collective-permute-start(bf16[96,1024]{1,0:T(8,128)(2,1)S(1)} %added.9.mine), channel_id=1, source_target_pairs={{0,6},{1,7},{2,4},{3,5},{4,2},{5,3},{6,0},{7,1},{8,10},{9,11},{10,... | collective-permute-start | bytes 589832 | tf_op jit(solution)/shard_map/ppermute | solution.py:53
  18.5 8.3 %collective-permute-start.9 = (bf16[96,1024]{1,0:T(8,128)(2,1)S(1)}, bf16[96,1024]{1,0:T(8,128)(2,1)S(1)}, u32[]{:S(2)}, u32[]{:S(2)}) collective-permute-start(bf16[96,1024]{1,0:T(8,128)(2,1)S(1)} %added.10.mine), channel_id=1, source_target_pairs={{0,1},{1,0},{2,3},{3,2},{4,5},{5,4},{6,7},{7,6},{8,14},{9,15},{10,... | collective-permute-start | bytes 589832 | tf_op jit(solution)/shard_map/ppermute | solution.py:53
  19.4 9.7 %collective-permute-start.12 = (bf16[96,1024]{1,0:T(8,128)(2,1)S(1)}, bf16[96,1024]{1,0:T(8,128)(2,1)S(1)}, u32[]{:S(2)}, u32[]{:S(2)}) collective-permute-start(bf16[96,1024]{1,0:T(8,128)(2,1)S(1)} %added.11.mine), channel_id=1, source_target_pairs={{0,2},{1,3},{2,0},{3,1},{4,6},{5,7},{6,4},{7,5},{8,9},{9,8},{10,11... | collective-permute-start | bytes 589832 | tf_op jit(solution)/shard_map/ppermute | solution.py:53
  24.5 5.8 %collective-permute-start.7 = (bf16[96,1024]{1,0:T(8,128)(2,1)S(1)}, bf16[96,1024]{1,0:T(8,128)(2,1)S(1)}, u32[]{:S(2)}, u32[]{:S(2)}) collective-permute-start(bf16[96,1024]{1,0:T(8,128)(2,1)S(1)} %added.12.mine), channel_id=1, source_target_pairs={{0,1},{1,0},{2,3},{3,2},{4,5},{5,4},{6,7},{7,6},{8,14},{9,15},{10,... | collective-permute-start | bytes 589832 | tf_op jit(solution)/shard_map/ppermute | solution.py:53
  26.8 7.8 %collective-permute-start.10 = (bf16[96,1024]{1,0:T(8,128)(2,1)S(1)}, bf16[96,1024]{1,0:T(8,128)(2,1)S(1)}, u32[]{:S(2)}, u32[]{:S(2)}) collective-permute-start(bf16[96,1024]{1,0:T(8,128)(2,1)S(1)} %added.14.mine), channel_id=1, source_target_pairs={{0,2},{1,3},{2,0},{3,1},{4,6},{5,7},{6,4},{7,5},{8,9},{9,8},{10,11... | collective-permute-start | bytes 589832 | tf_op jit(solution)/shard_map/ppermute | solution.py:53
  29.2 5.6 %collective-permute-start.13 = (bf16[96,1024]{1,0:T(8,128)(2,1)S(1)}, bf16[96,1024]{1,0:T(8,128)(2,1)S(1)}, u32[]{:S(2)}, u32[]{:S(2)}) collective-permute-start(bf16[96,1024]{1,0:T(8,128)(2,1)S(1)} %added.16.mine), channel_id=1, source_target_pairs={{0,6},{1,7},{2,4},{3,5},{4,2},{5,3},{6,0},{7,1},{8,10},{9,11},{10,... | collective-permute-start | bytes 589832 | tf_op jit(solution)/shard_map/ppermute | solution.py:53
  30.4 11.7 %collective-permute-start.8 = (bf16[96,1024]{1,0:T(8,128)(2,1)S(1)}, bf16[96,1024]{1,0:T(8,128)(2,1)S(1)}, u32[]{:S(2)}, u32[]{:S(2)}) collective-permute-start(bf16[96,1024]{1,0:T(8,128)(2,1)S(1)} %added.13.refs_0_), channel_id=1, source_target_pairs={{0,2},{1,3},{2,0},{3,1},{4,6},{5,7},{6,4},{7,5},{8,9},{9,8},{10,11... | collective-permute-start | bytes 589832 | tf_op jit(solution)/shard_map/ppermute | solution.py:53
  34.7 7.4 %collective-permute-start.11 = (bf16[96,1024]{1,0:T(8,128)(2,1)S(1)}, bf16[96,1024]{1,0:T(8,128)(2,1)S(1)}, u32[]{:S(2)}, u32[]{:S(2)}) collective-permute-start(bf16[96,1024]{1,0:T(8,128)(2,1)S(1)} %added.15.refs_1_), channel_id=1, source_target_pairs={{0,6},{1,7},{2,4},{3,5},{4,2},{5,3},{6,0},{7,1},{8,10},{9,11},{10,... | collective-permute-start | bytes 589832 | tf_op jit(solution)/shard_map/ppermute | solution.py:53
  34.9 7.2 %collective-permute-start.16 = (bf16[96,1024]{1,0:T(8,128)(2,1)S(1)}, bf16[96,1024]{1,0:T(8,128)(2,1)S(1)}, u32[]{:S(2)}, u32[]{:S(2)}) collective-permute-start(bf16[96,1024]{1,0:T(8,128)(2,1)S(1)} %added.17.refs_2_), channel_id=1, source_target_pairs={{0,1},{1,0},{2,3},{3,2},{4,5},{5,4},{6,7},{7,6},{8,14},{9,15},{10,... | collective-permute-start | bytes 589832 | tf_op jit(solution)/shard_map/ppermute | solution.py:53
  35.0 9.9 %collective-permute-start.18 = (bf16[96,3072]{1,0:T(8,128)(2,1)S(1)}, bf16[96,3072]{1,0:T(8,128)(2,1)S(1)}, u32[]{:S(2)}, u32[]{:S(2)}) collective-permute-start(bf16[96,3072]{1,0:T(8,128)(2,1)S(1)} %pack.3), channel_id=1, source_target_pairs={{0,8},{8,0},{16,24},{24,16},{32,40},{40,32},{48,56},{56,48},{64,72... | collective-permute-start | bytes 1769480 | tf_op jit(solution)/shard_map/ppermute | solution.py:31
  42.1 4.8 %collective-permute-start.17 = (bf16[96,3072]{1,0:T(8,128)(2,1)S(1)}, bf16[96,3072]{1,0:T(8,128)(2,1)S(1)}, u32[]{:S(2)}, u32[]{:S(2)}) collective-permute-start(bf16[96,3072]{1,0:T(8,128)(2,1)S(1)} %pack.2), channel_id=1, source_target_pairs={{0,8},{8,0},{16,24},{24,16},{32,40},{40,32},{48,56},{56,48},{64,72... | collective-permute-start | bytes 1769480 | tf_op jit(solution)/shard_map/ppermute | solution.py:31

commit v5 on v4

--- a/solution.py
+++ b/solution.py
@@ -182,11 +182,12 @@
     )
 
 
-def pair_kernel(flip_cube, clipped, residual, message, *outs):
+def pair_kernel(flip_cube, pieces, clipped, residual, message, *outs):
     rows, columns = residual.shape
     half = rows // 2
     bits = cube_bits(core_parity())
-    for out, bit, first, width in zip(outs, bits, STARTS, WIDTHS):
+    for out, piece in zip(outs, pieces):
+        bit, first, width = bits[piece], STARTS[piece], WIDTHS[piece]
         here = aligned((1 - bit if flip_cube else bit) * half, half)
         scale = message[here, columns:]
         for block in range(first // BLOCK, (first + width) // BLOCK):
@@ -197,12 +198,12 @@
             out[:, to] = clipped[here, at] + partner
 
 
-def pair_sums(flip_cube, clipped, residual, message):
+def pair_sums(flip_cube, pieces, clipped, residual, message):
     rows, columns = residual.shape
     size = rows * columns // 2
     return call(
-        functools.partial(pair_kernel, flip_cube),
-        [((rows // 2, width), BF16) for width in WIDTHS],
+        functools.partial(pair_kernel, flip_cube, pieces),
+        [((rows // 2, WIDTHS[piece]), BF16) for piece in pieces],
         [clipped, residual, message],
         5 * size,
         size,
@@ -351,9 +352,10 @@
     clipped, carried = clip_own(scales, grads, residual)
     held, weight = together(carried, weight_old)
     partner_residual, partner_weight = core_swap(held), core_swap(weight)
-    sent = pair_sums(True, clipped, carried, partner_message)
-    sent, carried, clipped = together(sent, carried, clipped)
-    kept = list(pair_sums(False, clipped, carried, partner_message))
+    pieces = range(PIECES)
+    sent = [pair_sums(True, [piece], clipped, carried, partner_message)[0] for piece in pieces]
+    sent[-1], carried, clipped = together(sent[-1], carried, clipped)
+    kept = list(pair_sums(False, list(pieces), clipped, carried, partner_message))
     left = residual_half(False, scales, carried, grads, ())
     sent = list(sent)
     last = PIECES - 1

time: 50.3 us -> 50.5 us (level)
    pallas_call x20 -> x22, Pallas kernels: 17.1 us -> 17.3 us  [call(): pl.pallas_call(body, in_specs=[IN_VMEM] * len(near) + [IN_HBM] * in_hbm,...]
  transfers between devices with their start and end apart: 19 -> 19, of which waited for: 3 -> 3; matrix products, arithmetic and copies ran while one was open for 0% -> 0% of each run, Pallas kernels for 25% -> 26%
where the time goes in v5:
time: 50.5 us; the launch traced here: 50.4 us
  starting transfers between devices  26.8 us (53%)
  Pallas kernels  17.3 us (34%)
  waiting for transfers between devices  5.19 us (10%)
  between operations  1.08 us (2%)
    pallas_call x22, Pallas kernels, call(): pl.pallas_call(body, in_specs=[IN_VMEM] * len(near) + [IN_HBM] * in_hbm,...  17.3 us
    ppermute x12, starting transfers between devices, cube_swap(): return lax.ppermute(value, ('section', 'dp'), pairs)  16 us
    ppermute x7, starting transfers between devices, core_swap(): return lax.ppermute(value, 'section', pairs)  10.9 us
    ppermute x12, waiting for transfers between devices, cube_swap(): return lax.ppermute(value, ('section', 'dp'), pairs)  5.17 us
  transfers between devices with their start and end apart: 19, of which 3 were waited for; matrix products, arithmetic and copies ran while one was open for 0% of the time, Pallas kernels for 26%

profile of v5, /device:TPU:1, one launch (start us, length us, event | category | flops | bytes accessed | tf_op | source)
XLA Modules:
  0.0 50.4 jit_solution(17603821417348958351)
XLA Ops:
  0.6 1.3 %make_message.1 = (bf16[192,3200]{1,0:T(8,128)(2,1)S(1)}, bf16[384,128]{1,0:T(8,128)(2,1)S(1)}) custom-call(s32[12,1,384]{2,1,0:T(1,128)} %bitcast.18, bf16[384,3072]{1,0:T(8,128)(2,1)} %bitcast.9), custom_call_target="tpu_custom_call" | custom-call | bytes 1179648 | tf_op jit(solution)/shard_map/make_message/pallas_call | solution.py:77
  1.9 1.5 %collective-permute-start = (bf16[192,3200]{1,0:T(8,128)(2,1)S(1)}, bf16[192,3200]{1,0:T(8,128)(2,1)S(1)}, u32[]{:S(2)}, u32[]{:S(2)}) collective-permute-start(bf16[192,3200]{1,0:T(8,128)(2,1)S(1)} %get-tuple-element.54), channel_id=1, source_target_pairs={{0,8},{8,0},{16,24},{24,16},{32,40},{40,32},{48,56},{56,48},{64,72... | collective-permute-start | bytes 3686408 | tf_op jit(solution)/shard_map/ppermute | solution.py:31
  3.4 2.1 %clip_own.1 = (bf16[192,3072]{1,0:T(8,128)(2,1)S(1)}, bf16[192,3072]{1,0:T(8,128)(2,1)S(1)}) custom-call(bf16[384,128]{1,0:T(8,128)(2,1)S(1)} %get-tuple-element.51.scales, bf16[384,3072]{1,0:T(8,128)(2,1)} %bitcast.10, bf16[192,3072]{1,0:T(8,128)(2,1)} %bitcast.17), custom_call_target="tpu_custom_call" | custom-call | flops 2359296 | bytes 2359296 | tf_op jit(solution)/shard_map/clip_own/pallas_call | solution.py:77
  5.5 0.2 collective-permute-start.4
  5.7 0.4 collective-permute-start.5
  6.1 0.2 pair_sums.6
  6.3 0.2 pair_sums.4
  6.5 2.9 %collective-permute-start.1 = (bf16[96,1024]{1,0:T(8,128)(2,1)S(1)}, bf16[96,1024]{1,0:T(8,128)(2,1)S(1)}, u32[]{:S(2)}, u32[]{:S(2)}) collective-permute-start(bf16[96,1024]{1,0:T(8,128)(2,1)S(1)} %pair_sums.4), channel_id=1, source_target_pairs={{0,2},{1,3},{2,0},{3,1},{4,6},{5,7},{6,4},{7,5},{8,9},{9,8},{10,11... | collective-permute-start | bytes 589832 | tf_op jit(solution)/shard_map/ppermute | solution.py:53
  9.4 0.2 pair_sums.5
  9.6 1.4 %collective-permute-start.2 = (bf16[96,1024]{1,0:T(8,128)(2,1)S(1)}, bf16[96,1024]{1,0:T(8,128)(2,1)S(1)}, u32[]{:S(2)}, u32[]{:S(2)}) collective-permute-start(bf16[96,1024]{1,0:T(8,128)(2,1)S(1)} %pair_sums.5), channel_id=1, source_target_pairs={{0,6},{1,7},{2,4},{3,5},{4,2},{5,3},{6,0},{7,1},{8,10},{9,11},{10,... | collective-permute-start | bytes 589832 | tf_op jit(solution)/shard_map/ppermute | solution.py:53
  11.0 1.9 %collective-permute-start.3 = (bf16[96,1024]{1,0:T(8,128)(2,1)S(1)}, bf16[96,1024]{1,0:T(8,128)(2,1)S(1)}, u32[]{:S(2)}, u32[]{:S(2)}) collective-permute-start(bf16[96,1024]{1,0:T(8,128)(2,1)S(1)} %pair_sums.6), channel_id=1, source_target_pairs={{0,1},{1,0},{2,3},{3,2},{4,5},{5,4},{6,7},{7,6},{8,14},{9,15},{10,... | collective-permute-start | bytes 589832 | tf_op jit(solution)/shard_map/ppermute | solution.py:53
  12.9 0.4 pair_sums.7
  13.3 2.9 %residual_half.2.refs_0_ = bf16[384,3072]{1,0:T(8,128)(2,1)} custom-call(bf16[384,128]{1,0:T(8,128)(2,1)S(1)} %get-tuple-element.51.scales, bf16[192,3072]{1,0:T(8,128)(2,1)S(1)} %get-tuple-element.61.residual, bf16[384,3072]{1,0:T(8,128)(2,1)} %bitcast.11), custom_call_target="tpu_custom_call" | custom-call | flops 3538944 | bytes 2359296 | tf_op jit(solution)/shard_map/residual_half/pallas_call | solution.py:77
  16.3 1.1 %collective-permute-done.3.theirs = bf16[96,1024]{1,0:T(8,128)(2,1)S(1)} collective-permute-done((bf16[96,1024]{1,0:T(8,128)(2,1)S(1)}, bf16[96,1024]{1,0:T(8,128)(2,1)S(1)}, u32[]{:S(2)}, u32[]{:S(2)}) %collective-permute-start.3) | collective-permute-done | bytes 196640 | tf_op jit(solution)/shard_map/ppermute | solution.py:53
  17.4 0.8 %collective-permute-start.14 = (f32[192,3072]{1,0:T(8,128)S(1)}, f32[192,3072]{1,0:T(8,128)S(1)}, u32[]{:S(2)}, u32[]{:S(2)}) collective-permute-start(f32[192,3072]{1,0:T(8,128)S(1)} %copy-done), channel_id=1, source_target_pairs={{0,8},{8,0},{16,24},{24,16},{32,40},{40,32},{48,56},{56,48},{64,72... | collective-permute-start | bytes 7077896 | tf_op jit(solution)/shard_map/ppermute | solution.py:31
  18.3 0.1 collective-permute-start.15
  18.4 0.4 collective-permute-start.6
  18.8 0.9 %collective-permute-start.9 = (bf16[96,1024]{1,0:T(8,128)(2,1)S(1)}, bf16[96,1024]{1,0:T(8,128)(2,1)S(1)}, u32[]{:S(2)}, u32[]{:S(2)}) collective-permute-start(bf16[96,1024]{1,0:T(8,128)(2,1)S(1)} %added.10.mine), channel_id=1, source_target_pairs={{0,1},{1,0},{2,3},{3,2},{4,5},{5,4},{6,7},{7,6},{8,14},{9,15},{10,... | collective-permute-start | bytes 589832 | tf_op jit(solution)/shard_map/ppermute | solution.py:53
  19.7 2.3 %collective-permute-start.12 = (bf16[96,1024]{1,0:T(8,128)(2,1)S(1)}, bf16[96,1024]{1,0:T(8,128)(2,1)S(1)}, u32[]{:S(2)}, u32[]{:S(2)}) collective-permute-start(bf16[96,1024]{1,0:T(8,128)(2,1)S(1)} %added.11.mine), channel_id=1, source_target_pairs={{0,2},{1,3},{2,0},{3,1},{4,6},{5,7},{6,4},{7,5},{8,9},{9,8},{10,11... | collective-permute-start | bytes 589832 | tf_op jit(solution)/shard_map/ppermute | solution.py:53
  21.9 2.7 %residual_half.3 = bf16[384,3072]{1,0:T(8,128)(2,1)} custom-call(bf16[384,128]{1,0:T(8,128)(2,1)S(1)} %get-tuple-element.51.scales, bf16[192,3072]{1,0:T(8,128)(2,1)S(1)} %collective-permute-done.4.residual, bf16[384,3072]{1,0:T(8,128)(2,1)} %bitcast.12, bf16[384,3072]{1,0:T(8,128)(2,1)} %residual_half.2.refs_0_), custom_call_target="tpu_custom_call", output_to_operand_aliasing={{}: (3, {})} | custom-call | flops 3538944 | bytes 2359296 | tf_op jit(solution)/shard_map/residual_half/pallas_call | solution.py:77
  24.7 2.3 %collective-permute-start.7 = (bf16[96,1024]{1,0:T(8,128)(2,1)S(1)}, bf16[96,1024]{1,0:T(8,128)(2,1)S(1)}, u32[]{:S(2)}, u32[]{:S(2)}) collective-permute-start(bf16[96,1024]{1,0:T(8,128)(2,1)S(1)} %added.12.mine), channel_id=1, source_target_pairs={{0,1},{1,0},{2,3},{3,2},{4,5},{5,4},{6,7},{7,6},{8,14},{9,15},{10,... | collective-permute-start | bytes 589832 | tf_op jit(solution)/shard_map/ppermute | solution.py:53
  27.1 2.3 %collective-permute-start.10 = (bf16[96,1024]{1,0:T(8,128)(2,1)S(1)}, bf16[96,1024]{1,0:T(8,128)(2,1)S(1)}, u32[]{:S(2)}, u32[]{:S(2)}) collective-permute-start(bf16[96,1024]{1,0:T(8,128)(2,1)S(1)} %added.14.mine), channel_id=1, source_target_pairs={{0,2},{1,3},{2,0},{3,1},{4,6},{5,7},{6,4},{7,5},{8,9},{9,8},{10,11... | collective-permute-start | bytes 589832 | tf_op jit(solution)/shard_map/ppermute | solution.py:53
  29.4 0.1 collective-permute-start.13
  29.5 1.0 %collective-permute-done.7.theirs = bf16[96,1024]{1,0:T(8,128)(2,1)S(1)} collective-permute-done((bf16[96,1024]{1,0:T(8,128)(2,1)S(1)}, bf16[96,1024]{1,0:T(8,128)(2,1)S(1)}, u32[]{:S(2)}, u32[]{:S(2)}) %collective-permute-start.7) | collective-permute-done | bytes 196640 | tf_op jit(solution)/shard_map/ppermute | solution.py:53
  30.6 1.3 %collective-permute-start.8 = (bf16[96,1024]{1,0:T(8,128)(2,1)S(1)}, bf16[96,1024]{1,0:T(8,128)(2,1)S(1)}, u32[]{:S(2)}, u32[]{:S(2)}) collective-permute-start(bf16[96,1024]{1,0:T(8,128)(2,1)S(1)} %added.13.refs_0_), channel_id=1, source_target_pairs={{0,2},{1,3},{2,0},{3,1},{4,6},{5,7},{6,4},{7,5},{8,9},{9,8},{10,11... | collective-permute-start | bytes 589832 | tf_op jit(solution)/shard_map/ppermute | solution.py:53
  31.9 3.0 %collective-permute-done.10.theirs = bf16[96,1024]{1,0:T(8,128)(2,1)S(1)} collective-permute-done((bf16[96,1024]{1,0:T(8,128)(2,1)S(1)}, bf16[96,1024]{1,0:T(8,128)(2,1)S(1)}, u32[]{:S(2)}, u32[]{:S(2)}) %collective-permute-start.10) | collective-permute-done | bytes 196640 | tf_op jit(solution)/shard_map/ppermute | solution.py:53
  35.0 0.1 collective-permute-start.11
  35.3 5.0 %collective-permute-start.18 = (bf16[96,3072]{1,0:T(8,128)(2,1)S(1)}, bf16[96,3072]{1,0:T(8,128)(2,1)S(1)}, u32[]{:S(2)}, u32[]{:S(2)}) collective-permute-start(bf16[96,3072]{1,0:T(8,128)(2,1)S(1)} %pack.3), channel_id=1, source_target_pairs={{0,8},{8,0},{16,24},{24,16},{32,40},{40,32},{48,56},{56,48},{64,72... | collective-permute-start | bytes 1769480 | tf_op jit(solution)/shard_map/ppermute | solution.py:31
  40.3 2.0 %adam.3 = (bf16[384,3072]{1,0:T(8,128)(2,1)}, f32[384,3072]{1,0:T(8,128)}, f32[384,3072]{1,0:T(8,128)}) custom-call(bf16[96,1024]{1,0:T(8,128)(2,1)S(1)} %added.13.refs_0_, bf16[96,1024]{1,0:T(8,128)(2,1)S(1)} %added.15.refs_1_, bf16[96,1024]{1,0:T(8,128)(2,1)S(1)} %added.17.refs_2_, bf16[192,3072]{1,0:T(8,128)(2,1)S(1)} %copy-done.2, ...), custom_call_target="tpu_custom_call" | custom-call | flops 8847360 | bytes 2949120 | tf_op jit(solution)/shard_map/adam/pallas_call | solution.py:77
  42.4 2.8 %collective-permute-start.17 = (bf16[96,3072]{1,0:T(8,128)(2,1)S(1)}, bf16[96,3072]{1,0:T(8,128)(2,1)S(1)}, u32[]{:S(2)}, u32[]{:S(2)}) collective-permute-start(bf16[96,3072]{1,0:T(8,128)(2,1)S(1)} %pack.2), channel_id=1, source_target_pairs={{0,8},{8,0},{16,24},{24,16},{32,40},{40,32},{48,56},{56,48},{64,72... | collective-permute-start | bytes 1769480 | tf_op jit(solution)/shard_map/ppermute | solution.py:31
  45.2 2.0 %adam.4 = (bf16[384,3072]{1,0:T(8,128)(2,1)}, f32[384,3072]{1,0:T(8,128)}, f32[384,3072]{1,0:T(8,128)}) custom-call(bf16[96,3072]{1,0:T(8,128)(2,1)S(1)} %collective-permute-done.18.refs_0_, bf16[192,3072]{1,0:T(8,128)(2,1)S(1)} %collective-permute-done.5.refs_1_.refs_7_, ...), custom_call_target="tpu_custom_call", output_to_operand_aliasing={{0}: (4, {}), {1}: (5, {}), {2}: (6, {})} | custom-call | flops 8847360 | bytes 2949120 | tf_op jit(solution)/shard_map/adam/pallas_call | solution.py:77
  47.2 3.0 %adam.5 = (bf16[384,3072]{1,0:T(8,128)(2,1)}, f32[384,3072]{1,0:T(8,128)}, f32[384,3072]{1,0:T(8,128)}) custom-call(bf16[96,1024]{1,0:T(8,128)(2,1)S(1)} %collective-permute-done.8.refs_0_, bf16[96,1024]{1,0:T(8,128)(2,1)S(1)} %collective-permute-done.11.refs_1_, ...), custom_call_target="tpu_custom_call", output_to_operand_aliasing={{0}: (10, {}), {1}: (11, {}), {2}: (12, {})} | custom-call | flops 17694720 | bytes 5898240 | tf_op jit(solution)/shard_map/adam/pallas_call | solution.py:77
  (34 shorter events, 0.4 us)
Async XLA Ops:
  1.9 3.8 %copy-start.2 = (bf16[192,3072]{1,0:T(8,128)(2,1)S(1)}, bf16[192,3072]{1,0:T(8,128)(2,1)}, u32[]{:S(2)}) copy-start(bf16[192,3072]{1,0:T(8,128)(2,1)} %refs_3_.3) | copy-start | bytes 3538948
  1.9 4.2 %collective-permute-start = (bf16[192,3200]{1,0:T(8,128)(2,1)S(1)}, bf16[192,3200]{1,0:T(8,128)(2,1)S(1)}, u32[]{:S(2)}, u32[]{:S(2)}) collective-permute-start(bf16[192,3200]{1,0:T(8,128)(2,1)S(1)} %get-tuple-element.54), channel_id=1, source_target_pairs={{0,8},{8,0},{16,24},{24,16},{32,40},{40,32},{48,56},{56,48},{64,72... | collective-permute-start | bytes 3686408 | tf_op jit(solution)/shard_map/ppermute | solution.py:31
  5.5 10.7 %collective-permute-start.4 = (bf16[192,3072]{1,0:T(8,128)(2,1)S(1)}, bf16[192,3072]{1,0:T(8,128)(2,1)S(1)}, u32[]{:S(2)}, u32[]{:S(2)}) collective-permute-start(bf16[192,3072]{1,0:T(8,128)(2,1)S(1)} %get-tuple-element.61.residual), channel_id=1, source_target_pairs={{0,8},{8,0},{16,24},{24,16},{32,40},{40,32},{48,56},{56,48},{64,72... | collective-permute-start | bytes 3538952 | tf_op jit(solution)/shard_map/ppermute | solution.py:31
  5.7 10.5 %collective-permute-start.5 = (bf16[192,3072]{1,0:T(8,128)(2,1)S(1)}, bf16[192,3072]{1,0:T(8,128)(2,1)S(1)}, u32[]{:S(2)}, u32[]{:S(2)}) collective-permute-start(bf16[192,3072]{1,0:T(8,128)(2,1)S(1)} %copy-done.2), channel_id=1, source_target_pairs={{0,8},{8,0},{16,24},{24,16},{32,40},{40,32},{48,56},{56,48},{64,72... | collective-permute-start | bytes 3538952 | tf_op jit(solution)/shard_map/ppermute | solution.py:31
  6.5 9.7 %collective-permute-start.1 = (bf16[96,1024]{1,0:T(8,128)(2,1)S(1)}, bf16[96,1024]{1,0:T(8,128)(2,1)S(1)}, u32[]{:S(2)}, u32[]{:S(2)}) collective-permute-start(bf16[96,1024]{1,0:T(8,128)(2,1)S(1)} %pair_sums.4), channel_id=1, source_target_pairs={{0,2},{1,3},{2,0},{3,1},{4,6},{5,7},{6,4},{7,5},{8,9},{9,8},{10,11... | collective-permute-start | bytes 589832 | tf_op jit(solution)/shard_map/ppermute | solution.py:53
  9.6 6.6 %collective-permute-start.2 = (bf16[96,1024]{1,0:T(8,128)(2,1)S(1)}, bf16[96,1024]{1,0:T(8,128)(2,1)S(1)}, u32[]{:S(2)}, u32[]{:S(2)}) collective-permute-start(bf16[96,1024]{1,0:T(8,128)(2,1)S(1)} %pair_sums.5), channel_id=1, source_target_pairs={{0,6},{1,7},{2,4},{3,5},{4,2},{5,3},{6,0},{7,1},{8,10},{9,11},{10,... | collective-permute-start | bytes 589832 | tf_op jit(solution)/shard_map/ppermute | solution.py:53
  11.0 6.4 %collective-permute-start.3 = (bf16[96,1024]{1,0:T(8,128)(2,1)S(1)}, bf16[96,1024]{1,0:T(8,128)(2,1)S(1)}, u32[]{:S(2)}, u32[]{:S(2)}) collective-permute-start(bf16[96,1024]{1,0:T(8,128)(2,1)S(1)} %pair_sums.6), channel_id=1, source_target_pairs={{0,1},{1,0},{2,3},{3,2},{4,5},{5,4},{6,7},{7,6},{8,14},{9,15},{10,... | collective-permute-start | bytes 589832 | tf_op jit(solution)/shard_map/ppermute | solution.py:53
  13.3 4.2 %copy-start = (f32[192,3072]{1,0:T(8,128)S(1)}, f32[192,3072]{1,0:T(8,128)}, u32[]{:S(2)}) copy-start(f32[192,3072]{1,0:T(8,128)} %refs_4_.3) | copy-start | bytes 7077892
  13.3 5.0 %copy-start.1 = (f32[192,3072]{1,0:T(8,128)S(1)}, f32[192,3072]{1,0:T(8,128)}, u32[]{:S(2)}) copy-start(f32[192,3072]{1,0:T(8,128)} %refs_5_.3) | copy-start | bytes 7077892
  17.4 17.6 %collective-permute-start.14 = (f32[192,3072]{1,0:T(8,128)S(1)}, f32[192,3072]{1,0:T(8,128)S(1)}, u32[]{:S(2)}, u32[]{:S(2)}) collective-permute-start(f32[192,3072]{1,0:T(8,128)S(1)} %copy-done), channel_id=1, source_target_pairs={{0,8},{8,0},{16,24},{24,16},{32,40},{40,32},{48,56},{56,48},{64,72... | collective-permute-start | bytes 7077896 | tf_op jit(solution)/shard_map/ppermute | solution.py:31
  18.3 16.8 %collective-permute-start.15 = (f32[192,3072]{1,0:T(8,128)S(1)}, f32[192,3072]{1,0:T(8,128)S(1)}, u32[]{:S(2)}, u32[]{:S(2)}) collective-permute-start(f32[192,3072]{1,0:T(8,128)S(1)} %copy-done.1), channel_id=1, source_target_pairs={{0,8},{8,0},{16,24},{24,16},{32,40},{40,32},{48,56},{56,48},{64,72... | collective-permute-start | bytes 7077896 | tf_op jit(solution)/shard_map/ppermute | solution.py:31
  18.4 6.3 %collective-permute-start.6 = (bf16[96,1024]{1,0:T(8,128)(2,1)S(1)}, bf16[96,1024]{1,0:T(8,128)(2,1)S(1)}, u32[]{:S(2)}, u32[]{:S(2)}) collective-permute-start(bf16[96,1024]{1,0:T(8,128)(2,1)S(1)} %added.9.mine), channel_id=1, source_target_pairs={{0,6},{1,7},{2,4},{3,5},{4,2},{5,3},{6,0},{7,1},{8,10},{9,11},{10,... | collective-permute-start | bytes 589832 | tf_op jit(solution)/shard_map/ppermute | solution.py:53
  18.8 8.3 %collective-permute-start.9 = (bf16[96,1024]{1,0:T(8,128)(2,1)S(1)}, bf16[96,1024]{1,0:T(8,128)(2,1)S(1)}, u32[]{:S(2)}, u32[]{:S(2)}) collective-permute-start(bf16[96,1024]{1,0:T(8,128)(2,1)S(1)} %added.10.mine), channel_id=1, source_target_pairs={{0,1},{1,0},{2,3},{3,2},{4,5},{5,4},{6,7},{7,6},{8,14},{9,15},{10,... | collective-permute-start | bytes 589832 | tf_op jit(solution)/shard_map/ppermute | solution.py:53
  19.7 9.7 %collective-permute-start.12 = (bf16[96,1024]{1,0:T(8,128)(2,1)S(1)}, bf16[96,1024]{1,0:T(8,128)(2,1)S(1)}, u32[]{:S(2)}, u32[]{:S(2)}) collective-permute-start(bf16[96,1024]{1,0:T(8,128)(2,1)S(1)} %added.11.mine), channel_id=1, source_target_pairs={{0,2},{1,3},{2,0},{3,1},{4,6},{5,7},{6,4},{7,5},{8,9},{9,8},{10,11... | collective-permute-start | bytes 589832 | tf_op jit(solution)/shard_map/ppermute | solution.py:53
  24.7 5.8 %collective-permute-start.7 = (bf16[96,1024]{1,0:T(8,128)(2,1)S(1)}, bf16[96,1024]{1,0:T(8,128)(2,1)S(1)}, u32[]{:S(2)}, u32[]{:S(2)}) collective-permute-start(bf16[96,1024]{1,0:T(8,128)(2,1)S(1)} %added.12.mine), channel_id=1, source_target_pairs={{0,1},{1,0},{2,3},{3,2},{4,5},{5,4},{6,7},{7,6},{8,14},{9,15},{10,... | collective-permute-start | bytes 589832 | tf_op jit(solution)/shard_map/ppermute | solution.py:53
  27.1 7.8 %collective-permute-start.10 = (bf16[96,1024]{1,0:T(8,128)(2,1)S(1)}, bf16[96,1024]{1,0:T(8,128)(2,1)S(1)}, u32[]{:S(2)}, u32[]{:S(2)}) collective-permute-start(bf16[96,1024]{1,0:T(8,128)(2,1)S(1)} %added.14.mine), channel_id=1, source_target_pairs={{0,2},{1,3},{2,0},{3,1},{4,6},{5,7},{6,4},{7,5},{8,9},{9,8},{10,11... | collective-permute-start | bytes 589832 | tf_op jit(solution)/shard_map/ppermute | solution.py:53
  29.4 5.6 %collective-permute-start.13 = (bf16[96,1024]{1,0:T(8,128)(2,1)S(1)}, bf16[96,1024]{1,0:T(8,128)(2,1)S(1)}, u32[]{:S(2)}, u32[]{:S(2)}) collective-permute-start(bf16[96,1024]{1,0:T(8,128)(2,1)S(1)} %added.16.mine), channel_id=1, source_target_pairs={{0,6},{1,7},{2,4},{3,5},{4,2},{5,3},{6,0},{7,1},{8,10},{9,11},{10,... | collective-permute-start | bytes 589832 | tf_op jit(solution)/shard_map/ppermute | solution.py:53
  30.6 11.7 %collective-permute-start.8 = (bf16[96,1024]{1,0:T(8,128)(2,1)S(1)}, bf16[96,1024]{1,0:T(8,128)(2,1)S(1)}, u32[]{:S(2)}, u32[]{:S(2)}) collective-permute-start(bf16[96,1024]{1,0:T(8,128)(2,1)S(1)} %added.13.refs_0_), channel_id=1, source_target_pairs={{0,2},{1,3},{2,0},{3,1},{4,6},{5,7},{6,4},{7,5},{8,9},{9,8},{10,11... | collective-permute-start | bytes 589832 | tf_op jit(solution)/shard_map/ppermute | solution.py:53
  35.0 7.3 %collective-permute-start.11 = (bf16[96,1024]{1,0:T(8,128)(2,1)S(1)}, bf16[96,1024]{1,0:T(8,128)(2,1)S(1)}, u32[]{:S(2)}, u32[]{:S(2)}) collective-permute-start(bf16[96,1024]{1,0:T(8,128)(2,1)S(1)} %added.15.refs_1_), channel_id=1, source_target_pairs={{0,6},{1,7},{2,4},{3,5},{4,2},{5,3},{6,0},{7,1},{8,10},{9,11},{10,... | collective-permute-start | bytes 589832 | tf_op jit(solution)/shard_map/ppermute | solution.py:53
  35.1 7.2 %collective-permute-start.16 = (bf16[96,1024]{1,0:T(8,128)(2,1)S(1)}, bf16[96,1024]{1,0:T(8,128)(2,1)S(1)}, u32[]{:S(2)}, u32[]{:S(2)}) collective-permute-start(bf16[96,1024]{1,0:T(8,128)(2,1)S(1)} %added.17.refs_2_), channel_id=1, source_target_pairs={{0,1},{1,0},{2,3},{3,2},{4,5},{5,4},{6,7},{7,6},{8,14},{9,15},{10,... | collective-permute-start | bytes 589832 | tf_op jit(solution)/shard_map/ppermute | solution.py:53
  35.3 9.9 %collective-permute-start.18 = (bf16[96,3072]{1,0:T(8,128)(2,1)S(1)}, bf16[96,3072]{1,0:T(8,128)(2,1)S(1)}, u32[]{:S(2)}, u32[]{:S(2)}) collective-permute-start(bf16[96,3072]{1,0:T(8,128)(2,1)S(1)} %pack.3), channel_id=1, source_target_pairs={{0,8},{8,0},{16,24},{24,16},{32,40},{40,32},{48,56},{56,48},{64,72... | collective-permute-start | bytes 1769480 | tf_op jit(solution)/shard_map/ppermute | solution.py:31
  42.4 4.8 %collective-permute-start.17 = (bf16[96,3072]{1,0:T(8,128)(2,1)S(1)}, bf16[96,3072]{1,0:T(8,128)(2,1)S(1)}, u32[]{:S(2)}, u32[]{:S(2)}) collective-permute-start(bf16[96,3072]{1,0:T(8,128)(2,1)S(1)} %pack.2), channel_id=1, source_target_pairs={{0,8},{8,0},{16,24},{24,16},{32,40},{40,32},{48,56},{56,48},{64,72... | collective-permute-start | bytes 1769480 | tf_op jit(solution)/shard_map/ppermute | solution.py:31
